TPU v7x, 256 devices: a whole 4x4x8 slice. The times are simulated.
256 devices in a mesh: dp: 8 (over x_lo, y), tm: 16 (over z, core), height: 2 (over x_hi).
Axes of the slice: x: 4 (x_hi: 2, x_lo: 2; x = x_hi * 2 + x_lo), y: 4, z: 8, core: 2. Of those that a mesh axis runs over, the one named last changes fastest.
Arguments:
- clip_input: bfloat16 [8, 64, 8, 96, 128], P('dp', 'tm', 'height'), may hold values from -6 to 6
- cotangent: bfloat16 [8, 64, 8, 96, 128], P('dp', 'tm', 'height'), may hold values from -6 to 6
- first_kernel: bfloat16 [2592, 96], replicated, may hold values from -0.125 to 0.125
- second_kernel: bfloat16 [2592, 96], replicated, may hold values from -0.125 to 0.125
Outputs:
- block_output: float32 [8, 64, 8, 96, 128], P('dp', 'tm', 'height')
- input_grad: float32 [8, 64, 8, 96, 128], P('dp', 'tm', 'height')
- first_grad: float32 [2592, 96], P('dp')
- second_grad: float32 [2592, 96], P('dp')
All inputs are finite; a program needn't handle non-finite values.
Results may differ from a plain program's by a relative error of at most 0.0048.
Values may be sent and summed in bfloat16 or wider, within the bound.
No kernel may reach another device: no remote copies, remote signals or barrier semaphores. Data moves between devices by JAX's collectives and lax.ppermute only.
A program may use at most 64 MiB of HBM per device.

v0:
```python
import math

import jax
import jax.numpy as jnp
from jax import lax
from jax.sharding import PartitionSpec as P

EPSILON = 1e-06


def extended_2(array, sides, width):
    for axis, dim in sides:
        peers, length = (lax.axis_size(axis), array.shape[dim])
        up = [(i, (i + 1) % peers) for i in range(peers - 1)]
        down = [(j, i) for i, j in up]
        last = lax.slice_in_dim(array, length - width, length, axis=dim)
        first = lax.slice_in_dim(array, 0, width, axis=dim)
        before = lax.ppermute(last, axis, up)
        after = lax.ppermute(first, axis, down)
        array = jnp.concatenate([before, array, after], axis=dim)
    return array


def passed_along(array, axis, by):
    peers = lax.axis_size(axis)
    pairs = [(i, i + by) for i in range(peers) if 0 <= i + by < peers]
    return lax.ppermute(array, axis, pairs)


def norm_silu(field):
    factor = lax.rsqrt(jnp.mean(field * field, axis=2, keepdims=True) + EPSILON)
    return jax.nn.silu(field * factor)


def pad_rows(extended):
    rimmed = extended_2(extended, (("height", 1),), 1)
    return jnp.pad(rimmed, ((0, 0), (0, 0), (0, 0), (1, 1)))


def time_stack(padded, tap_row, tap_col, frames):
    row_count = padded.shape[1] - 2
    col_count = padded.shape[3] - 2
    window = padded[:, tap_row : tap_row + row_count, :, tap_col : tap_col + col_count]
    return jnp.concatenate([window[offset : offset + frames] for offset in range(3)], axis=2)


def local_conv(padded, kernel, frames):
    channels = padded.shape[2]
    summed = None
    for tap_row in range(3):
        for tap_col in range(3):
            stacked = time_stack(padded, tap_row, tap_col, frames)
            weight = kernel[:, tap_row, tap_col].reshape(3 * channels, kernel.shape[4])
            partial_sum = jnp.einsum(
                "frkw,kd->frdw", stacked, weight, preferred_element_type=jnp.float32
            )
            summed = partial_sum if summed is None else summed + partial_sum
    return summed


def kernel_grad(padded, grad_out, frames):
    channels = padded.shape[2]
    row_list = []
    for tap_row in range(3):
        col_list = []
        for tap_col in range(3):
            stacked = time_stack(padded, tap_row, tap_col, frames)
            piece = jnp.einsum(
                "frkw,frdw->kd", stacked, grad_out, preferred_element_type=jnp.float32
            )
            col_list.append(piece.reshape(3, channels, grad_out.shape[2]))
        row_list.append(jnp.stack(col_list, axis=1))
    gathered = jnp.stack(row_list, axis=1)
    return gathered.reshape(27 * channels, grad_out.shape[2])


def flipped(kernel):
    return jnp.swapaxes(kernel[::-1, ::-1, ::-1], 3, 4)


def local(clip_input, cotangent, first_kernel, second_kernel):
    frames = clip_input.shape[1]
    channels = clip_input.shape[3]
    source = clip_input[0]
    upstream = cotangent[0]
    kernel_one = first_kernel.reshape(3, 3, 3, channels, channels)
    kernel_two = second_kernel.reshape(3, 3, 3, channels, channels)

    def extend_back(block):
        earlier = passed_along(block[frames - 2 :], "tm", 1)
        return pad_rows(jnp.concatenate([earlier, block], axis=0))

    def extend_ahead(block):
        later = passed_along(block[:2], "tm", -1)
        return pad_rows(jnp.concatenate([block, later], axis=0))

    source_float = source.astype(jnp.float32)
    first_act = norm_silu(source_float).astype(jnp.bfloat16)
    first_padded = extend_back(first_act)
    middle = local_conv(first_padded, kernel_one, frames)
    second_act = norm_silu(middle).astype(jnp.bfloat16)
    second_padded = extend_back(second_act)
    branch = local_conv(second_padded, kernel_two, frames)
    block_output = source_float + branch
    second_back = local_conv(extend_ahead(upstream), flipped(kernel_two), frames)
    unused, pull_mid = jax.vjp(norm_silu, middle)
    middle_grad = pull_mid(second_back)[0].astype(jnp.bfloat16)
    first_back = local_conv(extend_ahead(middle_grad), flipped(kernel_one), frames)
    unused, pull_src = jax.vjp(norm_silu, source_float)
    input_grad = upstream.astype(jnp.float32) + pull_src(first_back)[0]
    positions = (
        frames
        * source.shape[1]
        * source.shape[3]
        * lax.axis_size("dp")
        * lax.axis_size("tm")
        * lax.axis_size("height")
    )
    factor = 1.0 / math.sqrt(positions)
    first_term = kernel_grad(first_padded, middle_grad, frames) * factor
    second_term = kernel_grad(second_padded, upstream, frames) * factor
    first_whole, second_whole = lax.psum((first_term, second_term), ("tm", "height"))
    first_grad, second_grad = (
        lax.psum_scatter(first_whole, "dp", scatter_dimension=0, tiled=True),
        lax.psum_scatter(second_whole, "dp", scatter_dimension=0, tiled=True),
    )
    return (block_output[None], input_grad[None], first_grad, second_grad)


def solution(mesh):
    return jax.shard_map(
        local,
        mesh=mesh,
        in_specs=(
            P("dp", "tm", "height", None, None),
            P("dp", "tm", "height", None, None),
            P(),
            P(),
        ),
        out_specs=(
            P("dp", "tm", "height", None, None),
            P("dp", "tm", "height", None, None),
            P("dp", None),
            P("dp", None),
        ),
        check_vma=False,
    )
```

profile of v0, /device:TPU:1, one launch (start us, length us, event | category | flops | bytes accessed | tf_op | source)
XLA Modules:
  0.0 447.4 jit_solution(8222491943957164210)
XLA Ops:
  7.2 1.0 slice_bitcast_fusion
  8.2 5.1 %collective-permute-start.6 = (bf16[2,4,96,128]{3,2,1,0:T(8,128)(2,1)S(1)}, bf16[2,4,96,128]{3,2,1,0:T(8,128)(2,1)S(1)}, u32[]{:S(2)}, u32[]{:S(2)}) collective-permute-start(bf16[2,4,96,128]{3,2,1,0:T(8,128)(2,1)S(1)} %slice_bitcast_fusion), channel_id=1, source_target_pairs={{2,0},{4,2},{6,4},{8,6},{10,8},{12,10},{14,12},{16,14},{18,16},{20... | collective-permute-start | bytes 589832 | tf_op jit(solution)/shard_map/ppermute | solution.py:27
  13.4 1.1 fusion.134
  14.5 1.2 fusion.126
  15.7 2.1 collective-permute-start
  18.2 0.8 fusion.228
  19.4 0.9 fusion.227
  20.4 0.7 copy.160
  21.1 0.7 copy.158
  21.9 0.7 copy.156
  22.6 0.7 copy.154
  23.3 0.7 copy.152
  24.1 0.7 copy.150
  24.8 0.7 copy.148
  25.5 0.7 copy.146
  26.3 0.7 copy.144
  28.1 0.7 dynamic-slice.6
  29.5 4.4 collective-permute-start.7
  33.9 1.3 collective-permute-start.8
  35.3 1.3 collective-permute-start.2
  36.6 5.5 %collective-permute-start.1 = (bf16[6,1,96,128]{3,2,1,0:T(8,128)(2,1)S(1)}, bf16[6,1,96,128]{3,2,1,0:T(8,128)(2,1)S(1)}, u32[]{:S(2)}, u32[]{:S(2)}) collective-permute-start(bf16[6,1,96,128]{3,2,1,0:T(8,128)(2,1)S(1)} %get-tuple-element.167), channel_id=1, source_target_pairs={{0,1},{2,3},{4,5},{6,7},{8,9},{10,11},{12,13},{14,15},{16,17},{18,... | collective-permute-start | bytes 442376 | tf_op jit(solution)/shard_map/ppermute | solution.py:18
  42.2 1.0 collective-permute-done.8
  43.2 1.0 select_maximum_fusion.3
  44.2 2.0 fusion.214
  46.1 1.0 fusion.10
  47.1 2.1 fusion.216
  61.7 0.7 multiply_reduce_fusion
  66.5 2.0 collective-permute-start.9
  68.5 3.6 collective-permute-start.3
  72.9 1.7 collective-permute-done.3
  74.7 1.3 collective-permute-start.5
  76.0 5.5 %collective-permute-start.4 = (bf16[6,1,96,128]{3,2,1,0:T(8,128)(2,1)S(1)}, bf16[6,1,96,128]{3,2,1,0:T(8,128)(2,1)S(1)}, u32[]{:S(2)}, u32[]{:S(2)}) collective-permute-start(bf16[6,1,96,128]{3,2,1,0:T(8,128)(2,1)S(1)} %get-tuple-element.163), channel_id=1, source_target_pairs={{0,1},{2,3},{4,5},{6,7},{8,9},{10,11},{12,13},{14,15},{16,17},{18,... | collective-permute-start | bytes 442376 | tf_op jit(solution)/shard_map/ppermute | solution.py:18
  81.6 1.3 collective-permute-start.10
  82.9 1.5 collective-permute-start.11
  85.2 0.8 fusion.149
  86.3 3.9 collective-permute-done.11
  90.4 1.2 fusion.217
  91.6 1.1 fusion.218
  95.1 1.3 fusion.229
  96.4 1.0 select_maximum_fusion.6
  97.4 2.0 fusion.215
  103.9 1.2 copy.163
  105.1 35.9 %fusion.212 = (f32[336,96]{1,0:T(8,128)S(1)}, f32[336,96]{1,0:T(8,128)S(1)}) fusion(f32[2592,96]{1,0:T(8,128)S(1)} %bitcast.378, f32[2592,96]{1,0:T(8,128)} %bitcast.379), kind=kCustom, calls=%all-reduce-scatter.2 | all-reduce-scatter fusion | flops 516097 | bytes 2249728
  141.0 2.6 collective-permute-start.13
  143.6 2.2 collective-permute-start.12
  145.8 1.9 select_maximum_fusion
  147.7 2.0 fusion.213
  153.4 0.5 copy-done.58
  155.3 0.5 copy-done.52
  156.5 0.5 copy-done.1
  157.0 0.7 fusion.135
  159.0 0.5 copy-done.27
  160.2 0.5 copy-done.21
  161.5 0.5 copy-done.45
  162.5 0.5 copy-done.15
  163.7 1.1 fusion.133
  166.6 0.7 constant_dynamic-slice_fusion
  167.3 0.5 concatenate.234
  167.8 0.7 constant_dynamic-slice_fusion.1
  169.1 0.5 copy-done.3
  169.8 1.3 fusion.18
  171.1 266.0 %all-reduce.12.cloned.1.call-done = (f32[324,96]{1,0:T(8,128)}, f32[324,96]{1,0:T(8,128)}) async-done(((f32[324,96]{1,0:T(8,128)}, f32[324,96]{1,0:T(8,128)}), (f32[324,96]{1,0:T(8,128)}, f32[324,96]{1,0:T(8,128)})) %all-reduce.12.cloned.1.call-update) | async-done | bytes 248848 | tf_op jit(solution)/shard_map/psum | solution.py:122
  437.1 1.7 copy.164
  438.8 1.7 copy.165
  (288 shorter events, 38.8 us)
Async XLA Ops:
  7.2 10.6 %copy-start.50 = (bf16[2592,96]{0,1:T(8,128)(2,1)S(1)}, bf16[2592,96]{0,1:T(8,128)(2,1)}, u32[]{:S(2)}) copy-start(bf16[2592,96]{0,1:T(8,128)(2,1)} %param.6) | copy-start | bytes 1492996
  7.2 430.0 %all-reduce.12.cloned.1.call-start = ((), (), s32[]{:S(2)}) async-start(), calls=%async_computation | async-start | bytes 671744 | tf_op jit(solution)/shard_map/psum | solution.py:122
  8.2 21.2 %collective-permute-start.6 = (bf16[2,4,96,128]{3,2,1,0:T(8,128)(2,1)S(1)}, bf16[2,4,96,128]{3,2,1,0:T(8,128)(2,1)S(1)}, u32[]{:S(2)}, u32[]{:S(2)}) collective-permute-start(bf16[2,4,96,128]{3,2,1,0:T(8,128)(2,1)S(1)} %slice_bitcast_fusion), channel_id=1, source_target_pairs={{2,0},{4,2},{6,4},{8,6},{10,8},{12,10},{14,12},{16,14},{18,16},{20... | collective-permute-start | bytes 589832 | tf_op jit(solution)/shard_map/ppermute | solution.py:27
  15.7 3.3 copy-start.51
  15.7 19.5 %collective-permute-start = (bf16[2,4,96,128]{3,2,1,0:T(8,128)(2,1)S(1)}, bf16[2,4,96,128]{3,2,1,0:T(8,128)(2,1)S(1)}, u32[]{:S(2)}, u32[]{:S(2)}) collective-permute-start(bf16[2,4,96,128]{3,2,1,0:T(8,128)(2,1)S(1)} %slice.856), channel_id=1, source_target_pairs={{0,2},{2,4},{4,6},{6,8},{8,10},{10,12},{12,14},{14,16},{16,18},{18... | collective-permute-start | bytes 589832 | tf_op jit(solution)/shard_map/ppermute | solution.py:27
  20.3 7.7 %copy-start.86 = (u32[256]{0:T(256)S(1)}, u32[256]{0:T(256)}, u32[]{:S(2)}) copy-start(u32[256]{0:T(256)} %constant.36) | copy-start | bytes 3076
  20.3 9.1 %copy-start = (bf16[1,4,4,96,128]{4,3,2,1,0:T(8,128)(2,1)S(1)}, bf16[1,4,4,96,128]{4,3,2,1,0:T(8,128)(2,1)}, u32[]{:S(2)}) copy-start(bf16[1,4,4,96,128]{4,3,2,1,0:T(8,128)(2,1)} %param.5) | copy-start | bytes 1179652
  29.5 12.7 %collective-permute-start.7 = (bf16[6,1,96,128]{3,2,1,0:T(8,128)(2,1)S(1)}, bf16[6,1,96,128]{3,2,1,0:T(8,128)(2,1)S(1)}, u32[]{:S(2)}, u32[]{:S(2)}) collective-permute-start(bf16[6,1,96,128]{3,2,1,0:T(8,128)(2,1)S(1)} %get-tuple-element.158), channel_id=1, source_target_pairs={{0,1},{2,3},{4,5},{6,7},{8,9},{10,11},{12,13},{14,15},{16,17},{18,... | collective-permute-start | bytes 442376 | tf_op jit(solution)/shard_map/ppermute | solution.py:18
  33.9 9.3 %collective-permute-start.8 = (bf16[6,1,96,128]{3,2,1,0:T(8,128)(2,1)S(1)}, bf16[6,1,96,128]{3,2,1,0:T(8,128)(2,1)S(1)}, u32[]{:S(2)}, u32[]{:S(2)}) collective-permute-start(bf16[6,1,96,128]{3,2,1,0:T(8,128)(2,1)S(1)} %get-tuple-element.159), channel_id=1, source_target_pairs={{1,0},{3,2},{5,4},{7,6},{9,8},{11,10},{13,12},{15,14},{17,16},{19,... | collective-permute-start | bytes 442376 | tf_op jit(solution)/shard_map/ppermute | solution.py:19
  35.3 10.9 %collective-permute-start.2 = (bf16[6,1,96,128]{3,2,1,0:T(8,128)(2,1)S(1)}, bf16[6,1,96,128]{3,2,1,0:T(8,128)(2,1)S(1)}, u32[]{:S(2)}, u32[]{:S(2)}) collective-permute-start(bf16[6,1,96,128]{3,2,1,0:T(8,128)(2,1)S(1)} %get-tuple-element.166), channel_id=1, source_target_pairs={{1,0},{3,2},{5,4},{7,6},{9,8},{11,10},{13,12},{15,14},{17,16},{19,... | collective-permute-start | bytes 442376 | tf_op jit(solution)/shard_map/ppermute | solution.py:19
  36.6 9.6 %collective-permute-start.1 = (bf16[6,1,96,128]{3,2,1,0:T(8,128)(2,1)S(1)}, bf16[6,1,96,128]{3,2,1,0:T(8,128)(2,1)S(1)}, u32[]{:S(2)}, u32[]{:S(2)}) collective-permute-start(bf16[6,1,96,128]{3,2,1,0:T(8,128)(2,1)S(1)} %get-tuple-element.167), channel_id=1, source_target_pairs={{0,1},{2,3},{4,5},{6,7},{8,9},{10,11},{12,13},{14,15},{16,17},{18,... | collective-permute-start | bytes 442376 | tf_op jit(solution)/shard_map/ppermute | solution.py:18
  66.5 15.0 %collective-permute-start.9 = (bf16[2,4,96,128]{3,2,1,0:T(8,128)(2,1)S(1)}, bf16[2,4,96,128]{3,2,1,0:T(8,128)(2,1)S(1)}, u32[]{:S(2)}, u32[]{:S(2)}) collective-permute-start(bf16[2,4,96,128]{3,2,1,0:T(8,128)(2,1)S(1)} %slice.975), channel_id=1, source_target_pairs={{2,0},{4,2},{6,4},{8,6},{10,8},{12,10},{14,12},{16,14},{18,16},{20... | collective-permute-start | bytes 589832 | tf_op jit(solution)/shard_map/ppermute | solution.py:27
  68.5 6.2 %collective-permute-start.3 = (bf16[2,4,96,128]{3,2,1,0:T(8,128)(2,1)S(1)}, bf16[2,4,96,128]{3,2,1,0:T(8,128)(2,1)S(1)}, u32[]{:S(2)}, u32[]{:S(2)}) collective-permute-start(bf16[2,4,96,128]{3,2,1,0:T(8,128)(2,1)S(1)} %slice.896), channel_id=1, source_target_pairs={{0,2},{2,4},{4,6},{6,8},{8,10},{10,12},{12,14},{14,16},{16,18},{18... | collective-permute-start | bytes 589832 | tf_op jit(solution)/shard_map/ppermute | solution.py:27
  74.7 18.0 %collective-permute-start.5 = (bf16[6,1,96,128]{3,2,1,0:T(8,128)(2,1)S(1)}, bf16[6,1,96,128]{3,2,1,0:T(8,128)(2,1)S(1)}, u32[]{:S(2)}, u32[]{:S(2)}) collective-permute-start(bf16[6,1,96,128]{3,2,1,0:T(8,128)(2,1)S(1)} %get-tuple-element.162), channel_id=1, source_target_pairs={{1,0},{3,2},{5,4},{7,6},{9,8},{11,10},{13,12},{15,14},{17,16},{19,... | collective-permute-start | bytes 442376 | tf_op jit(solution)/shard_map/ppermute | solution.py:19
  76.0 16.7 %collective-permute-start.4 = (bf16[6,1,96,128]{3,2,1,0:T(8,128)(2,1)S(1)}, bf16[6,1,96,128]{3,2,1,0:T(8,128)(2,1)S(1)}, u32[]{:S(2)}, u32[]{:S(2)}) collective-permute-start(bf16[6,1,96,128]{3,2,1,0:T(8,128)(2,1)S(1)} %get-tuple-element.163), channel_id=1, source_target_pairs={{0,1},{2,3},{4,5},{6,7},{8,9},{10,11},{12,13},{14,15},{16,17},{18,... | collective-permute-start | bytes 442376 | tf_op jit(solution)/shard_map/ppermute | solution.py:18
  81.6 4.8 %collective-permute-start.10 = (bf16[6,1,96,128]{3,2,1,0:T(8,128)(2,1)S(1)}, bf16[6,1,96,128]{3,2,1,0:T(8,128)(2,1)S(1)}, u32[]{:S(2)}, u32[]{:S(2)}) collective-permute-start(bf16[6,1,96,128]{3,2,1,0:T(8,128)(2,1)S(1)} %get-tuple-element.154), channel_id=1, source_target_pairs={{0,1},{2,3},{4,5},{6,7},{8,9},{10,11},{12,13},{14,15},{16,17},{18,... | collective-permute-start | bytes 442376 | tf_op jit(solution)/shard_map/ppermute | solution.py:18
  82.9 7.4 %collective-permute-start.11 = (bf16[6,1,96,128]{3,2,1,0:T(8,128)(2,1)S(1)}, bf16[6,1,96,128]{3,2,1,0:T(8,128)(2,1)S(1)}, u32[]{:S(2)}, u32[]{:S(2)}) collective-permute-start(bf16[6,1,96,128]{3,2,1,0:T(8,128)(2,1)S(1)} %get-tuple-element.155), channel_id=1, source_target_pairs={{1,0},{3,2},{5,4},{7,6},{9,8},{11,10},{13,12},{15,14},{17,16},{19,... | collective-permute-start | bytes 442376 | tf_op jit(solution)/shard_map/ppermute | solution.py:19
  90.3 1.3 copy-start.49
  99.4 1.2 copy-start.10
  99.4 1.3 copy-start.12
  99.4 1.9 copy-start.14
  99.4 1.9 copy-start.16
  99.4 1.9 copy-start.18
  99.4 2.4 copy-start.20
  99.4 2.4 copy-start.22
  99.4 2.4 copy-start.24
  99.5 3.0 copy-start.26
  99.5 3.0 copy-start.28
  99.5 3.0 copy-start.30
  99.5 3.5 copy-start.32
  99.5 3.5 copy-start.34
  99.5 3.5 copy-start.36
  141.0 8.7 %copy-start.46 = (f32[336,96]{1,0:T(8,128)}, f32[336,96]{1,0:T(8,128)S(1)}, u32[]{:S(2)}) copy-start(f32[336,96]{1,0:T(8,128)S(1)} %get-tuple-element.17) | copy-start | bytes 387076
  141.0 24.7 %collective-permute-start.13 = (f32[84,96]{1,0:T(8,128)S(1)}, f32[84,96]{1,0:T(8,128)S(1)}, u32[]{:S(2)}, u32[]{:S(2)}) collective-permute-start(f32[84,96]{1,0:T(8,128)S(1)} %slice.1016), channel_id=1, source_target_pairs={{0,32},{32,64},{64,96},{96,128},{128,160},{160,192},{192,224},{1,3... | collective-permute-start | bytes 96776
  143.6 23.7 %collective-permute-start.12 = (f32[84,96]{1,0:T(8,128)S(1)}, f32[84,96]{1,0:T(8,128)S(1)}, u32[]{:S(2)}, u32[]{:S(2)}) collective-permute-start(f32[84,96]{1,0:T(8,128)S(1)} %slice.1015), channel_id=1, source_target_pairs={{0,32},{32,64},{64,96},{96,128},{128,160},{160,192},{192,224},{1,3... | collective-permute-start | bytes 96776
  147.7 2.0 copy-start.55
  147.7 2.0 copy-start.56
  147.7 2.0 copy-start.57
  147.7 2.0 copy-start.68
  154.8 1.1 copy-start.53
  154.8 1.2 copy-start.54
  154.8 1.2 copy-start.61
  157.0 1.1 copy-start.35
  157.0 1.2 copy-start.37
  157.0 1.5 copy-start.48
  157.0 1.5 copy-start.76
  158.5 1.1 copy-start.29
  158.5 1.2 copy-start.31
  158.5 1.2 copy-start.75
  159.8 1.1 copy-start.23
  159.8 1.2 copy-start.25
  159.8 1.2 copy-start.74
  162.0 1.1 copy-start.17
  162.0 1.2 copy-start.19
  162.0 1.2 copy-start.72
  163.7 1.1 copy-start.9
  163.7 1.5 copy-start.13
  163.7 1.5 copy-start.71
  165.7 2.8 copy-start.39
  165.7 2.8 copy-start.41
  165.7 2.8 copy-start.43
  165.7 2.8 copy-start.70
  168.6 1.2 copy-start.7
  168.6 1.2 copy-start.69
  (38 other events, 35.5 us)
Sparse Core Ops, SparseCore 0:
  168.6 268.4 all-reduce.11
where the time goes:
time: 449 us; the launch traced here: 447 us
  waiting for transfers between devices  273 us (61%)
  local copies, waits for them, and re-layouts  44.3 us (10%)
  starting transfers between devices  39.7 us (9%)
  blocking collectives  35.9 us (8%)
  matrix products  26.7 us (6%)
  between operations  16.4 us (4%)
  other arithmetic  11.4 us (3%)
    psum x1, waiting for transfers between devices, local(): lax.psum((first_term, second_term), ('tm', 'height'))  266 us
    unnamed x1, blocking collectives  35.9 us
    unnamed x185, local copies, waits for them, and re-layouts  20.9 us
    dot_general x36, matrix products, local_conv(): jnp.einsum('frkw,kd->frdw', stacked, weight, preferred_element_type=jnp.f...  18.5 us
    ppermute x4, starting transfers between devices, extended_2(): before = lax.ppermute(last, axis, up)  16.8 us
    ppermute x4, starting transfers between devices, passed_along(): return lax.ppermute(array, axis, pairs)  12.8 us
    slice x10, local copies, waits for them, and re-layouts, time_stack(): window[offset:offset + frames]  11.6 us
    slice x22, local copies, waits for them, and re-layouts, local_conv(): weight = kernel[:, tap_row, tap_col].reshape(3 * channels, kernel.shape[4])  9.41 us
  transfers between devices with their start and end apart: 15, of which 5 were waited for; matrix products, arithmetic and copies ran while one was open for 8% of the time, Pallas kernels for 0%

commit v1 on v0

v1 whole, which is shorter than its diff:
```python
import functools
import math

import jax
import jax.numpy as jnp
from jax import lax
from jax.experimental import pallas as pl
from jax.experimental.pallas import tpu as pltpu
from jax.sharding import Mesh, PartitionSpec as P

EPSILON = 1e-06
TIME = ("z", "core")
CLIP_AXES = ("x_lo", "y")
PEER_AXES = ("z", "x_hi")
HALVES = ("z", "core", "x_hi")
SWAP = [(0, 1), (1, 0)]
BF16, F32 = jnp.bfloat16, jnp.float32

MAIN, STRIP = 256, 80


def sigmoid(u):
    return 1.0 / (1.0 + jnp.exp(-u))


def normed(v):
    scale = lax.rsqrt(jnp.mean(v * v, axis=0, keepdims=True) + EPSILON)
    return v * scale, scale


def norm_silu(v):
    u, _ = normed(v)
    return u * sigmoid(u)


def norm_silu_and_grad(v, back):
    u, scale = normed(v)
    gate = sigmoid(u)
    inner = back * (gate * (1.0 + u * (1.0 - gate)))
    grad = scale * (inner - u * jnp.mean(u * inner, axis=0, keepdims=True))
    return u * gate, grad


def fill(pairs, own, far, side, side_at, own_first, is_upper, change):
    channels, cols = own.shape[2], own.shape[3]
    frames, extra, rows = own.shape[0], far.shape[0], own.shape[1]
    lane = lax.broadcasted_iota(jnp.int32, (channels, cols), 1)
    upper = is_upper.astype(F32)
    own_at, far_at = (0, frames) if own_first else (extra, 0)

    def put(value, frame, row):
        shifted = (
            jnp.where(lane == 0, 0.0, pltpu.roll(value, 1, 1)),
            value,
            jnp.where(lane == cols - 1, 0.0, pltpu.roll(value, cols - 1, 1)),
        )
        for k, part in enumerate(shifted):
            part = part.astype(BF16)
            band = pl.ds(k * channels, channels)
            if frame < frames:
                pairs[frame, row, band, pl.ds(0, cols)] = part
            if frame >= 2:
                pairs[frame - 2, row, band, pl.ds(cols, cols)] = part

    for field, base in ((own, own_at), (far, far_at)):
        for f in range(field.shape[0]):

            @pl.loop(0, rows)
            def _(r):
                put(change(field[f, r].astype(F32)), base + f, r + 1)

            edge = side[side_at + f] if field is own else far[f, rows]
            value = change(edge.astype(F32))
            put(value * (1.0 - upper), base + f, 0)
            put(value * upper, base + f, rows + 1)


def conv_pair(weight, pairs, f, r):
    stacked = jnp.concatenate(
        [pairs[f + kt, pl.ds(r, 3)].reshape(-1, pairs.shape[3]) for kt in range(3)], axis=0
    )
    return jnp.dot(weight[...], stacked, preferred_element_type=F32)


def nt_dot(left, right):
    return lax.dot_general(left, right, (((1,), (1,)), ((), ())), preferred_element_type=F32)


def head_kernel(
    scale, owners, flags, x, x_far, c, c_far, side, w_one, w_two_back,
    act_out, grad_out, side_out, kept, given, px, pc, lanes_act, lanes_grad, sums,
):
    frames, rows, channels, cols = x.shape
    is_upper, core = flags[0] == 0, flags[1]
    fill(px, x, x_far, side, 0, False, is_upper, norm_silu)
    fill(pc, c, c_far, side, frames, True, is_upper, lambda v: v)

    for f in range(frames // 2):

        @pl.loop(0, rows)
        def _(r):
            middle = conv_pair(w_one, px, f, r)
            back = conv_pair(w_two_back, pc, f, r)
            act, grad = norm_silu_and_grad(middle, back)
            act, grad = act.astype(BF16), grad.astype(BF16)
            spot = f * rows + r
            lanes_act[spot] = act
            lanes_grad[spot] = grad
            for half in range(2):
                part = pl.ds(half * cols, cols)
                act_out[f + 2 * half, r] = act[:, half * cols : (half + 1) * cols]
                grad_out[f + 2 * half, r] = grad[:, half * cols : (half + 1) * cols]

    edge = jnp.where(is_upper, rows - 1, 0)
    for f in range(frames):
        side_out[f] = act_out[f, edge]
        side_out[frames + f] = grad_out[f, edge]

    spots = [(f, r) for f in range(frames // 2) for r in range(rows)]
    taps = 3 * channels

    @pl.loop(0, 9)
    def _(k):
        kt, kh = k // 3, k % 3
        left = jnp.concatenate([px[f + kt, r + kh] for f, r in spots], axis=1)
        right = jnp.concatenate([lanes_grad[i] for i in range(len(spots))], axis=1)
        first = pl.multiple_of(k * taps, 8)
        sums[0, pl.ds(first, taps), pl.ds(0, channels)] = nt_dot(left, right)

    @pl.loop(0, 9)
    def _(k):
        kt, kh = k // 3, k % 3
        left = jnp.concatenate([lanes_act[i] for i in range(len(spots))], axis=1)
        right = jnp.concatenate([pc[f + kt, r + kh] for f, r in spots], axis=1)
        product = nt_dot(left, right)
        for kw in range(3):
            tap = 26 - (3 * k + kw)
            first = pl.multiple_of(tap * channels, 8)
            sums[1, pl.ds(first, channels), pl.ds(0, channels)] = product[:, kw * channels : (kw + 1) * channels]

    total = 27 * channels
    sums[:, pl.ds(total, sums.shape[1] - total), :] = jnp.zeros((2, sums.shape[1] - total, cols), F32)
    share = total // owners
    lane = lax.broadcasted_iota(jnp.int32, (STRIP, cols), 1)
    for target, source in ((kept, core), (given, 1 - core)):
        for d in range(owners):
            rest = sums[source, pl.ds(share * d + MAIN, STRIP), :]
            for s in range(4):
                height = min(STRIP, MAIN - s * STRIP)
                main = sums[source, pl.ds(share * d + s * STRIP, height), :]
                if s < 3:
                    strip = pltpu.roll(rest, 96 - 32 * s, 1)
                else:
                    strip = jnp.zeros((STRIP, cols), F32)
                mixed = jnp.where(lane[:height] < channels, main, strip[:height])
                target[d, pl.ds(s * STRIP, height), :] = mixed * scale


def branch_kernel(flags, x, act, a_far, side, w_two, block_out, pa):
    frames, rows, channels, cols = x.shape
    fill(pa, act, a_far, side, 0, False, flags[0] == 0, lambda v: v)
    for f in range(frames // 2):

        @pl.loop(0, rows)
        def _(r):
            branch = conv_pair(w_two, pa, f, r)
            for half in range(2):
                part = slice(half * cols, (half + 1) * cols)
                at = f + 2 * half
                block_out[at, r] = x[at, r].astype(F32) + branch[:, part]


def input_kernel(flags, x, c, grad, g_far, side, w_one_back, input_out, pg):
    frames, rows, channels, cols = x.shape
    fill(pg, grad, g_far, side, frames, True, flags[0] == 0, lambda v: v)
    for f in range(frames // 2):

        @pl.loop(0, rows)
        def _(r):
            back = conv_pair(w_one_back, pg, f, r)
            for half in range(2):
                part = slice(half * cols, (half + 1) * cols)
                at = f + 2 * half
                _, grad_in = norm_silu_and_grad(x[at, r].astype(F32), back[:, part])
                input_out[at, r] = c[at, r].astype(F32) + grad_in


def weights_kernel(first, second, w_one, w_two_back, w_two, w_one_back):
    channels = first.shape[1]
    for source, ahead, back in ((first, w_one, w_one_back), (second, w_two, w_two_back)):
        ahead[...] = source[...].astype(F32).T.astype(BF16)
        taps = [source[pl.ds((26 - t) * channels, channels), :].astype(F32) for t in range(27)]
        back[...] = jnp.concatenate(taps, axis=1).astype(BF16)


def weights(first, second):
    turned = jax.ShapeDtypeStruct(first.shape[::-1], BF16)
    vmem = pl.BlockSpec(memory_space=pltpu.VMEM)
    return pl.pallas_call(
        weights_kernel,
        out_shape=(turned,) * 4,
        in_specs=[vmem] * 2,
        out_specs=[vmem] * 4,
        compiler_params=pltpu.CompilerParams(vmem_limit_bytes=24 * 1024 * 1024),
        cost_estimate=pl.CostEstimate(flops=3 * 10**9, bytes_accessed=6 * first.size, transcendentals=0),
    )(first, second)


def call(kernel, outs, scratch, flops, args):
    vmem = pl.BlockSpec(memory_space=pltpu.VMEM)
    moved = sum(a.size * a.dtype.itemsize for a in list(args[1:]) + list(outs))
    return pl.pallas_call(
        kernel,
        out_shape=outs,
        in_specs=[pl.BlockSpec(memory_space=pltpu.SMEM)] + [vmem] * (len(args) - 1),
        out_specs=[vmem] * len(outs),
        scratch_shapes=scratch,
        compiler_params=pltpu.CompilerParams(vmem_limit_bytes=24 * 1024 * 1024),
        cost_estimate=pl.CostEstimate(flops=flops, bytes_accessed=moved, transcendentals=0),
    )(*args)


def halos(earlier, later, side):
    frames = earlier.shape[0]
    peers = lax.axis_size(TIME)
    ahead = [(i, i + 1) for i in range(peers - 1)]
    behind = [(j, i) for i, j in ahead]
    edge = lax.ppermute(side, "x_hi", SWAP)
    last = jnp.concatenate([earlier[frames - 2 :], edge[frames - 2 : frames, None]], axis=1)
    first = jnp.concatenate([later[:2], edge[frames : frames + 2, None]], axis=1)
    far_a = lax.ppermute(last, TIME, ahead)
    far_b = lax.ppermute(first, TIME, behind)
    return far_a, far_b, edge


def clip_total(kept, given):
    pieces = (kept + lax.ppermute(given, "core", SWAP)).astype(BF16)
    arrived = lax.all_to_all(pieces, CLIP_AXES, 0, 0, tiled=True)
    return jnp.sum(arrived.astype(F32), axis=0)


def exchanged(parts):
    return lax.all_to_all(parts, PEER_AXES, 0, 0, tiled=True)


def unpacked(packed, share, channels):
    left = share - MAIN
    strips = [packed[s * STRIP : s * STRIP + left, channels:] for s in range(3)]
    return jnp.concatenate([packed[:, :channels], jnp.concatenate(strips, axis=1)], axis=0)


def local(clip_input, cotangent, first_kernel, second_kernel):
    source, upstream = clip_input[0], cotangent[0]
    frames, rows, channels, cols = source.shape
    half, core = lax.axis_index("x_hi"), lax.axis_index("core")
    flags = jnp.stack([half, core]).astype(jnp.int32)
    edge = jnp.where(half == 0, rows - 1, 0)
    side = jnp.concatenate(
        [lax.dynamic_index_in_dim(a, edge, 1, keepdims=False) for a in (source, upstream)], axis=0
    )
    w_one, w_two_back, w_two, w_one_back = weights(first_kernel, second_kernel)
    x_far, c_far, side = halos(source, upstream, side)

    owners = lax.axis_size(CLIP_AXES)
    positions = frames * rows * cols * lax.axis_size(CLIP_AXES + HALVES)
    field = jax.ShapeDtypeStruct(source.shape, BF16)
    packed = jax.ShapeDtypeStruct((owners, MAIN, cols), F32)
    pairs = pltpu.VMEM((frames, rows + 2, 3 * channels, 2 * cols), BF16)
    spots = frames * rows // 2
    conv_flops = 2 * 27 * channels * channels * frames * rows * cols
    act, grad, side, kept, given = call(
        functools.partial(head_kernel, 1.0 / math.sqrt(positions), owners),
        (field, field, jax.ShapeDtypeStruct((2 * frames, channels, cols), BF16), packed, packed),
        [
            pairs,
            pairs,
            pltpu.VMEM((spots, channels, 2 * cols), BF16),
            pltpu.VMEM((spots, channels, 2 * cols), BF16),
            pltpu.VMEM((2, 27 * channels + 32, cols), F32),
        ],
        4 * conv_flops,
        (flags, source, x_far, upstream, c_far, side, w_one, w_two_back),
    )
    out = jax.ShapeDtypeStruct(source.shape, F32)
    peers = lax.axis_size(PEER_AXES)
    a_far, g_far, side = halos(act, grad, side)
    clip_sum = clip_total(kept, given)
    clip_sum, a_far, g_far, side = lax.optimization_barrier((clip_sum, a_far, g_far, side))
    parts = exchanged(clip_sum.reshape(peers, MAIN // peers, -1))
    (block_output,) = call(
        branch_kernel, (out,), [pairs], conv_flops, (flags, source, act, a_far, side, w_two)
    )
    parts, block_output, g_far, side = lax.optimization_barrier((parts, block_output, g_far, side))
    part_sum = jnp.sum(parts, axis=0)
    sent = jnp.broadcast_to(part_sum[None], (peers,) + part_sum.shape)
    sent, g_far, side = lax.optimization_barrier((sent, g_far, side))
    whole = exchanged(sent).reshape(MAIN, -1)
    (input_grad,) = call(
        input_kernel, (out,), [pairs], conv_flops, (flags, source, upstream, grad, g_far, side, w_one_back)
    )
    whole, input_grad = lax.optimization_barrier((whole, input_grad))
    other = lax.ppermute(whole, "core", SWAP)
    first_packed = jnp.where(core == 0, whole, other)
    second_packed = jnp.where(core == 0, other, whole)
    share = 27 * channels // owners
    return (
        block_output[None],
        input_grad[None],
        unpacked(first_packed, share, channels),
        unpacked(second_packed, share, channels),
    )


def solution(mesh):
    shape = mesh.shape
    axes = CLIP_AXES + TIME + ("x_hi",)
    split = Mesh(mesh.devices.reshape(2, shape["dp"] // 2, shape["tm"] // 2, 2, shape["height"]), axes)
    field = P(CLIP_AXES, TIME, "x_hi", None, None)
    return jax.shard_map(
        local,
        mesh=split,
        in_specs=(field, field, P(), P()),
        out_specs=(field, field, P(CLIP_AXES, None), P(CLIP_AXES, None)),
        check_vma=False,
    )
```

time: 449 us -> 111 us (0.25)
  waiting for transfers between devices: 273 us -> 17.7 us
  Pallas kernels: 0 us -> 38.3 us
  local copies, waits for them, and re-layouts: 44.3 us -> 6.15 us
  blocking collectives: 35.9 us -> 0 us
  matrix products: 26.7 us -> 0 us
  between operations: 16.4 us -> 0.86 us
  other arithmetic: 11.4 us -> 4.54 us
    psum x1 -> x0, waiting for transfers between devices: 266 us -> none  [local(): lax.psum((first_term, second_term), ('tm', 'height'))]
    pallas_call x0 -> x4, Pallas kernels: none -> 38.3 us  [the longest x3 37.5 us: call(): pl.pallas_call(kernel, out_shape=outs, in_specs=[pl.BlockSpec(memory_spac...]
    unnamed x1 -> x0, blocking collectives: 35.9 us -> none
    dot_general x54 -> x0, matrix products: 26.7 us -> none  [the longest x36 18.5 us: local_conv(): jnp.einsum('frkw,kd->frdw', stacked, weight, preferred_element_type=jnp.f...]
    slice x36 -> x6, local copies, waits for them, and re-layouts: 22 us -> 0.9 us  [the longest x2 0.7 us: halos(): first = jnp.concatenate([later[:2], edge[frames:frames + 2, None]], axis=1)]
    all_to_all x0 -> x3, starting transfers between devices: none -> 19.7 us  [the longest x2 15.4 us: exchanged(): return lax.all_to_all(parts, PEER_AXES, 0, 0, tiled=True)]
    unnamed x185 -> x14, local copies, waits for them, and re-layouts: 20.9 us -> 3.53 us
    ppermute x12 -> x8, starting transfers between devices: 34.9 us -> 22.7 us  [the longest x2 10.3 us: halos(): far_a = lax.ppermute(last, TIME, ahead)]
  transfers between devices with their start and end apart: 15 -> 11, of which waited for: 5 -> 8; matrix products, arithmetic and copies ran while one was open for 8% -> 5% of each run, Pallas kernels for 0% -> 14%
where the time goes in v1:
time: 111 us; the launch traced here: 110 us
  starting transfers between devices  42.4 us (38%)
  Pallas kernels  38.3 us (35%)
  waiting for transfers between devices  17.7 us (16%)
  local copies, waits for them, and re-layouts  6.15 us (6%)
  other arithmetic  4.54 us (4%)
    pallas_call x3, Pallas kernels, call(): pl.pallas_call(kernel, out_shape=outs, in_specs=[pl.BlockSpec(memory_spac...  37.5 us
    all_to_all x2, starting transfers between devices, exchanged(): return lax.all_to_all(parts, PEER_AXES, 0, 0, tiled=True)  15.4 us
    ppermute x2, starting transfers between devices, halos(): far_a = lax.ppermute(last, TIME, ahead)  10.3 us
    ppermute x2, waiting for transfers between devices, halos(): far_b = lax.ppermute(first, TIME, behind)  8.29 us
    ppermute x2, starting transfers between devices, halos(): edge = lax.ppermute(side, 'x_hi', SWAP)  6.41 us
    all_to_all x2, waiting for transfers between devices, exchanged(): return lax.all_to_all(parts, PEER_AXES, 0, 0, tiled=True)  6.39 us
    all_to_all x1, starting transfers between devices, clip_total(): arrived = lax.all_to_all(pieces, CLIP_AXES, 0, 0, tiled=True)  4.3 us
    ppermute x2, starting transfers between devices, halos(): far_b = lax.ppermute(first, TIME, behind)  3.83 us
  transfers between devices with their start and end apart: 11, of which 8 were waited for; matrix products, arithmetic and copies ran while one was open for 5% of the time, Pallas kernels for 14%

profile of v1, /device:TPU:1, one launch (start us, length us, event | category | flops | bytes accessed | tf_op | source)
XLA Modules:
  0.0 110.0 jit_solution(15234163971630414393)
XLA Ops:
  0.6 0.0 copy-start
  0.6 0.0 copy-start.3
  0.7 1.0 dynamic-slice_bitcast_fusion
  1.7 3.7 %collective-permute-start = (bf16[8,96,128]{2,1,0:T(8,128)(2,1)S(1)}, bf16[8,96,128]{2,1,0:T(8,128)(2,1)S(1)}, u32[]{:S(2)}, u32[]{:S(2)}) collective-permute-start(bf16[8,96,128]{2,1,0:T(8,128)(2,1)S(1)} %pad_maximum_fusion.4), channel_id=1, source_target_pairs={{0,1},{1,0},{2,3},{3,2},{4,5},{5,4},{6,7},{7,6},{8,9},{9,8},{10,11... | collective-permute-start | bytes 589832 | tf_op jit(solution)/shard_map/ppermute | solution.py:228
  5.4 0.0 copy-done
  5.4 0.0 copy-done.3
  5.4 0.0 copy-start.4
  5.4 0.3 copy.16.first
  5.8 0.7 copy-done.4
  6.5 0.0 copy-start.1
  6.5 0.3 copy.17.second
  6.8 0.1 pad_add_fusion.flags
  6.9 0.6 copy-done.1
  7.5 1.5 %collective-permute-done.side = bf16[8,96,128]{2,1,0:T(8,128)(2,1)S(1)} collective-permute-done((bf16[8,96,128]{2,1,0:T(8,128)(2,1)S(1)}, bf16[8,96,128]{2,1,0:T(8,128)(2,1)S(1)}, u32[]{:S(2)}, u32[]{:S(2)}) %collective-permute-start) | collective-permute-done | bytes 196640 | tf_op jit(solution)/shard_map/ppermute | solution.py:228
  9.0 5.9 %collective-permute-start.1 = (bf16[2,5,96,128]{3,2,1,0:T(8,128)(2,1)S(1)}, bf16[2,5,96,128]{3,2,1,0:T(8,128)(2,1)S(1)}, u32[]{:S(2)}, u32[]{:S(2)}) collective-permute-start(bf16[2,5,96,128]{3,2,1,0:T(8,128)(2,1)S(1)} %pad_maximum_fusion), channel_id=1, source_target_pairs={{0,2},{2,4},{4,6},{6,8},{8,10},{10,12},{12,14},{14,16},{16,18},{18... | collective-permute-start | bytes 737288 | tf_op jit(solution)/shard_map/ppermute | solution.py:231
  15.0 1.9 %collective-permute-start.2 = (bf16[2,5,96,128]{3,2,1,0:T(8,128)(2,1)S(1)}, bf16[2,5,96,128]{3,2,1,0:T(8,128)(2,1)S(1)}, u32[]{:S(2)}, u32[]{:S(2)}) collective-permute-start(bf16[2,5,96,128]{3,2,1,0:T(8,128)(2,1)S(1)} %pad_maximum_fusion.1), channel_id=1, source_target_pairs={{2,0},{4,2},{6,4},{8,6},{10,8},{12,10},{14,12},{16,14},{18,16},{20... | collective-permute-start | bytes 737288 | tf_op jit(solution)/shard_map/ppermute | solution.py:232
  16.9 0.7 shard_map.75
  17.6 0.4 collective-permute-done.1.x_far
  18.1 4.4 %collective-permute-done.2.c_far = bf16[2,5,96,128]{3,2,1,0:T(8,128)(2,1)S(1)} collective-permute-done((bf16[2,5,96,128]{3,2,1,0:T(8,128)(2,1)S(1)}, bf16[2,5,96,128]{3,2,1,0:T(8,128)(2,1)S(1)}, u32[]{:S(2)}, u32[]{:S(2)}) %collective-permute-start.2) | collective-permute-done | bytes 245792 | tf_op jit(solution)/shard_map/ppermute | solution.py:232
  22.5 23.3 %shard_map.76 = (bf16[4,4,96,128]{3,2,1,0:T(8,128)(2,1)S(1)}, bf16[4,4,96,128]{3,2,1,0:T(8,128)(2,1)S(1)}, bf16[8,96,128]{2,1,0:T(8,128)(2,1)S(1)}, f32[8,256,128]{2,1,0:T(8,128)S(1)}, f32[8,256,128]{2,1,0:T(8,128)S(1)}) custom-call(s32[2]{0:T(128)S(1)} %pad_add_fusion.flags, bf16[4,4,96,128]{3,2,1,0:T(8,128)(2,1)S(1)} %bitcast.34, ...), custom_call_target="tpu_custom_call" | custom-call | flops 4076863488 | bytes 5550080 | tf_op jit(solution)/shard_map/pallas_call | solution.py:212
  45.8 0.1 collective-permute-start.3
  45.9 0.7 slice.62
  46.6 2.7 %collective-permute-start.4 = (bf16[8,96,128]{2,1,0:T(8,128)(2,1)S(1)}, bf16[8,96,128]{2,1,0:T(8,128)(2,1)S(1)}, u32[]{:S(2)}, u32[]{:S(2)}) collective-permute-start(bf16[8,96,128]{2,1,0:T(8,128)(2,1)S(1)} %get-tuple-element.31), channel_id=1, source_target_pairs={{0,1},{1,0},{2,3},{3,2},{4,5},{5,4},{6,7},{7,6},{8,9},{9,8},{10,11... | collective-permute-start | bytes 589832 | tf_op jit(solution)/shard_map/ppermute | solution.py:228
  49.4 0.0 collective-permute-done.3
  49.4 0.9 add_convert_fusion
  50.3 4.3 %all-to-all-start = ((bf16[8,256,128]{2,1,0:T(8,128)(2,1)}), bf16[8,256,128]{2,1,0:T(8,128)(2,1)}, u32[]{:S(2)}, u32[]{:S(2)}) async-start(bf16[8,256,128]{2,1,0:T(8,128)(2,1)} %add_convert_fusion), calls=%async_computation | async-start | bytes 1048576 | tf_op jit(solution)/shard_map/all_to_all | solution.py:238
  54.6 0.0 collective-permute-done.4.side
  54.6 0.0 copy-start.2
  54.6 0.7 pad_maximum_fusion.2
  55.4 4.4 %collective-permute-start.5 = (bf16[2,5,96,128]{3,2,1,0:T(8,128)(2,1)}, bf16[2,5,96,128]{3,2,1,0:T(8,128)(2,1)S(1)}, u32[]{:S(2)}, u32[]{:S(2)}) collective-permute-start(bf16[2,5,96,128]{3,2,1,0:T(8,128)(2,1)} %pad_maximum_fusion.2), channel_id=1, source_target_pairs={{0,2},{2,4},{4,6},{6,8},{8,10},{10,12},{12,14},{14,16},{16,18},{18... | collective-permute-start | bytes 737288 | tf_op jit(solution)/shard_map/ppermute | solution.py:231
  59.7 0.0 copy-done.2
  59.7 0.7 pad_maximum_fusion.3
  60.5 1.9 %collective-permute-start.6 = (bf16[2,5,96,128]{3,2,1,0:T(8,128)(2,1)}, bf16[2,5,96,128]{3,2,1,0:T(8,128)(2,1)S(1)}, u32[]{:S(2)}, u32[]{:S(2)}) collective-permute-start(bf16[2,5,96,128]{3,2,1,0:T(8,128)(2,1)} %pad_maximum_fusion.3), channel_id=1, source_target_pairs={{2,0},{4,2},{6,4},{8,6},{10,8},{12,10},{14,12},{16,14},{18,16},{20... | collective-permute-start | bytes 737288 | tf_op jit(solution)/shard_map/ppermute | solution.py:232
  62.4 0.2 all-to-all-done
  62.5 1.8 %convert_reduce_fusion = f32[256,128]{1,0:T(8,128)} fusion(bf16[8,256,128]{2,1,0:T(8,128)(2,1)} %all-to-all-done), kind=kLoop, calls=%fused_computation | loop fusion | flops 491520 | bytes 655360 | tf_op jit(solution)/shard_map/reduce_sum | solution.py:239
  64.3 0.0 collective-permute-done.5.a_far
  64.3 3.9 %collective-permute-done.6.g_far = bf16[2,5,96,128]{3,2,1,0:T(8,128)(2,1)S(1)} collective-permute-done((bf16[2,5,96,128]{3,2,1,0:T(8,128)(2,1)}, bf16[2,5,96,128]{3,2,1,0:T(8,128)(2,1)S(1)}, u32[]{:S(2)}, u32[]{:S(2)}) %collective-permute-start.6) | collective-permute-done | bytes 245792 | tf_op jit(solution)/shard_map/ppermute | solution.py:232
  68.2 10.0 %all-to-all-start.1 = ((f32[16,16,128]{2,1,0:T(8,128)}), f32[16,16,128]{2,1,0:T(8,128)S(1)}, u32[]{:S(2)}, u32[]{:S(2)}) async-start(f32[16,16,128]{2,1,0:T(8,128)} %bitcast.16), calls=%async_computation.1 | async-start | bytes 262144 | tf_op jit(solution)/shard_map/all_to_all | solution.py:243
  78.2 7.0 %shard_map.77 = f32[4,4,96,128]{3,2,1,0:T(8,128)} custom-call(s32[2]{0:T(128)S(1)} %pad_add_fusion.flags, bf16[4,4,96,128]{3,2,1,0:T(8,128)(2,1)S(1)} %bitcast.35, bf16[4,4,96,128]{3,2,1,0:T(8,128)(2,1)S(1)} %get-tuple-element.30.act, bf16[2,5,96,128]{3,2,1,0:T(8,128)(2,1)S(1)} %collective-permute-done.5.a_far, ...), custom_call_target="tpu_custom_call" | custom-call | flops 1019215872 | bytes 2512896 | tf_op jit(solution)/shard_map/pallas_call | solution.py:212
  85.2 3.6 %all-to-all-done.1 = f32[16,16,128]{2,1,0:T(8,128)S(1)} async-done(((f32[16,16,128]{2,1,0:T(8,128)}), f32[16,16,128]{2,1,0:T(8,128)S(1)}, u32[]{:S(2)}, u32[]{:S(2)}) %all-to-all-start.1) | async-done | bytes 131104 | tf_op jit(solution)/shard_map/all_to_all | solution.py:243
  88.8 0.7 broadcast_in_dim.29
  89.5 5.5 %all-to-all-start.2 = ((f32[16,16,128]{2,1,0:T(8,128)}), f32[16,16,128]{2,1,0:T(8,128)S(1)}, u32[]{:S(2)}, u32[]{:S(2)}) async-start(f32[16,16,128]{2,1,0:T(8,128)} %broadcast_in_dim.29), calls=%async_computation.2 | async-start | bytes 262144 | tf_op jit(solution)/shard_map/all_to_all | solution.py:243
  94.9 7.3 %shard_map.78 = f32[4,4,96,128]{3,2,1,0:T(8,128)} custom-call(s32[2]{0:T(128)S(1)} %pad_add_fusion.flags, bf16[4,4,96,128]{3,2,1,0:T(8,128)(2,1)S(1)} %bitcast.36, bf16[4,4,96,128]{3,2,1,0:T(8,128)(2,1)S(1)} %bitcast.38, bf16[4,4,96,128]{3,2,1,0:T(8,128)(2,1)S(1)} %get-tuple-element.32.grad, bf16[2,5,96,128]{3,2,1,0:T(8,128)(2,1)S(1)} %collective-permute-done.6.g_far, ...), custom_call_target="tpu_custom_call" | custom-call | flops 1019215872 | bytes 2906112 | tf_op jit(solution)/shard_map/pallas_call | solution.py:212
  102.2 2.8 %all-to-all-done.2 = f32[16,16,128]{2,1,0:T(8,128)S(1)} async-done(((f32[16,16,128]{2,1,0:T(8,128)}), f32[16,16,128]{2,1,0:T(8,128)S(1)}, u32[]{:S(2)}, u32[]{:S(2)}) %all-to-all-start.2) | async-done | bytes 131104 | tf_op jit(solution)/shard_map/all_to_all | solution.py:243
  105.0 2.0 %collective-permute-start.7 = (f32[256,128]{1,0:T(8,128)S(1)}, f32[256,128]{1,0:T(8,128)S(1)}, u32[]{:S(2)}, u32[]{:S(2)}) collective-permute-start(f32[256,128]{1,0:T(8,128)S(1)} %bitcast.41), channel_id=1, source_target_pairs={{0,2},{2,0},{1,3},{3,1},{4,6},{6,4},{5,7},{7,5},{8,10},{10,8},{9,1... | collective-permute-start | bytes 393224 | tf_op jit(solution)/shard_map/ppermute | solution.py:302
  107.0 1.0 collective-permute-done.7
  108.0 0.1 fusion
  108.1 0.1 maximum_maximum_fusion.1
  108.2 0.8 copy.21
  109.0 0.1 fusion.1
  109.1 0.1 maximum_maximum_fusion
  109.2 0.8 copy.20
  (10 shorter events, 0.2 us)
Async XLA Ops:
  0.6 4.8 %copy-start = (bf16[1,4,4,96,128]{4,3,2,1,0:T(8,128)(2,1)S(1)}, bf16[1,4,4,96,128]{4,3,2,1,0:T(8,128)(2,1)}, u32[]{:S(2)}) copy-start(bf16[1,4,4,96,128]{4,3,2,1,0:T(8,128)(2,1)} %param.4) | copy-start | bytes 1179652
  0.6 4.8 %copy-start.3 = (bf16[2592,96]{0,1:T(8,128)(2,1)S(1)}, bf16[2592,96]{0,1:T(8,128)(2,1)}, u32[]{:S(2)}) copy-start(bf16[2592,96]{0,1:T(8,128)(2,1)} %param.6) | copy-start | bytes 1492996
  1.7 7.2 %collective-permute-start = (bf16[8,96,128]{2,1,0:T(8,128)(2,1)S(1)}, bf16[8,96,128]{2,1,0:T(8,128)(2,1)S(1)}, u32[]{:S(2)}, u32[]{:S(2)}) collective-permute-start(bf16[8,96,128]{2,1,0:T(8,128)(2,1)S(1)} %pad_maximum_fusion.4), channel_id=1, source_target_pairs={{0,1},{1,0},{2,3},{3,2},{4,5},{5,4},{6,7},{7,6},{8,9},{9,8},{10,11... | collective-permute-start | bytes 589832 | tf_op jit(solution)/shard_map/ppermute | solution.py:228
  5.4 1.0 copy-start.4
  6.5 1.0 copy-start.1
  9.0 9.1 %collective-permute-start.1 = (bf16[2,5,96,128]{3,2,1,0:T(8,128)(2,1)S(1)}, bf16[2,5,96,128]{3,2,1,0:T(8,128)(2,1)S(1)}, u32[]{:S(2)}, u32[]{:S(2)}) collective-permute-start(bf16[2,5,96,128]{3,2,1,0:T(8,128)(2,1)S(1)} %pad_maximum_fusion), channel_id=1, source_target_pairs={{0,2},{2,4},{4,6},{6,8},{8,10},{10,12},{12,14},{14,16},{16,18},{18... | collective-permute-start | bytes 737288 | tf_op jit(solution)/shard_map/ppermute | solution.py:231
  15.0 7.5 %collective-permute-start.2 = (bf16[2,5,96,128]{3,2,1,0:T(8,128)(2,1)S(1)}, bf16[2,5,96,128]{3,2,1,0:T(8,128)(2,1)S(1)}, u32[]{:S(2)}, u32[]{:S(2)}) collective-permute-start(bf16[2,5,96,128]{3,2,1,0:T(8,128)(2,1)S(1)} %pad_maximum_fusion.1), channel_id=1, source_target_pairs={{2,0},{4,2},{6,4},{8,6},{10,8},{12,10},{14,12},{16,14},{18,16},{20... | collective-permute-start | bytes 737288 | tf_op jit(solution)/shard_map/ppermute | solution.py:232
  45.8 3.6 %collective-permute-start.3 = (f32[8,256,128]{2,1,0:T(8,128)S(1)}, f32[8,256,128]{2,1,0:T(8,128)S(1)}, u32[]{:S(2)}, u32[]{:S(2)}) collective-permute-start(f32[8,256,128]{2,1,0:T(8,128)S(1)} %get-tuple-element.29), channel_id=1, source_target_pairs={{0,2},{2,0},{1,3},{3,1},{4,6},{6,4},{5,7},{7,5},{8,10},{10,8},{9,1... | collective-permute-start | bytes 3145736 | tf_op jit(solution)/shard_map/ppermute | solution.py:237
  46.6 8.0 %collective-permute-start.4 = (bf16[8,96,128]{2,1,0:T(8,128)(2,1)S(1)}, bf16[8,96,128]{2,1,0:T(8,128)(2,1)S(1)}, u32[]{:S(2)}, u32[]{:S(2)}) collective-permute-start(bf16[8,96,128]{2,1,0:T(8,128)(2,1)S(1)} %get-tuple-element.31), channel_id=1, source_target_pairs={{0,1},{1,0},{2,3},{3,2},{4,5},{5,4},{6,7},{7,6},{8,9},{9,8},{10,11... | collective-permute-start | bytes 589832 | tf_op jit(solution)/shard_map/ppermute | solution.py:228
  50.3 12.2 %all-to-all-start = ((bf16[8,256,128]{2,1,0:T(8,128)(2,1)}), bf16[8,256,128]{2,1,0:T(8,128)(2,1)}, u32[]{:S(2)}, u32[]{:S(2)}) async-start(bf16[8,256,128]{2,1,0:T(8,128)(2,1)} %add_convert_fusion), calls=%async_computation | async-start | bytes 1048576 | tf_op jit(solution)/shard_map/all_to_all | solution.py:238
  54.6 5.1 %copy-start.2 = (bf16[2,4,96,128]{3,2,1,0:T(8,128)(2,1)S(1)}, bf16[2,4,96,128]{3,2,1,0:T(8,128)(2,1)}, u32[]{:S(2)}) copy-start(bf16[2,4,96,128]{3,2,1,0:T(8,128)(2,1)} %slice.62) | copy-start | bytes 589828
  55.4 9.0 %collective-permute-start.5 = (bf16[2,5,96,128]{3,2,1,0:T(8,128)(2,1)}, bf16[2,5,96,128]{3,2,1,0:T(8,128)(2,1)S(1)}, u32[]{:S(2)}, u32[]{:S(2)}) collective-permute-start(bf16[2,5,96,128]{3,2,1,0:T(8,128)(2,1)} %pad_maximum_fusion.2), channel_id=1, source_target_pairs={{0,2},{2,4},{4,6},{6,8},{8,10},{10,12},{12,14},{14,16},{16,18},{18... | collective-permute-start | bytes 737288 | tf_op jit(solution)/shard_map/ppermute | solution.py:231
  60.5 7.7 %collective-permute-start.6 = (bf16[2,5,96,128]{3,2,1,0:T(8,128)(2,1)}, bf16[2,5,96,128]{3,2,1,0:T(8,128)(2,1)S(1)}, u32[]{:S(2)}, u32[]{:S(2)}) collective-permute-start(bf16[2,5,96,128]{3,2,1,0:T(8,128)(2,1)} %pad_maximum_fusion.3), channel_id=1, source_target_pairs={{2,0},{4,2},{6,4},{8,6},{10,8},{12,10},{14,12},{16,14},{18,16},{20... | collective-permute-start | bytes 737288 | tf_op jit(solution)/shard_map/ppermute | solution.py:232
  68.2 20.6 %all-to-all-start.1 = ((f32[16,16,128]{2,1,0:T(8,128)}), f32[16,16,128]{2,1,0:T(8,128)S(1)}, u32[]{:S(2)}, u32[]{:S(2)}) async-start(f32[16,16,128]{2,1,0:T(8,128)} %bitcast.16), calls=%async_computation.1 | async-start | bytes 262144 | tf_op jit(solution)/shard_map/all_to_all | solution.py:243
  89.5 15.5 %all-to-all-start.2 = ((f32[16,16,128]{2,1,0:T(8,128)}), f32[16,16,128]{2,1,0:T(8,128)S(1)}, u32[]{:S(2)}, u32[]{:S(2)}) async-start(f32[16,16,128]{2,1,0:T(8,128)} %broadcast_in_dim.29), calls=%async_computation.2 | async-start | bytes 262144 | tf_op jit(solution)/shard_map/all_to_all | solution.py:243
  105.0 3.0 %collective-permute-start.7 = (f32[256,128]{1,0:T(8,128)S(1)}, f32[256,128]{1,0:T(8,128)S(1)}, u32[]{:S(2)}, u32[]{:S(2)}) collective-permute-start(f32[256,128]{1,0:T(8,128)S(1)} %bitcast.41), channel_id=1, source_target_pairs={{0,2},{2,0},{1,3},{3,1},{4,6},{6,4},{5,7},{7,5},{8,10},{10,8},{9,1... | collective-permute-start | bytes 393224 | tf_op jit(solution)/shard_map/ppermute | solution.py:302

commit v2 on v1

v2 whole, which is shorter than its diff:
```python
import functools
import math

import jax
import jax.numpy as jnp
from jax import lax
from jax.experimental import pallas as pl
from jax.experimental.pallas import tpu as pltpu
from jax.sharding import Mesh, PartitionSpec as P

EPSILON = 1e-06
TIME = ("z", "core")
CLIP_AXES = ("x_lo", "y")
PEER_AXES = ("z", "x_hi")
HALVES = ("z", "core", "x_hi")
SWAP = [(0, 1), (1, 0)]
BF16, F32 = jnp.bfloat16, jnp.float32

MAIN, STRIP = 256, 80


def sigmoid(u):
    return 0.5 + 0.5 * jnp.tanh(0.5 * u)


def normed(v):
    scale = lax.rsqrt(jnp.mean(v * v, axis=0, keepdims=True) + EPSILON)
    return v * scale, scale


def norm_silu(v):
    u, _ = normed(v)
    return u * sigmoid(u)


def norm_silu_and_grad(v, back):
    u, scale = normed(v)
    gate = sigmoid(u)
    inner = back * (gate * (1.0 + u * (1.0 - gate)))
    grad = scale * (inner - u * jnp.mean(u * inner, axis=0, keepdims=True))
    return u * gate, grad


def fill(pairs, own, far, side, side_at, own_first, is_upper, change):
    frames, extra, rows, cols = own.shape[0], far.shape[0], own.shape[1], own.shape[3]
    upper = is_upper.astype(F32)
    own_at, far_at = (0, frames) if own_first else (extra, 0)

    def put(value, frame, row):
        value = value.astype(BF16)
        if frame < frames:
            pairs[frame, row, :, pl.ds(0, cols)] = value
        if frame >= 2:
            pairs[frame - 2, row, :, pl.ds(cols, cols)] = value

    for field, base in ((own, own_at), (far, far_at)):
        for f in range(field.shape[0]):
            for r in range(rows):
                put(change(field[f, r].astype(F32)), base + f, r + 1)
            edge = side[side_at + f] if field is own else far[f, rows]
            value = change(edge.astype(F32))
            put(value * (1.0 - upper), base + f, 0)
            put(value * upper, base + f, rows + 1)


def shifted(value, by):
    cols = value.shape[1]
    lane = lax.broadcasted_iota(jnp.int32, value.shape, 1)
    return jnp.where(lane == (0 if by == 1 else cols - 1), 0.0, pltpu.roll(value, by % cols, 1))


def halves(value):
    cols = value.shape[1] // 2
    return value[:, :cols], value[:, cols:]


def conv_pair(weight, pairs, f, r):
    channels = pairs.shape[2]
    stacked = jnp.concatenate(
        [pairs[f + kt, pl.ds(r, 3)].reshape(3 * channels, -1) for kt in range(3)], axis=0
    )
    product = jnp.dot(weight[...], stacked, preferred_element_type=F32)
    return jnp.concatenate(
        [
            shifted(part[:channels], 1) + part[channels : 2 * channels] + shifted(part[2 * channels :], -1)
            for part in halves(product)
        ],
        axis=1,
    )


def put_shifts(target, spot, value):
    channels = value.shape[0]
    cols = value.shape[1] // 2
    for half, part in enumerate(halves(value)):
        lanes = pl.ds(half * cols, cols)
        for k, by in ((0, -1), (1, 0), (2, 1)):
            moved = shifted(part, by) if by else part
            target[spot, pl.ds(k * channels, channels), lanes] = moved.astype(BF16)


def nt_dot(left, right):
    return lax.dot_general(left, right, (((1,), (1,)), ((), ())), preferred_element_type=F32)


def head_kernel(
    scale, owners, flags, x, x_far, c, c_far, side, w_one, w_two_back,
    act_out, grad_out, side_out, kept, given, px, pc, lanes_act, lanes_grad, sums,
):
    frames, rows, channels, cols = x.shape
    is_upper, core = flags[0] == 0, flags[1]
    fill(px, x, x_far, side, 0, False, is_upper, norm_silu)
    fill(pc, c, c_far, side, frames, True, is_upper, lambda v: v)

    for f in range(frames // 2):

        @pl.loop(0, rows, unroll=True)
        def _(r):
            middle = conv_pair(w_one, px, f, r)
            back = conv_pair(w_two_back, pc, f, r)
            act, grad = norm_silu_and_grad(middle, back)
            spot = f * rows + r
            put_shifts(lanes_act, spot, act)
            put_shifts(lanes_grad, spot, grad)
            for half in range(2):
                act_out[f + 2 * half, r] = act[:, half * cols : (half + 1) * cols].astype(BF16)
                grad_out[f + 2 * half, r] = grad[:, half * cols : (half + 1) * cols].astype(BF16)

    edge = jnp.where(is_upper, rows - 1, 0)
    for f in range(frames):
        side_out[f] = act_out[f, edge]
        side_out[frames + f] = grad_out[f, edge]

    spots = [(f, r) for f in range(frames // 2) for r in range(rows)]
    taps = 3 * channels

    def lined(scratch):
        return jnp.concatenate([scratch[i] for i in range(len(spots))], axis=1)

    def padded(pairs, kt):
        return jnp.concatenate([pairs[f + kt, pl.ds(r, 3)].reshape(taps, -1) for f, r in spots], axis=1)

    @pl.loop(0, 3, unroll=True)
    def _(kt):
        product = nt_dot(padded(px, kt), lined(lanes_grad))
        for kh in range(3):
            for kw in range(3):
                first = pl.multiple_of((9 * kt + 3 * kh + kw) * channels, 8)
                block = product[kh * channels : (kh + 1) * channels, kw * channels : (kw + 1) * channels]
                sums[0, pl.ds(first, channels), pl.ds(0, channels)] = block

    @pl.loop(0, 3, unroll=True)
    def _(kt):
        product = nt_dot(lined(lanes_act), padded(pc, kt))
        for kh in range(3):
            for kw in range(3):
                first = pl.multiple_of((26 - (9 * kt + 3 * kh + kw)) * channels, 8)
                block = product[kw * channels : (kw + 1) * channels, kh * channels : (kh + 1) * channels]
                sums[1, pl.ds(first, channels), pl.ds(0, channels)] = block

    total = 27 * channels
    sums[:, pl.ds(total, sums.shape[1] - total), :] = jnp.zeros((2, sums.shape[1] - total, cols), F32)
    share = total // owners
    lane = lax.broadcasted_iota(jnp.int32, (STRIP, cols), 1)
    for target, source in ((kept, core), (given, 1 - core)):
        for d in range(owners):
            rest = sums[source, pl.ds(share * d + MAIN, STRIP), :]
            for s in range(4):
                height = min(STRIP, MAIN - s * STRIP)
                main = sums[source, pl.ds(share * d + s * STRIP, height), :]
                if s < 3:
                    strip = pltpu.roll(rest, 96 - 32 * s, 1)
                else:
                    strip = jnp.zeros((STRIP, cols), F32)
                mixed = jnp.where(lane[:height] < channels, main, strip[:height])
                target[d, pl.ds(s * STRIP, height), :] = mixed * scale


def branch_kernel(flags, x, act, a_far, side, w_two, block_out, pa):
    frames, rows, channels, cols = x.shape
    fill(pa, act, a_far, side, 0, False, flags[0] == 0, lambda v: v)
    for f in range(frames // 2):

        @pl.loop(0, rows, unroll=True)
        def _(r):
            branch = conv_pair(w_two, pa, f, r)
            for half in range(2):
                part = slice(half * cols, (half + 1) * cols)
                at = f + 2 * half
                block_out[at, r] = x[at, r].astype(F32) + branch[:, part]


def input_kernel(flags, x, c, grad, g_far, side, w_one_back, input_out, pg):
    frames, rows, channels, cols = x.shape
    fill(pg, grad, g_far, side, frames, True, flags[0] == 0, lambda v: v)
    for f in range(frames // 2):

        @pl.loop(0, rows, unroll=True)
        def _(r):
            back = conv_pair(w_one_back, pg, f, r)
            for half in range(2):
                part = slice(half * cols, (half + 1) * cols)
                at = f + 2 * half
                _, grad_in = norm_silu_and_grad(x[at, r].astype(F32), back[:, part])
                input_out[at, r] = c[at, r].astype(F32) + grad_in


def weights_kernel(first, second, w_one, w_two_back, w_two, w_one_back):
    channels = first.shape[0]
    for source, ahead, back in ((first, w_one, w_one_back), (second, w_two, w_two_back)):
        whole = source[...].astype(F32)
        taps = [whole[:, t * channels : (t + 1) * channels] for t in range(27)]
        for kw in range(3):
            rows = pl.ds(kw * channels, channels)
            ahead[rows, :] = jnp.concatenate([taps[3 * k + kw] for k in range(9)], axis=1).astype(BF16)
            back[rows, :] = jnp.concatenate([taps[26 - 3 * k - kw].T for k in range(9)], axis=1).astype(BF16)


def weights(first, second):
    turned = jax.ShapeDtypeStruct((3 * first.shape[0], first.shape[1] // 3), BF16)
    vmem = pl.BlockSpec(memory_space=pltpu.VMEM)
    return pl.pallas_call(
        weights_kernel,
        out_shape=(turned,) * 4,
        in_specs=[vmem] * 2,
        out_specs=[vmem] * 4,
        compiler_params=pltpu.CompilerParams(vmem_limit_bytes=10 * 1024 * 1024),
        cost_estimate=pl.CostEstimate(flops=3 * 10**9, bytes_accessed=6 * first.size, transcendentals=0),
    )(first, second)


def call(kernel, outs, scratch, flops, args, mib=12):
    vmem = pl.BlockSpec(memory_space=pltpu.VMEM)
    moved = sum(a.size * a.dtype.itemsize for a in list(args[1:]) + list(outs))
    return pl.pallas_call(
        kernel,
        out_shape=outs,
        in_specs=[pl.BlockSpec(memory_space=pltpu.SMEM)] + [vmem] * (len(args) - 1),
        out_specs=[vmem] * len(outs),
        scratch_shapes=scratch,
        compiler_params=pltpu.CompilerParams(vmem_limit_bytes=mib * 1024 * 1024),
        cost_estimate=pl.CostEstimate(flops=flops, bytes_accessed=moved, transcendentals=0),
    )(*args)


def halos(earlier, later, side):
    frames = earlier.shape[0]
    peers = lax.axis_size(TIME)
    ahead = [(i, i + 1) for i in range(peers - 1)]
    behind = [(j, i) for i, j in ahead]
    edge = lax.ppermute(side, "x_hi", SWAP)
    last = jnp.concatenate([earlier[frames - 2 :], edge[frames - 2 : frames, None]], axis=1)
    first = jnp.concatenate([later[:2], edge[frames : frames + 2, None]], axis=1)
    far_a = lax.ppermute(last, TIME, ahead)
    far_b = lax.ppermute(first, TIME, behind)
    return far_a, far_b, edge


def chip_total(kept, given):
    return (kept + lax.ppermute(given, "core", SWAP)).astype(BF16)


def clip_total(pieces):
    arrived = lax.all_to_all(pieces, CLIP_AXES, 0, 0, tiled=True)
    total = jax.ShapeDtypeStruct(pieces.shape[1:], F32)
    return small_call(total_kernel, (total,), (arrived,), False)[0]


def exchanged(parts):
    return lax.all_to_all(parts, PEER_AXES, 0, 0, tiled=True)


def total_kernel(arrived, total):
    acc = arrived[0].astype(F32)
    for d in range(1, arrived.shape[0]):
        acc = acc + arrived[d].astype(F32)
    total[...] = acc


def unpack_kernel(flags, whole, other, first, second):
    channels, share = first.shape
    left = share - MAIN
    cols = whole.shape[1]

    def write(target, packed):
        target[:, pl.ds(0, MAIN)] = packed[...].T[:channels]
        lane = lax.broadcasted_iota(jnp.int32, (STRIP, cols), 1)
        width = cols - channels
        strips = [pltpu.roll(packed[pl.ds(s * STRIP, STRIP), :], (s + 1) * width, 1) for s in range(3)]
        rest = jnp.where(lane < width, strips[0], jnp.where(lane < 2 * width, strips[1], strips[2]))
        target[:, pl.ds(MAIN, left)] = rest.T[:channels, :left]

    for core, pair in ((0, (first, second)), (1, (second, first))):

        @pl.when(flags[1] == core)
        def _():
            write(pair[0], whole)
            write(pair[1], other)


def small_call(kernel, outs, args, flagged):
    vmem = pl.BlockSpec(memory_space=pltpu.VMEM)
    moved = sum(a.size * a.dtype.itemsize for a in list(args) + list(outs))
    specs = [vmem] * len(args)
    if flagged:
        specs[0] = pl.BlockSpec(memory_space=pltpu.SMEM)
    return pl.pallas_call(
        kernel,
        out_shape=outs,
        in_specs=specs,
        out_specs=[vmem] * len(outs),
        compiler_params=pltpu.CompilerParams(vmem_limit_bytes=4 * 1024 * 1024),
        cost_estimate=pl.CostEstimate(flops=0, bytes_accessed=moved, transcendentals=0),
    )(*args)


def head(source, x_far, upstream, c_far, side, w_one, w_two_back, flags, owners, scale):
    frames, rows, channels, cols = source.shape
    field = jax.ShapeDtypeStruct(source.shape, BF16)
    packed = jax.ShapeDtypeStruct((owners, MAIN, cols), F32)
    pairs = pltpu.VMEM((frames, rows + 2, channels, 2 * cols), BF16)
    spots = frames * rows // 2
    conv_flops = 2 * 27 * channels * channels * frames * rows * cols
    return call(
        functools.partial(head_kernel, scale, owners),
        (field, field, jax.ShapeDtypeStruct((2 * frames, channels, cols), BF16), packed, packed),
        [
            pairs,
            pairs,
            pltpu.VMEM((spots, 3 * channels, 2 * cols), BF16),
            pltpu.VMEM((spots, 3 * channels, 2 * cols), BF16),
            pltpu.VMEM((2, 27 * channels + 32, cols), F32),
        ],
        4 * conv_flops,
        (flags, source, x_far, upstream, c_far, side, w_one, w_two_back),
        mib=22,
    )


def local(clip_input, cotangent, first_kernel, second_kernel):
    source, upstream = clip_input[0], cotangent[0]
    frames, rows, channels, cols = source.shape
    half, core = lax.axis_index("x_hi"), lax.axis_index("core")
    flags = jnp.stack([half, core]).astype(jnp.int32)
    edge = jnp.where(half == 0, rows - 1, 0)
    side = jnp.concatenate(
        [lax.dynamic_index_in_dim(a, edge, 1, keepdims=False) for a in (source, upstream)], axis=0
    )
    w_one, w_two_back, w_two, w_one_back = weights(first_kernel.T, second_kernel.T)
    x_far, c_far, side = halos(source, upstream, side)

    owners = lax.axis_size(CLIP_AXES)
    positions = frames * rows * cols * lax.axis_size(CLIP_AXES + HALVES)
    act, grad, side, kept, given = head(
        source, x_far, upstream, c_far, side, w_one, w_two_back, flags, owners, 1.0 / math.sqrt(positions)
    )
    pairs = pltpu.VMEM((frames, rows + 2, channels, 2 * cols), BF16)
    conv_flops = 2 * 27 * channels * channels * frames * rows * cols
    out = jax.ShapeDtypeStruct(source.shape, F32)
    peers = lax.axis_size(PEER_AXES)
    pieces, side = lax.optimization_barrier((chip_total(kept, given), side))
    clip_sum = clip_total(pieces)
    a_far, g_far, side = halos(act, grad, side)
    clip_sum, a_far, g_far, side = lax.optimization_barrier((clip_sum, a_far, g_far, side))
    parts = exchanged(clip_sum.reshape(peers, MAIN // peers, -1))
    (block_output,) = call(
        branch_kernel, (out,), [pairs], conv_flops, (flags, source, act, a_far, side, w_two)
    )
    parts, block_output, g_far, side = lax.optimization_barrier((parts, block_output, g_far, side))
    part_sum = jnp.sum(parts, axis=0)
    sent = jnp.broadcast_to(part_sum[None], (peers,) + part_sum.shape)
    sent, g_far, side = lax.optimization_barrier((sent, g_far, side))
    whole = exchanged(sent).reshape(MAIN, -1)
    (input_grad,) = call(
        input_kernel, (out,), [pairs], conv_flops, (flags, source, upstream, grad, g_far, side, w_one_back)
    )
    whole, input_grad = lax.optimization_barrier((whole, input_grad))
    other = lax.ppermute(whole, "core", SWAP)
    owned = jax.ShapeDtypeStruct((channels, 27 * channels // owners), F32)
    first_grad, second_grad = small_call(unpack_kernel, (owned, owned), (flags, whole, other), True)
    return (
        block_output[None],
        input_grad[None],
        first_grad.T,
        second_grad.T,
    )


def solution(mesh):
    shape = mesh.shape
    axes = CLIP_AXES + TIME + ("x_hi",)
    split = Mesh(mesh.devices.reshape(2, shape["dp"] // 2, shape["tm"] // 2, 2, shape["height"]), axes)
    field = P(CLIP_AXES, TIME, "x_hi", None, None)
    return jax.shard_map(
        local,
        mesh=split,
        in_specs=(field, field, P(), P()),
        out_specs=(field, field, P(CLIP_AXES, None), P(CLIP_AXES, None)),
        check_vma=False,
    )
```

time: 111 us -> 96 us (0.86)
  Pallas kernels: 38.3 us -> 18.3 us
  waiting for transfers between devices: 17.7 us -> 29.5 us
  local copies, waits for them, and re-layouts: 6.15 us -> 3.58 us
  other arithmetic: 4.54 us -> 2.49 us
  starting transfers between devices: 42.4 us -> 40.7 us
    pallas_call x3, Pallas kernels: 37.5 us -> 14.2 us  [call(): pl.pallas_call(kernel, out_shape=outs, in_specs=[pl.BlockSpec(memory_spac...]
    all_to_all x2, waiting for transfers between devices: 6.39 us -> 13.5 us  [exchanged(): return lax.all_to_all(parts, PEER_AXES, 0, 0, tiled=True)]
    ppermute x2, waiting for transfers between devices: 1.48 us -> 4.32 us  [halos(): edge = lax.ppermute(side, 'x_hi', SWAP)]
    ppermute x1, waiting for transfers between devices: 0.01 us -> 2.65 us  [chip_total(): return (kept + lax.ppermute(given, 'core', SWAP)).astype(BF16)]
    pallas_call x0 -> x2, Pallas kernels: none -> 2.31 us  [small_call(): pl.pallas_call(kernel, out_shape=outs, in_specs=specs, out_specs=[vmem] *...]
    all_to_all x2, starting transfers between devices: 15.4 us -> 13.3 us  [exchanged(): return lax.all_to_all(parts, PEER_AXES, 0, 0, tiled=True)]
    reduce_sum x1 -> x0, other arithmetic: 1.78 us -> none  [clip_total(): return jnp.sum(arrived.astype(F32), axis=0)]
    unnamed x14 -> x12, local copies, waits for them, and re-layouts: 3.53 us -> 1.84 us
  transfers between devices with their start and end apart: 11 -> 11, of which waited for: 8 -> 9; matrix products, arithmetic and copies ran while one was open for 5% -> 2% of each run, Pallas kernels for 14% -> 9%
where the time goes in v2:
time: 96 us; the launch traced here: 95.4 us
  starting transfers between devices  40.7 us (42%)
  waiting for transfers between devices  29.5 us (31%)
  Pallas kernels  18.3 us (19%)
  local copies, waits for them, and re-layouts  3.58 us (4%)
  other arithmetic  2.49 us (3%)
    pallas_call x3, Pallas kernels, call(): pl.pallas_call(kernel, out_shape=outs, in_specs=[pl.BlockSpec(memory_spac...  14.2 us
    all_to_all x2, waiting for transfers between devices, exchanged(): return lax.all_to_all(parts, PEER_AXES, 0, 0, tiled=True)  13.5 us
    all_to_all x2, starting transfers between devices, exchanged(): return lax.all_to_all(parts, PEER_AXES, 0, 0, tiled=True)  13.3 us
    ppermute x2, starting transfers between devices, halos(): far_a = lax.ppermute(last, TIME, ahead)  10.4 us
    ppermute x2, waiting for transfers between devices, halos(): far_b = lax.ppermute(first, TIME, behind)  7.99 us
    ppermute x2, starting transfers between devices, halos(): edge = lax.ppermute(side, 'x_hi', SWAP)  6.38 us
    ppermute x2, waiting for transfers between devices, halos(): edge = lax.ppermute(side, 'x_hi', SWAP)  4.32 us
    all_to_all x1, starting transfers between devices, clip_total(): arrived = lax.all_to_all(pieces, CLIP_AXES, 0, 0, tiled=True)  4.23 us
  transfers between devices with their start and end apart: 11, of which 9 were waited for; matrix products, arithmetic and copies ran while one was open for 2% of the time, Pallas kernels for 9%

profile of v2, /device:TPU:1, one launch (start us, length us, event | category | flops | bytes accessed | tf_op | source)
XLA Modules:
  0.0 95.4 jit_solution(14925800077157364234)
XLA Ops:
  0.6 0.0 copy-start
  0.6 1.0 %dynamic-slice_bitcast_fusion = (bf16[4,96,128]{2,1,0:T(8,128)(2,1)S(1)}, bf16[4,96,128]{2,1,0:T(8,128)(2,1)S(1)}) fusion(bf16[1,4,4,96,128]{4,3,2,1,0:T(8,128)(2,1)} %param.5, s32[]{:T(128)S(6)} %select_n.7, bf16[1,4,4,96,128]{4,3,2,1,0:T(8,128)(2,1)} %param.4), kind=kLoop, calls=%fused_computation.8 | loop fusion | bytes 393220 | tf_op jit(solution)/shard_map/jit(dynamic_index_in_dim)/squeeze | solution.py:347
  1.7 0.0 copy-start.1
  1.7 3.7 %collective-permute-start = (bf16[8,96,128]{2,1,0:T(8,128)(2,1)S(1)}, bf16[8,96,128]{2,1,0:T(8,128)(2,1)S(1)}, u32[]{:S(2)}, u32[]{:S(2)}) collective-permute-start(bf16[8,96,128]{2,1,0:T(8,128)(2,1)S(1)} %pad_maximum_fusion.4), channel_id=1, source_target_pairs={{0,1},{1,0},{2,3},{3,2},{4,5},{5,4},{6,7},{7,6},{8,9},{9,8},{10,11... | collective-permute-start | bytes 589832 | tf_op jit(solution)/shard_map/ppermute | solution.py:251
  5.4 0.0 copy-done
  5.4 0.1 pad_add_fusion.flags
  5.5 0.0 copy-done.1
  5.5 3.4 %collective-permute-done.side = bf16[8,96,128]{2,1,0:T(8,128)(2,1)S(1)} collective-permute-done((bf16[8,96,128]{2,1,0:T(8,128)(2,1)S(1)}, bf16[8,96,128]{2,1,0:T(8,128)(2,1)S(1)}, u32[]{:S(2)}, u32[]{:S(2)}) %collective-permute-start) | collective-permute-done | bytes 196640 | tf_op jit(solution)/shard_map/ppermute | solution.py:251
  8.9 0.0 copy-start.3
  8.9 0.0 copy-start.2
  9.0 6.1 %collective-permute-start.1 = (bf16[2,5,96,128]{3,2,1,0:T(8,128)(2,1)S(1)}, bf16[2,5,96,128]{3,2,1,0:T(8,128)(2,1)S(1)}, u32[]{:S(2)}, u32[]{:S(2)}) collective-permute-start(bf16[2,5,96,128]{3,2,1,0:T(8,128)(2,1)S(1)} %pad_maximum_fusion), channel_id=1, source_target_pairs={{0,2},{2,4},{4,6},{6,8},{8,10},{10,12},{12,14},{14,16},{16,18},{18... | collective-permute-start | bytes 737288 | tf_op jit(solution)/shard_map/ppermute | solution.py:254
  15.1 1.9 %collective-permute-start.2 = (bf16[2,5,96,128]{3,2,1,0:T(8,128)(2,1)S(1)}, bf16[2,5,96,128]{3,2,1,0:T(8,128)(2,1)S(1)}, u32[]{:S(2)}, u32[]{:S(2)}) collective-permute-start(bf16[2,5,96,128]{3,2,1,0:T(8,128)(2,1)S(1)} %pad_maximum_fusion.1), channel_id=1, source_target_pairs={{2,0},{4,2},{6,4},{8,6},{10,8},{12,10},{14,12},{16,14},{18,16},{20... | collective-permute-start | bytes 737288 | tf_op jit(solution)/shard_map/ppermute | solution.py:255
  17.0 0.0 copy-done.3
  17.0 0.0 copy-done.2
  17.1 1.8 %shard_map.75 = (bf16[288,864]{1,0:T(8,128)(2,1)S(1)}, bf16[288,864]{1,0:T(8,128)(2,1)S(1)}, bf16[288,864]{1,0:T(8,128)(2,1)S(1)}, bf16[288,864]{1,0:T(8,128)(2,1)S(1)}) custom-call(bf16[96,2592]{1,0:T(8,128)(2,1)S(1)} %bitcast.43, bf16[96,2592]{1,0:T(8,128)(2,1)S(1)} %bitcast.44), custom_call_target="tpu_custom_call" | custom-call | flops 3000000000 | bytes 1492992 | tf_op jit(solution)/shard_map/pallas_call | solution.py:222
  18.8 0.0 copy-start.4
  18.8 0.8 copy-done.4
  19.6 0.0 collective-permute-done.1.x_far
  19.6 3.0 %collective-permute-done.2.c_far = bf16[2,5,96,128]{3,2,1,0:T(8,128)(2,1)S(1)} collective-permute-done((bf16[2,5,96,128]{3,2,1,0:T(8,128)(2,1)S(1)}, bf16[2,5,96,128]{3,2,1,0:T(8,128)(2,1)S(1)}, u32[]{:S(2)}, u32[]{:S(2)}) %collective-permute-start.2) | collective-permute-done | bytes 245792 | tf_op jit(solution)/shard_map/ppermute | solution.py:255
  22.6 8.1 %shard_map.76 = (bf16[4,4,96,128]{3,2,1,0:T(8,128)(2,1)S(1)}, bf16[4,4,96,128]{3,2,1,0:T(8,128)(2,1)S(1)}, bf16[8,96,128]{2,1,0:T(8,128)(2,1)S(1)}, f32[8,256,128]{2,1,0:T(8,128)S(1)}, f32[8,256,128]{2,1,0:T(8,128)S(1)}) custom-call(s32[2]{0:T(128)S(1)} %pad_add_fusion.flags, bf16[4,4,96,128]{3,2,1,0:T(8,128)(2,1)S(1)} %bitcast.38, ...), custom_call_target="tpu_custom_call" | custom-call | flops 4076863488 | bytes 5550080 | tf_op jit(solution)/shard_map/pallas_call | solution.py:235
  30.7 0.1 collective-permute-start.3
  30.8 2.6 %collective-permute-done.3 = f32[8,256,128]{2,1,0:T(8,128)S(1)} collective-permute-done((f32[8,256,128]{2,1,0:T(8,128)S(1)}, f32[8,256,128]{2,1,0:T(8,128)S(1)}, u32[]{:S(2)}, u32[]{:S(2)}) %collective-permute-start.3) | collective-permute-done | bytes 1048608 | tf_op jit(solution)/shard_map/ppermute | solution.py:260
  33.5 0.9 add_convert_fusion
  34.4 2.7 %collective-permute-start.4 = (bf16[8,96,128]{2,1,0:T(8,128)(2,1)S(1)}, bf16[8,96,128]{2,1,0:T(8,128)(2,1)S(1)}, u32[]{:S(2)}, u32[]{:S(2)}) collective-permute-start(bf16[8,96,128]{2,1,0:T(8,128)(2,1)S(1)} %get-tuple-element.37), channel_id=1, source_target_pairs={{0,1},{1,0},{2,3},{3,2},{4,5},{5,4},{6,7},{7,6},{8,9},{9,8},{10,11... | collective-permute-start | bytes 589832 | tf_op jit(solution)/shard_map/ppermute | solution.py:251
  37.1 4.2 %all-to-all-start = ((bf16[8,256,128]{2,1,0:T(8,128)(2,1)}), bf16[8,256,128]{2,1,0:T(8,128)(2,1)S(1)}, u32[]{:S(2)}, u32[]{:S(2)}) async-start(bf16[8,256,128]{2,1,0:T(8,128)(2,1)} %add_convert_fusion), calls=%async_computation | async-start | bytes 1048576 | tf_op jit(solution)/shard_map/all_to_all | solution.py:264
  41.4 0.9 collective-permute-done.4.side
  42.3 0.7 pad_maximum_fusion.2
  43.0 4.4 %collective-permute-start.5 = (bf16[2,5,96,128]{3,2,1,0:T(8,128)(2,1)}, bf16[2,5,96,128]{3,2,1,0:T(8,128)(2,1)S(1)}, u32[]{:S(2)}, u32[]{:S(2)}) collective-permute-start(bf16[2,5,96,128]{3,2,1,0:T(8,128)(2,1)} %pad_maximum_fusion.2), channel_id=1, source_target_pairs={{0,2},{2,4},{4,6},{6,8},{8,10},{10,12},{12,14},{14,16},{16,18},{18... | collective-permute-start | bytes 737288 | tf_op jit(solution)/shard_map/ppermute | solution.py:254
  47.4 0.7 pad_maximum_fusion.3
  48.1 1.9 %collective-permute-start.6 = (bf16[2,5,96,128]{3,2,1,0:T(8,128)(2,1)}, bf16[2,5,96,128]{3,2,1,0:T(8,128)(2,1)S(1)}, u32[]{:S(2)}, u32[]{:S(2)}) collective-permute-start(bf16[2,5,96,128]{3,2,1,0:T(8,128)(2,1)} %pad_maximum_fusion.3), channel_id=1, source_target_pairs={{2,0},{4,2},{6,4},{8,6},{10,8},{12,10},{14,12},{16,14},{18,16},{20... | collective-permute-start | bytes 737288 | tf_op jit(solution)/shard_map/ppermute | solution.py:255
  50.0 0.0 all-to-all-done.arrived
  50.0 0.7 shard_map.77
  50.7 0.1 collective-permute-done.5.a_far
  50.8 5.0 %collective-permute-done.6.g_far = bf16[2,5,96,128]{3,2,1,0:T(8,128)(2,1)S(1)} collective-permute-done((bf16[2,5,96,128]{3,2,1,0:T(8,128)(2,1)}, bf16[2,5,96,128]{3,2,1,0:T(8,128)(2,1)S(1)}, u32[]{:S(2)}, u32[]{:S(2)}) %collective-permute-start.6) | collective-permute-done | bytes 245792 | tf_op jit(solution)/shard_map/ppermute | solution.py:255
  55.8 9.7 %all-to-all-start.1 = ((f32[16,16,128]{2,1,0:T(8,128)}), f32[16,16,128]{2,1,0:T(8,128)S(1)}, u32[]{:S(2)}, u32[]{:S(2)}) async-start(f32[16,16,128]{2,1,0:T(8,128)} %bitcast.18), calls=%async_computation.1 | async-start | bytes 262144 | tf_op jit(solution)/shard_map/all_to_all | solution.py:270
  65.5 0.0 copy-start.5
  65.6 1.0 %copy-done.5 = bf16[288,864]{1,0:T(8,128)(2,1)S(1)} copy-done((bf16[288,864]{1,0:T(8,128)(2,1)S(1)}, bf16[288,864]{1,0:T(8,128)(2,1)}, u32[]{:S(2)}) %copy-start.5) | copy-done | bytes 497688
  66.6 3.0 %shard_map.78 = f32[4,4,96,128]{3,2,1,0:T(8,128)} custom-call(s32[2]{0:T(128)S(1)} %pad_add_fusion.flags, bf16[4,4,96,128]{3,2,1,0:T(8,128)(2,1)S(1)} %bitcast.39, bf16[4,4,96,128]{3,2,1,0:T(8,128)(2,1)S(1)} %get-tuple-element.36.act, bf16[2,5,96,128]{3,2,1,0:T(8,128)(2,1)S(1)} %collective-permute-done.5.a_far, ...), custom_call_target="tpu_custom_call" | custom-call | flops 1019215872 | bytes 2512896 | tf_op jit(solution)/shard_map/pallas_call | solution.py:235
  69.6 6.6 %all-to-all-done.1 = f32[16,16,128]{2,1,0:T(8,128)S(1)} async-done(((f32[16,16,128]{2,1,0:T(8,128)}), f32[16,16,128]{2,1,0:T(8,128)S(1)}, u32[]{:S(2)}, u32[]{:S(2)}) %all-to-all-start.1) | async-done | bytes 131104 | tf_op jit(solution)/shard_map/all_to_all | solution.py:270
  76.2 0.7 broadcast_in_dim.29
  76.8 3.5 %all-to-all-start.2 = ((f32[16,16,128]{2,1,0:T(8,128)}), f32[16,16,128]{2,1,0:T(8,128)S(1)}, u32[]{:S(2)}, u32[]{:S(2)}) async-start(f32[16,16,128]{2,1,0:T(8,128)} %broadcast_in_dim.29), calls=%async_computation.2 | async-start | bytes 262144 | tf_op jit(solution)/shard_map/all_to_all | solution.py:270
  80.3 3.1 %shard_map.79 = f32[4,4,96,128]{3,2,1,0:T(8,128)} custom-call(s32[2]{0:T(128)S(1)} %pad_add_fusion.flags, bf16[4,4,96,128]{3,2,1,0:T(8,128)(2,1)S(1)} %bitcast.40, bf16[4,4,96,128]{3,2,1,0:T(8,128)(2,1)S(1)} %bitcast.42, bf16[4,4,96,128]{3,2,1,0:T(8,128)(2,1)S(1)} %get-tuple-element.38.grad, bf16[2,5,96,128]{3,2,1,0:T(8,128)(2,1)S(1)} %collective-permute-done.6.g_far, ...), custom_call_target="tpu_custom_call" | custom-call | flops 1019215872 | bytes 2906112 | tf_op jit(solution)/shard_map/pallas_call | solution.py:235
  83.4 6.9 %all-to-all-done.2 = f32[16,16,128]{2,1,0:T(8,128)S(1)} async-done(((f32[16,16,128]{2,1,0:T(8,128)}), f32[16,16,128]{2,1,0:T(8,128)S(1)}, u32[]{:S(2)}, u32[]{:S(2)}) %all-to-all-start.2) | async-done | bytes 131104 | tf_op jit(solution)/shard_map/all_to_all | solution.py:270
  90.4 2.5 %collective-permute-start.7 = (f32[256,128]{1,0:T(8,128)S(1)}, f32[256,128]{1,0:T(8,128)S(1)}, u32[]{:S(2)}, u32[]{:S(2)}) collective-permute-start(f32[256,128]{1,0:T(8,128)S(1)} %bitcast.36), channel_id=1, source_target_pairs={{0,2},{2,0},{1,3},{3,1},{4,6},{6,4},{5,7},{7,5},{8,10},{10,8},{9,1... | collective-permute-start | bytes 393224 | tf_op jit(solution)/shard_map/ppermute | solution.py:378
  92.9 1.0 %collective-permute-done.7.other = f32[256,128]{1,0:T(8,128)S(1)} collective-permute-done((f32[256,128]{1,0:T(8,128)S(1)}, f32[256,128]{1,0:T(8,128)S(1)}, u32[]{:S(2)}, u32[]{:S(2)}) %collective-permute-start.7) | collective-permute-done | bytes 131104 | tf_op jit(solution)/shard_map/ppermute | solution.py:378
  93.9 1.6 %shard_map.80 = (f32[96,324]{1,0:T(8,128)}, f32[96,324]{1,0:T(8,128)}) custom-call(s32[2]{0:T(128)S(1)} %pad_add_fusion.flags, f32[256,128]{1,0:T(8,128)S(1)} %bitcast.37, f32[256,128]{1,0:T(8,128)S(1)} %collective-permute-done.7.other), custom_call_target="tpu_custom_call" | custom-call | bytes 510984 | tf_op jit(solution)/shard_map/pallas_call | solution.py:307
  (10 shorter events, 0.2 us)
Async XLA Ops:
  0.6 4.7 %copy-start = (bf16[1,4,4,96,128]{4,3,2,1,0:T(8,128)(2,1)S(1)}, bf16[1,4,4,96,128]{4,3,2,1,0:T(8,128)(2,1)}, u32[]{:S(2)}) copy-start(bf16[1,4,4,96,128]{4,3,2,1,0:T(8,128)(2,1)} %param.4) | copy-start | bytes 1179652
  1.7 3.8 %copy-start.1 = (bf16[1,4,4,96,128]{4,3,2,1,0:T(8,128)(2,1)S(1)}, bf16[1,4,4,96,128]{4,3,2,1,0:T(8,128)(2,1)}, u32[]{:S(2)}) copy-start(bf16[1,4,4,96,128]{4,3,2,1,0:T(8,128)(2,1)} %param.5) | copy-start | bytes 1179652
  1.7 7.2 %collective-permute-start = (bf16[8,96,128]{2,1,0:T(8,128)(2,1)S(1)}, bf16[8,96,128]{2,1,0:T(8,128)(2,1)S(1)}, u32[]{:S(2)}, u32[]{:S(2)}) collective-permute-start(bf16[8,96,128]{2,1,0:T(8,128)(2,1)S(1)} %pad_maximum_fusion.4), channel_id=1, source_target_pairs={{0,1},{1,0},{2,3},{3,2},{4,5},{5,4},{6,7},{7,6},{8,9},{9,8},{10,11... | collective-permute-start | bytes 589832 | tf_op jit(solution)/shard_map/ppermute | solution.py:251
  8.9 8.1 %copy-start.3 = (bf16[2592,96]{0,1:T(8,128)(2,1)S(1)}, bf16[2592,96]{0,1:T(8,128)(2,1)}, u32[]{:S(2)}) copy-start(bf16[2592,96]{0,1:T(8,128)(2,1)} %param.7) | copy-start | bytes 1492996
  8.9 8.1 %copy-start.2 = (bf16[2592,96]{0,1:T(8,128)(2,1)S(1)}, bf16[2592,96]{0,1:T(8,128)(2,1)}, u32[]{:S(2)}) copy-start(bf16[2592,96]{0,1:T(8,128)(2,1)} %param.6) | copy-start | bytes 1492996
  9.0 10.6 %collective-permute-start.1 = (bf16[2,5,96,128]{3,2,1,0:T(8,128)(2,1)S(1)}, bf16[2,5,96,128]{3,2,1,0:T(8,128)(2,1)S(1)}, u32[]{:S(2)}, u32[]{:S(2)}) collective-permute-start(bf16[2,5,96,128]{3,2,1,0:T(8,128)(2,1)S(1)} %pad_maximum_fusion), channel_id=1, source_target_pairs={{0,2},{2,4},{4,6},{6,8},{8,10},{10,12},{12,14},{14,16},{16,18},{18... | collective-permute-start | bytes 737288 | tf_op jit(solution)/shard_map/ppermute | solution.py:254
  15.1 7.5 %collective-permute-start.2 = (bf16[2,5,96,128]{3,2,1,0:T(8,128)(2,1)S(1)}, bf16[2,5,96,128]{3,2,1,0:T(8,128)(2,1)S(1)}, u32[]{:S(2)}, u32[]{:S(2)}) collective-permute-start(bf16[2,5,96,128]{3,2,1,0:T(8,128)(2,1)S(1)} %pad_maximum_fusion.1), channel_id=1, source_target_pairs={{2,0},{4,2},{6,4},{8,6},{10,8},{12,10},{14,12},{16,14},{18,16},{20... | collective-permute-start | bytes 737288 | tf_op jit(solution)/shard_map/ppermute | solution.py:255
  18.8 0.8 copy-start.4
  30.7 2.7 %collective-permute-start.3 = (f32[8,256,128]{2,1,0:T(8,128)S(1)}, f32[8,256,128]{2,1,0:T(8,128)S(1)}, u32[]{:S(2)}, u32[]{:S(2)}) collective-permute-start(f32[8,256,128]{2,1,0:T(8,128)S(1)} %get-tuple-element.33), channel_id=1, source_target_pairs={{0,2},{2,0},{1,3},{3,1},{4,6},{6,4},{5,7},{7,5},{8,10},{10,8},{9,1... | collective-permute-start | bytes 3145736 | tf_op jit(solution)/shard_map/ppermute | solution.py:260
  34.4 7.9 %collective-permute-start.4 = (bf16[8,96,128]{2,1,0:T(8,128)(2,1)S(1)}, bf16[8,96,128]{2,1,0:T(8,128)(2,1)S(1)}, u32[]{:S(2)}, u32[]{:S(2)}) collective-permute-start(bf16[8,96,128]{2,1,0:T(8,128)(2,1)S(1)} %get-tuple-element.37), channel_id=1, source_target_pairs={{0,1},{1,0},{2,3},{3,2},{4,5},{5,4},{6,7},{7,6},{8,9},{9,8},{10,11... | collective-permute-start | bytes 589832 | tf_op jit(solution)/shard_map/ppermute | solution.py:251
  37.1 12.8 %all-to-all-start = ((bf16[8,256,128]{2,1,0:T(8,128)(2,1)}), bf16[8,256,128]{2,1,0:T(8,128)(2,1)S(1)}, u32[]{:S(2)}, u32[]{:S(2)}) async-start(bf16[8,256,128]{2,1,0:T(8,128)(2,1)} %add_convert_fusion), calls=%async_computation | async-start | bytes 1048576 | tf_op jit(solution)/shard_map/all_to_all | solution.py:264
  43.0 7.8 %collective-permute-start.5 = (bf16[2,5,96,128]{3,2,1,0:T(8,128)(2,1)}, bf16[2,5,96,128]{3,2,1,0:T(8,128)(2,1)S(1)}, u32[]{:S(2)}, u32[]{:S(2)}) collective-permute-start(bf16[2,5,96,128]{3,2,1,0:T(8,128)(2,1)} %pad_maximum_fusion.2), channel_id=1, source_target_pairs={{0,2},{2,4},{4,6},{6,8},{8,10},{10,12},{12,14},{14,16},{16,18},{18... | collective-permute-start | bytes 737288 | tf_op jit(solution)/shard_map/ppermute | solution.py:254
  48.1 7.7 %collective-permute-start.6 = (bf16[2,5,96,128]{3,2,1,0:T(8,128)(2,1)}, bf16[2,5,96,128]{3,2,1,0:T(8,128)(2,1)S(1)}, u32[]{:S(2)}, u32[]{:S(2)}) collective-permute-start(bf16[2,5,96,128]{3,2,1,0:T(8,128)(2,1)} %pad_maximum_fusion.3), channel_id=1, source_target_pairs={{2,0},{4,2},{6,4},{8,6},{10,8},{12,10},{14,12},{16,14},{18,16},{20... | collective-permute-start | bytes 737288 | tf_op jit(solution)/shard_map/ppermute | solution.py:255
  55.8 20.4 %all-to-all-start.1 = ((f32[16,16,128]{2,1,0:T(8,128)}), f32[16,16,128]{2,1,0:T(8,128)S(1)}, u32[]{:S(2)}, u32[]{:S(2)}) async-start(f32[16,16,128]{2,1,0:T(8,128)} %bitcast.18), calls=%async_computation.1 | async-start | bytes 262144 | tf_op jit(solution)/shard_map/all_to_all | solution.py:270
  65.5 1.0 %copy-start.5 = (bf16[288,864]{1,0:T(8,128)(2,1)S(1)}, bf16[288,864]{1,0:T(8,128)(2,1)}, u32[]{:S(2)}) copy-start(bf16[288,864]{1,0:T(8,128)(2,1)} %copy-done.4) | copy-start | bytes 1492996
  76.8 13.5 %all-to-all-start.2 = ((f32[16,16,128]{2,1,0:T(8,128)}), f32[16,16,128]{2,1,0:T(8,128)S(1)}, u32[]{:S(2)}, u32[]{:S(2)}) async-start(f32[16,16,128]{2,1,0:T(8,128)} %broadcast_in_dim.29), calls=%async_computation.2 | async-start | bytes 262144 | tf_op jit(solution)/shard_map/all_to_all | solution.py:270
  90.4 3.5 %collective-permute-start.7 = (f32[256,128]{1,0:T(8,128)S(1)}, f32[256,128]{1,0:T(8,128)S(1)}, u32[]{:S(2)}, u32[]{:S(2)}) collective-permute-start(f32[256,128]{1,0:T(8,128)S(1)} %bitcast.36), channel_id=1, source_target_pairs={{0,2},{2,0},{1,3},{3,1},{4,6},{6,4},{5,7},{7,5},{8,10},{10,8},{9,1... | collective-permute-start | bytes 393224 | tf_op jit(solution)/shard_map/ppermute | solution.py:378

commit v3 on v2

--- a/solution.py
+++ b/solution.py
@@ -11,7 +11,6 @@
 EPSILON = 1e-06
 TIME = ("z", "core")
 CLIP_AXES = ("x_lo", "y")
-PEER_AXES = ("z", "x_hi")
 HALVES = ("z", "core", "x_hi")
 SWAP = [(0, 1), (1, 0)]
 BF16, F32 = jnp.bfloat16, jnp.float32
@@ -243,17 +242,19 @@
     )(*args)
 
 
-def halos(earlier, later, side):
-    frames = earlier.shape[0]
-    peers = lax.axis_size(TIME)
-    ahead = [(i, i + 1) for i in range(peers - 1)]
-    behind = [(j, i) for i, j in ahead]
-    edge = lax.ppermute(side, "x_hi", SWAP)
-    last = jnp.concatenate([earlier[frames - 2 :], edge[frames - 2 : frames, None]], axis=1)
-    first = jnp.concatenate([later[:2], edge[frames : frames + 2, None]], axis=1)
-    far_a = lax.ppermute(last, TIME, ahead)
-    far_b = lax.ppermute(first, TIME, behind)
-    return far_a, far_b, edge
+def from_before(field, edge):
+    frames = field.shape[0]
+    sent = jnp.concatenate([field[frames - 2 :], edge[frames - 2 : frames, None]], axis=1)
+    return lax.ppermute(sent, TIME, [(i, i + 1) for i in range(lax.axis_size(TIME) - 1)])
+
+
+def ahead_of(field, edge):
+    frames = field.shape[0]
+    return jnp.concatenate([field[:2], edge[frames : frames + 2, None]], axis=1)
+
+
+def from_after(sent):
+    return lax.ppermute(sent, TIME, [(i + 1, i) for i in range(lax.axis_size(TIME) - 1)])
 
 
 def chip_total(kept, given):
@@ -267,7 +268,7 @@
 
 
 def exchanged(parts):
-    return lax.all_to_all(parts, PEER_AXES, 0, 0, tiled=True)
+    return lax.all_to_all(parts, "z", 0, 0, tiled=True)
 
 
 def total_kernel(arrived, total):
@@ -275,6 +276,12 @@
     for d in range(1, arrived.shape[0]):
         acc = acc + arrived[d].astype(F32)
     total[...] = acc
+
+
+def spread_kernel(mine, other, sent):
+    value = mine[...] + other[...]
+    for d in range(sent.shape[0]):
+        sent[d] = value
 
 
 def unpack_kernel(flags, whole, other, first, second):
@@ -347,7 +354,9 @@
         [lax.dynamic_index_in_dim(a, edge, 1, keepdims=False) for a in (source, upstream)], axis=0
     )
     w_one, w_two_back, w_two, w_one_back = weights(first_kernel.T, second_kernel.T)
-    x_far, c_far, side = halos(source, upstream, side)
+    side = lax.ppermute(side, "x_hi", SWAP)
+    x_far = from_before(source, side)
+    c_far = from_after(ahead_of(upstream, side))
 
     owners = lax.axis_size(CLIP_AXES)
     positions = frames * rows * cols * lax.axis_size(CLIP_AXES + HALVES)
@@ -357,19 +366,27 @@
     pairs = pltpu.VMEM((frames, rows + 2, channels, 2 * cols), BF16)
     conv_flops = 2 * 27 * channels * channels * frames * rows * cols
     out = jax.ShapeDtypeStruct(source.shape, F32)
-    peers = lax.axis_size(PEER_AXES)
+    peers = lax.axis_size("z")
+    part_shape = (MAIN // peers, cols)
+
     pieces, side = lax.optimization_barrier((chip_total(kept, given), side))
     clip_sum = clip_total(pieces)
-    a_far, g_far, side = halos(act, grad, side)
-    clip_sum, a_far, g_far, side = lax.optimization_barrier((clip_sum, a_far, g_far, side))
-    parts = exchanged(clip_sum.reshape(peers, MAIN // peers, -1))
+    side = lax.ppermute(side, "x_hi", SWAP)
+    a_far = from_before(act, side)
+    clip_sum, g_sent = lax.optimization_barrier((clip_sum, ahead_of(grad, side)))
+    parts = exchanged(clip_sum.reshape((peers,) + part_shape))
+    g_far = from_after(g_sent)
+    part = jax.ShapeDtypeStruct(part_shape, F32)
+    (part_sum,) = small_call(total_kernel, (part,), (parts,), False)
+    part_sum, a_far = lax.optimization_barrier((part_sum, a_far))
+    part_other = lax.ppermute(part_sum, "x_hi", SWAP)
     (block_output,) = call(
         branch_kernel, (out,), [pairs], conv_flops, (flags, source, act, a_far, side, w_two)
     )
-    parts, block_output, g_far, side = lax.optimization_barrier((parts, block_output, g_far, side))
-    part_sum = jnp.sum(parts, axis=0)
-    sent = jnp.broadcast_to(part_sum[None], (peers,) + part_sum.shape)
-    sent, g_far, side = lax.optimization_barrier((sent, g_far, side))
+    part_other, block_output = lax.optimization_barrier((part_other, block_output))
+    spread = jax.ShapeDtypeStruct((peers,) + part_shape, F32)
+    (sent,) = small_call(spread_kernel, (spread,), (part_sum, part_other), False)
+    sent, g_far = lax.optimization_barrier((sent, g_far))
     whole = exchanged(sent).reshape(MAIN, -1)
     (input_grad,) = call(
         input_kernel, (out,), [pairs], conv_flops, (flags, source, upstream, grad, g_far, side, w_one_back)

time: 96 us -> 92.4 us (0.963)
  waiting for transfers between devices: 29.5 us -> 21.5 us
  starting transfers between devices: 40.7 us -> 45.9 us
    all_to_all x2, waiting for transfers between devices: 13.5 us -> 8.41 us  [exchanged(): return lax.all_to_all(parts, 'z', 0, 0, tiled=True)]
    ppermute x6 -> x7, waiting for transfers between devices: 12.4 us -> 7.34 us  [the longest x2 4.32 us: local(): side = lax.ppermute(side, 'x_hi', SWAP)]
    ppermute x6 -> x7, starting transfers between devices: 20.7 us -> 25.2 us  [the longest x2 10.4 us: from_before(): lax.ppermute(sent, TIME, [(i, i + 1) for i in range(lax.axis_size(TIME) -...]
    ppermute x1, starting transfers between devices: 2.51 us -> 4.96 us  [local(): other = lax.ppermute(whole, 'core', SWAP)]
    all_to_all x1, waiting for transfers between devices: 0.01 us -> 2.12 us  [clip_total(): arrived = lax.all_to_all(pieces, CLIP_AXES, 0, 0, tiled=True)]
    all_to_all x2, starting transfers between devices: 13.3 us -> 11.4 us  [exchanged(): return lax.all_to_all(parts, 'z', 0, 0, tiled=True)]
    pallas_call x2 -> x4, Pallas kernels: 2.31 us -> 2.99 us  [small_call(): pl.pallas_call(kernel, out_shape=outs, in_specs=specs, out_specs=[vmem] *...]
  transfers between devices with their start and end apart: 11 -> 12, of which waited for: 9 -> 8; matrix products, arithmetic and copies ran while one was open for 2% -> 1% of each run, Pallas kernels for 9% -> 10%
where the time goes in v3:
time: 92.4 us; the launch traced here: 91.8 us
  starting transfers between devices  45.9 us (50%)
  waiting for transfers between devices  21.5 us (23%)
  Pallas kernels  18.9 us (20%)
  local copies, waits for them, and re-layouts  2.92 us (3%)
  other arithmetic  1.79 us (2%)
    pallas_call x3, Pallas kernels, call(): pl.pallas_call(kernel, out_shape=outs, in_specs=[pl.BlockSpec(memory_spac...  14.2 us
    all_to_all x2, starting transfers between devices, exchanged(): return lax.all_to_all(parts, 'z', 0, 0, tiled=True)  11.4 us
    ppermute x2, starting transfers between devices, from_before(): lax.ppermute(sent, TIME, [(i, i + 1) for i in range(lax.axis_size(TIME) -...  10.4 us
    all_to_all x2, waiting for transfers between devices, exchanged(): return lax.all_to_all(parts, 'z', 0, 0, tiled=True)  8.41 us
    ppermute x2, starting transfers between devices, local(): side = lax.ppermute(side, 'x_hi', SWAP)  6.38 us
    ppermute x2, starting transfers between devices, from_after(): lax.ppermute(sent, TIME, [(i + 1, i) for i in range(lax.axis_size(TIME) -...  6.34 us
    ppermute x1, starting transfers between devices, local(): other = lax.ppermute(whole, 'core', SWAP)  4.96 us
    ppermute x2, waiting for transfers between devices, local(): side = lax.ppermute(side, 'x_hi', SWAP)  4.32 us
  transfers between devices with their start and end apart: 12, of which 8 were waited for; matrix products, arithmetic and copies ran while one was open for 1% of the time, Pallas kernels for 10%

profile of v3, /device:TPU:1, one launch (start us, length us, event | category | flops | bytes accessed | tf_op | source)
XLA Modules:
  0.0 91.8 jit_solution(7971341092645384053)
XLA Ops:
  0.6 0.0 copy-start
  0.6 1.0 %dynamic-slice_bitcast_fusion = (bf16[4,96,128]{2,1,0:T(8,128)(2,1)S(1)}, bf16[4,96,128]{2,1,0:T(8,128)(2,1)S(1)}) fusion(bf16[1,4,4,96,128]{4,3,2,1,0:T(8,128)(2,1)} %param.5, s32[]{:T(128)S(6)} %select_n.7, bf16[1,4,4,96,128]{4,3,2,1,0:T(8,128)(2,1)} %param.4), kind=kLoop, calls=%fused_computation.8 | loop fusion | bytes 393220 | tf_op jit(solution)/shard_map/jit(dynamic_index_in_dim)/squeeze | solution.py:354
  1.7 0.0 copy-start.1
  1.7 3.7 %collective-permute-start = (bf16[8,96,128]{2,1,0:T(8,128)(2,1)S(1)}, bf16[8,96,128]{2,1,0:T(8,128)(2,1)S(1)}, u32[]{:S(2)}, u32[]{:S(2)}) collective-permute-start(bf16[8,96,128]{2,1,0:T(8,128)(2,1)S(1)} %pad_maximum_fusion.4), channel_id=1, source_target_pairs={{0,1},{1,0},{2,3},{3,2},{4,5},{5,4},{6,7},{7,6},{8,9},{9,8},{10,11... | collective-permute-start | bytes 589832 | tf_op jit(solution)/shard_map/ppermute | solution.py:357
  5.4 0.0 copy-done
  5.4 0.1 pad_add_fusion.flags
  5.5 0.0 copy-done.1
  5.5 3.4 %collective-permute-done.side = bf16[8,96,128]{2,1,0:T(8,128)(2,1)S(1)} collective-permute-done((bf16[8,96,128]{2,1,0:T(8,128)(2,1)S(1)}, bf16[8,96,128]{2,1,0:T(8,128)(2,1)S(1)}, u32[]{:S(2)}, u32[]{:S(2)}) %collective-permute-start) | collective-permute-done | bytes 196640 | tf_op jit(solution)/shard_map/ppermute | solution.py:357
  8.9 0.0 copy-start.3
  8.9 0.0 copy-start.2
  9.0 6.1 %collective-permute-start.1 = (bf16[2,5,96,128]{3,2,1,0:T(8,128)(2,1)S(1)}, bf16[2,5,96,128]{3,2,1,0:T(8,128)(2,1)S(1)}, u32[]{:S(2)}, u32[]{:S(2)}) collective-permute-start(bf16[2,5,96,128]{3,2,1,0:T(8,128)(2,1)S(1)} %pad_maximum_fusion), channel_id=1, source_target_pairs={{0,2},{2,4},{4,6},{6,8},{8,10},{10,12},{12,14},{14,16},{16,18},{18... | collective-permute-start | bytes 737288 | tf_op jit(solution)/shard_map/ppermute | solution.py:248
  15.1 1.9 %collective-permute-start.2 = (bf16[2,5,96,128]{3,2,1,0:T(8,128)(2,1)S(1)}, bf16[2,5,96,128]{3,2,1,0:T(8,128)(2,1)S(1)}, u32[]{:S(2)}, u32[]{:S(2)}) collective-permute-start(bf16[2,5,96,128]{3,2,1,0:T(8,128)(2,1)S(1)} %pad_maximum_fusion.1), channel_id=1, source_target_pairs={{2,0},{4,2},{6,4},{8,6},{10,8},{12,10},{14,12},{16,14},{18,16},{20... | collective-permute-start | bytes 737288 | tf_op jit(solution)/shard_map/ppermute | solution.py:257
  17.0 0.0 copy-done.3
  17.0 0.0 copy-done.2
  17.1 1.8 %shard_map.75 = (bf16[288,864]{1,0:T(8,128)(2,1)S(1)}, bf16[288,864]{1,0:T(8,128)(2,1)S(1)}, bf16[288,864]{1,0:T(8,128)(2,1)S(1)}, bf16[288,864]{1,0:T(8,128)(2,1)S(1)}) custom-call(bf16[96,2592]{1,0:T(8,128)(2,1)S(1)} %bitcast.43, bf16[96,2592]{1,0:T(8,128)(2,1)S(1)} %bitcast.44), custom_call_target="tpu_custom_call" | custom-call | flops 3000000000 | bytes 1492992 | tf_op jit(solution)/shard_map/pallas_call | solution.py:221
  18.8 0.0 copy-start.4
  18.8 0.8 copy-done.4
  19.6 0.0 collective-permute-done.1.x_far
  19.6 3.0 %collective-permute-done.2.c_far = bf16[2,5,96,128]{3,2,1,0:T(8,128)(2,1)S(1)} collective-permute-done((bf16[2,5,96,128]{3,2,1,0:T(8,128)(2,1)S(1)}, bf16[2,5,96,128]{3,2,1,0:T(8,128)(2,1)S(1)}, u32[]{:S(2)}, u32[]{:S(2)}) %collective-permute-start.2) | collective-permute-done | bytes 245792 | tf_op jit(solution)/shard_map/ppermute | solution.py:257
  22.6 8.1 %shard_map.76 = (bf16[4,4,96,128]{3,2,1,0:T(8,128)(2,1)S(1)}, bf16[4,4,96,128]{3,2,1,0:T(8,128)(2,1)S(1)}, bf16[8,96,128]{2,1,0:T(8,128)(2,1)S(1)}, f32[8,256,128]{2,1,0:T(8,128)S(1)}, f32[8,256,128]{2,1,0:T(8,128)S(1)}) custom-call(s32[2]{0:T(128)S(1)} %pad_add_fusion.flags, bf16[4,4,96,128]{3,2,1,0:T(8,128)(2,1)S(1)} %bitcast.38, ...), custom_call_target="tpu_custom_call" | custom-call | flops 4076863488 | bytes 5550080 | tf_op jit(solution)/shard_map/pallas_call | solution.py:234
  30.7 0.1 collective-permute-start.3
  30.8 2.6 %collective-permute-done.3 = f32[8,256,128]{2,1,0:T(8,128)S(1)} collective-permute-done((f32[8,256,128]{2,1,0:T(8,128)S(1)}, f32[8,256,128]{2,1,0:T(8,128)S(1)}, u32[]{:S(2)}, u32[]{:S(2)}) %collective-permute-start.3) | collective-permute-done | bytes 1048608 | tf_op jit(solution)/shard_map/ppermute | solution.py:261
  33.5 0.9 add_convert_fusion
  34.4 2.7 %collective-permute-start.4 = (bf16[8,96,128]{2,1,0:T(8,128)(2,1)S(1)}, bf16[8,96,128]{2,1,0:T(8,128)(2,1)S(1)}, u32[]{:S(2)}, u32[]{:S(2)}) collective-permute-start(bf16[8,96,128]{2,1,0:T(8,128)(2,1)S(1)} %get-tuple-element.34), channel_id=1, source_target_pairs={{0,1},{1,0},{2,3},{3,2},{4,5},{5,4},{6,7},{7,6},{8,9},{9,8},{10,11... | collective-permute-start | bytes 589832 | tf_op jit(solution)/shard_map/ppermute | solution.py:374
  37.1 4.2 %all-to-all-start = ((bf16[8,256,128]{2,1,0:T(8,128)(2,1)}), bf16[8,256,128]{2,1,0:T(8,128)(2,1)S(1)}, u32[]{:S(2)}, u32[]{:S(2)}) async-start(bf16[8,256,128]{2,1,0:T(8,128)(2,1)} %add_convert_fusion), calls=%async_computation | async-start | bytes 1048576 | tf_op jit(solution)/shard_map/all_to_all | solution.py:265
  41.4 0.9 collective-permute-done.4.side
  42.3 0.7 pad_maximum_fusion.3
  43.0 4.4 %collective-permute-start.5 = (bf16[2,5,96,128]{3,2,1,0:T(8,128)(2,1)}, bf16[2,5,96,128]{3,2,1,0:T(8,128)(2,1)S(1)}, u32[]{:S(2)}, u32[]{:S(2)}) collective-permute-start(bf16[2,5,96,128]{3,2,1,0:T(8,128)(2,1)} %pad_maximum_fusion.3), channel_id=1, source_target_pairs={{0,2},{2,4},{4,6},{6,8},{8,10},{10,12},{12,14},{14,16},{16,18},{18... | collective-permute-start | bytes 737288 | tf_op jit(solution)/shard_map/ppermute | solution.py:248
  47.4 2.1 %all-to-all-done.arrived = bf16[8,256,128]{2,1,0:T(8,128)(2,1)S(1)} async-done(((bf16[8,256,128]{2,1,0:T(8,128)(2,1)}), bf16[8,256,128]{2,1,0:T(8,128)(2,1)S(1)}, u32[]{:S(2)}, u32[]{:S(2)}) %all-to-all-start) | async-done | bytes 524320 | tf_op jit(solution)/shard_map/all_to_all | solution.py:265
  49.5 0.7 shard_map.77
  50.2 8.0 %all-to-all-start.1 = ((f32[8,32,128]{2,1,0:T(8,128)}), f32[8,32,128]{2,1,0:T(8,128)S(1)}, u32[]{:S(2)}, u32[]{:S(2)}) async-start(f32[8,32,128]{2,1,0:T(8,128)} %bitcast.16), calls=%async_computation.1 | async-start | bytes 262144 | tf_op jit(solution)/shard_map/all_to_all | solution.py:271
  58.3 4.4 %collective-permute-start.7 = (bf16[2,5,96,128]{3,2,1,0:T(8,128)(2,1)S(1)}, bf16[2,5,96,128]{3,2,1,0:T(8,128)(2,1)S(1)}, u32[]{:S(2)}, u32[]{:S(2)}) collective-permute-start(bf16[2,5,96,128]{3,2,1,0:T(8,128)(2,1)S(1)} %pad_maximum_fusion.2), channel_id=1, source_target_pairs={{2,0},{4,2},{6,4},{8,6},{10,8},{12,10},{14,12},{16,14},{18,16},{20... | collective-permute-start | bytes 737288 | tf_op jit(solution)/shard_map/ppermute | solution.py:257
  62.7 3.6 %all-to-all-done.1.arrived = f32[8,32,128]{2,1,0:T(8,128)S(1)} async-done(((f32[8,32,128]{2,1,0:T(8,128)}), f32[8,32,128]{2,1,0:T(8,128)S(1)}, u32[]{:S(2)}, u32[]{:S(2)}) %all-to-all-start.1) | async-done | bytes 131104 | tf_op jit(solution)/shard_map/all_to_all | solution.py:271
  66.3 0.0 collective-permute-done.5.a_far
  66.3 2.0 %collective-permute-start.6 = (f32[32,128]{1,0:T(8,128)S(1)}, f32[32,128]{1,0:T(8,128)S(1)}, u32[]{:S(2)}, u32[]{:S(2)}) collective-permute-start(f32[32,128]{1,0:T(8,128)S(1)} %shard_map.78.mine), channel_id=1, source_target_pairs={{0,1},{1,0},{2,3},{3,2},{4,5},{5,4},{6,7},{7,6},{8,9},{9,8},{10,11... | collective-permute-start | bytes 49160 | tf_op jit(solution)/shard_map/ppermute | solution.py:382
  68.3 0.0 copy-start.5
  68.4 1.0 %copy-done.5 = bf16[288,864]{1,0:T(8,128)(2,1)S(1)} copy-done((bf16[288,864]{1,0:T(8,128)(2,1)S(1)}, bf16[288,864]{1,0:T(8,128)(2,1)}, u32[]{:S(2)}) %copy-start.5) | copy-done | bytes 497688
  69.4 3.0 %shard_map.79 = f32[4,4,96,128]{3,2,1,0:T(8,128)} custom-call(s32[2]{0:T(128)S(1)} %pad_add_fusion.flags, bf16[4,4,96,128]{3,2,1,0:T(8,128)(2,1)S(1)} %bitcast.39, bf16[4,4,96,128]{3,2,1,0:T(8,128)(2,1)S(1)} %get-tuple-element.36.act, bf16[2,5,96,128]{3,2,1,0:T(8,128)(2,1)S(1)} %collective-permute-done.5.a_far, ...), custom_call_target="tpu_custom_call" | custom-call | flops 1019215872 | bytes 2512896 | tf_op jit(solution)/shard_map/pallas_call | solution.py:234
  72.4 0.0 collective-permute-done.6.other
  72.4 0.7 shard_map.80
  73.0 0.0 collective-permute-done.7.g_far
  73.0 3.4 %all-to-all-start.2 = ((f32[8,32,128]{2,1,0:T(8,128)}), f32[8,32,128]{2,1,0:T(8,128)S(1)}, u32[]{:S(2)}, u32[]{:S(2)}) async-start(f32[8,32,128]{2,1,0:T(8,128)} %shard_map.80), calls=%async_computation.2 | async-start | bytes 262144 | tf_op jit(solution)/shard_map/all_to_all | solution.py:271
  76.4 3.1 %shard_map.81 = f32[4,4,96,128]{3,2,1,0:T(8,128)} custom-call(s32[2]{0:T(128)S(1)} %pad_add_fusion.flags, bf16[4,4,96,128]{3,2,1,0:T(8,128)(2,1)S(1)} %bitcast.40, bf16[4,4,96,128]{3,2,1,0:T(8,128)(2,1)S(1)} %bitcast.42, bf16[4,4,96,128]{3,2,1,0:T(8,128)(2,1)S(1)} %get-tuple-element.33.grad, bf16[2,5,96,128]{3,2,1,0:T(8,128)(2,1)S(1)} %collective-permute-done.7.g_far, ...), custom_call_target="tpu_custom_call" | custom-call | flops 1019215872 | bytes 2906112 | tf_op jit(solution)/shard_map/pallas_call | solution.py:234
  79.5 4.8 %all-to-all-done.2 = f32[8,32,128]{2,1,0:T(8,128)S(1)} async-done(((f32[8,32,128]{2,1,0:T(8,128)}), f32[8,32,128]{2,1,0:T(8,128)S(1)}, u32[]{:S(2)}, u32[]{:S(2)}) %all-to-all-start.2) | async-done | bytes 131104 | tf_op jit(solution)/shard_map/all_to_all | solution.py:271
  84.3 5.0 %collective-permute-start.8 = (f32[256,128]{1,0:T(8,128)S(1)}, f32[256,128]{1,0:T(8,128)S(1)}, u32[]{:S(2)}, u32[]{:S(2)}) collective-permute-start(f32[256,128]{1,0:T(8,128)S(1)} %bitcast.36), channel_id=1, source_target_pairs={{0,2},{2,0},{1,3},{3,1},{4,6},{6,4},{5,7},{7,5},{8,10},{10,8},{9,1... | collective-permute-start | bytes 393224 | tf_op jit(solution)/shard_map/ppermute | solution.py:395
  89.3 1.0 %collective-permute-done.8.other = f32[256,128]{1,0:T(8,128)S(1)} collective-permute-done((f32[256,128]{1,0:T(8,128)S(1)}, f32[256,128]{1,0:T(8,128)S(1)}, u32[]{:S(2)}, u32[]{:S(2)}) %collective-permute-start.8) | collective-permute-done | bytes 131104 | tf_op jit(solution)/shard_map/ppermute | solution.py:395
  90.3 1.6 %shard_map.82 = (f32[96,324]{1,0:T(8,128)}, f32[96,324]{1,0:T(8,128)}) custom-call(s32[2]{0:T(128)S(1)} %pad_add_fusion.flags, f32[256,128]{1,0:T(8,128)S(1)} %bitcast.37, f32[256,128]{1,0:T(8,128)S(1)} %collective-permute-done.8.other), custom_call_target="tpu_custom_call" | custom-call | bytes 510984 | tf_op jit(solution)/shard_map/pallas_call | solution.py:314
  (11 shorter events, 0.2 us)
Async XLA Ops:
  0.6 4.7 %copy-start = (bf16[1,4,4,96,128]{4,3,2,1,0:T(8,128)(2,1)S(1)}, bf16[1,4,4,96,128]{4,3,2,1,0:T(8,128)(2,1)}, u32[]{:S(2)}) copy-start(bf16[1,4,4,96,128]{4,3,2,1,0:T(8,128)(2,1)} %param.4) | copy-start | bytes 1179652
  1.7 3.8 %copy-start.1 = (bf16[1,4,4,96,128]{4,3,2,1,0:T(8,128)(2,1)S(1)}, bf16[1,4,4,96,128]{4,3,2,1,0:T(8,128)(2,1)}, u32[]{:S(2)}) copy-start(bf16[1,4,4,96,128]{4,3,2,1,0:T(8,128)(2,1)} %param.5) | copy-start | bytes 1179652
  1.7 7.2 %collective-permute-start = (bf16[8,96,128]{2,1,0:T(8,128)(2,1)S(1)}, bf16[8,96,128]{2,1,0:T(8,128)(2,1)S(1)}, u32[]{:S(2)}, u32[]{:S(2)}) collective-permute-start(bf16[8,96,128]{2,1,0:T(8,128)(2,1)S(1)} %pad_maximum_fusion.4), channel_id=1, source_target_pairs={{0,1},{1,0},{2,3},{3,2},{4,5},{5,4},{6,7},{7,6},{8,9},{9,8},{10,11... | collective-permute-start | bytes 589832 | tf_op jit(solution)/shard_map/ppermute | solution.py:357
  8.9 8.1 %copy-start.3 = (bf16[2592,96]{0,1:T(8,128)(2,1)S(1)}, bf16[2592,96]{0,1:T(8,128)(2,1)}, u32[]{:S(2)}) copy-start(bf16[2592,96]{0,1:T(8,128)(2,1)} %param.7) | copy-start | bytes 1492996
  8.9 8.1 %copy-start.2 = (bf16[2592,96]{0,1:T(8,128)(2,1)S(1)}, bf16[2592,96]{0,1:T(8,128)(2,1)}, u32[]{:S(2)}) copy-start(bf16[2592,96]{0,1:T(8,128)(2,1)} %param.6) | copy-start | bytes 1492996
  9.0 10.6 %collective-permute-start.1 = (bf16[2,5,96,128]{3,2,1,0:T(8,128)(2,1)S(1)}, bf16[2,5,96,128]{3,2,1,0:T(8,128)(2,1)S(1)}, u32[]{:S(2)}, u32[]{:S(2)}) collective-permute-start(bf16[2,5,96,128]{3,2,1,0:T(8,128)(2,1)S(1)} %pad_maximum_fusion), channel_id=1, source_target_pairs={{0,2},{2,4},{4,6},{6,8},{8,10},{10,12},{12,14},{14,16},{16,18},{18... | collective-permute-start | bytes 737288 | tf_op jit(solution)/shard_map/ppermute | solution.py:248
  15.1 7.5 %collective-permute-start.2 = (bf16[2,5,96,128]{3,2,1,0:T(8,128)(2,1)S(1)}, bf16[2,5,96,128]{3,2,1,0:T(8,128)(2,1)S(1)}, u32[]{:S(2)}, u32[]{:S(2)}) collective-permute-start(bf16[2,5,96,128]{3,2,1,0:T(8,128)(2,1)S(1)} %pad_maximum_fusion.1), channel_id=1, source_target_pairs={{2,0},{4,2},{6,4},{8,6},{10,8},{12,10},{14,12},{16,14},{18,16},{20... | collective-permute-start | bytes 737288 | tf_op jit(solution)/shard_map/ppermute | solution.py:257
  18.8 0.8 copy-start.4
  30.7 2.7 %collective-permute-start.3 = (f32[8,256,128]{2,1,0:T(8,128)S(1)}, f32[8,256,128]{2,1,0:T(8,128)S(1)}, u32[]{:S(2)}, u32[]{:S(2)}) collective-permute-start(f32[8,256,128]{2,1,0:T(8,128)S(1)} %get-tuple-element.30), channel_id=1, source_target_pairs={{0,2},{2,0},{1,3},{3,1},{4,6},{6,4},{5,7},{7,5},{8,10},{10,8},{9,1... | collective-permute-start | bytes 3145736 | tf_op jit(solution)/shard_map/ppermute | solution.py:261
  34.4 7.9 %collective-permute-start.4 = (bf16[8,96,128]{2,1,0:T(8,128)(2,1)S(1)}, bf16[8,96,128]{2,1,0:T(8,128)(2,1)S(1)}, u32[]{:S(2)}, u32[]{:S(2)}) collective-permute-start(bf16[8,96,128]{2,1,0:T(8,128)(2,1)S(1)} %get-tuple-element.34), channel_id=1, source_target_pairs={{0,1},{1,0},{2,3},{3,2},{4,5},{5,4},{6,7},{7,6},{8,9},{9,8},{10,11... | collective-permute-start | bytes 589832 | tf_op jit(solution)/shard_map/ppermute | solution.py:374
  37.1 12.4 %all-to-all-start = ((bf16[8,256,128]{2,1,0:T(8,128)(2,1)}), bf16[8,256,128]{2,1,0:T(8,128)(2,1)S(1)}, u32[]{:S(2)}, u32[]{:S(2)}) async-start(bf16[8,256,128]{2,1,0:T(8,128)(2,1)} %add_convert_fusion), calls=%async_computation | async-start | bytes 1048576 | tf_op jit(solution)/shard_map/all_to_all | solution.py:265
  43.0 23.3 %collective-permute-start.5 = (bf16[2,5,96,128]{3,2,1,0:T(8,128)(2,1)}, bf16[2,5,96,128]{3,2,1,0:T(8,128)(2,1)S(1)}, u32[]{:S(2)}, u32[]{:S(2)}) collective-permute-start(bf16[2,5,96,128]{3,2,1,0:T(8,128)(2,1)} %pad_maximum_fusion.3), channel_id=1, source_target_pairs={{0,2},{2,4},{4,6},{6,8},{8,10},{10,12},{12,14},{14,16},{16,18},{18... | collective-permute-start | bytes 737288 | tf_op jit(solution)/shard_map/ppermute | solution.py:248
  50.2 16.1 %all-to-all-start.1 = ((f32[8,32,128]{2,1,0:T(8,128)}), f32[8,32,128]{2,1,0:T(8,128)S(1)}, u32[]{:S(2)}, u32[]{:S(2)}) async-start(f32[8,32,128]{2,1,0:T(8,128)} %bitcast.16), calls=%async_computation.1 | async-start | bytes 262144 | tf_op jit(solution)/shard_map/all_to_all | solution.py:271
  58.3 14.8 %collective-permute-start.7 = (bf16[2,5,96,128]{3,2,1,0:T(8,128)(2,1)S(1)}, bf16[2,5,96,128]{3,2,1,0:T(8,128)(2,1)S(1)}, u32[]{:S(2)}, u32[]{:S(2)}) collective-permute-start(bf16[2,5,96,128]{3,2,1,0:T(8,128)(2,1)S(1)} %pad_maximum_fusion.2), channel_id=1, source_target_pairs={{2,0},{4,2},{6,4},{8,6},{10,8},{12,10},{14,12},{16,14},{18,16},{20... | collective-permute-start | bytes 737288 | tf_op jit(solution)/shard_map/ppermute | solution.py:257
  66.3 6.0 %collective-permute-start.6 = (f32[32,128]{1,0:T(8,128)S(1)}, f32[32,128]{1,0:T(8,128)S(1)}, u32[]{:S(2)}, u32[]{:S(2)}) collective-permute-start(f32[32,128]{1,0:T(8,128)S(1)} %shard_map.78.mine), channel_id=1, source_target_pairs={{0,1},{1,0},{2,3},{3,2},{4,5},{5,4},{6,7},{7,6},{8,9},{9,8},{10,11... | collective-permute-start | bytes 49160 | tf_op jit(solution)/shard_map/ppermute | solution.py:382
  68.3 1.0 %copy-start.5 = (bf16[288,864]{1,0:T(8,128)(2,1)S(1)}, bf16[288,864]{1,0:T(8,128)(2,1)}, u32[]{:S(2)}) copy-start(bf16[288,864]{1,0:T(8,128)(2,1)} %copy-done.4) | copy-start | bytes 1492996
  73.0 11.3 %all-to-all-start.2 = ((f32[8,32,128]{2,1,0:T(8,128)}), f32[8,32,128]{2,1,0:T(8,128)S(1)}, u32[]{:S(2)}, u32[]{:S(2)}) async-start(f32[8,32,128]{2,1,0:T(8,128)} %shard_map.80), calls=%async_computation.2 | async-start | bytes 262144 | tf_op jit(solution)/shard_map/all_to_all | solution.py:271
  84.3 5.9 %collective-permute-start.8 = (f32[256,128]{1,0:T(8,128)S(1)}, f32[256,128]{1,0:T(8,128)S(1)}, u32[]{:S(2)}, u32[]{:S(2)}) collective-permute-start(f32[256,128]{1,0:T(8,128)S(1)} %bitcast.36), channel_id=1, source_target_pairs={{0,2},{2,0},{1,3},{3,1},{4,6},{6,4},{5,7},{7,5},{8,10},{10,8},{9,1... | collective-permute-start | bytes 393224 | tf_op jit(solution)/shard_map/ppermute | solution.py:395

commit v4 on v3

--- a/solution.py
+++ b/solution.py
@@ -172,11 +172,12 @@
                 else:
                     strip = jnp.zeros((STRIP, cols), F32)
                 mixed = jnp.where(lane[:height] < channels, main, strip[:height])
-                target[d, pl.ds(s * STRIP, height), :] = mixed * scale
-
-
-def branch_kernel(flags, x, act, a_far, side, w_two, block_out, pa):
+                target[d, pl.ds(s * STRIP, height), :] = (mixed * scale).astype(target.dtype)
+
+
+def branch_kernel(flags, x, act, a_far, side, k_two, block_out, pa, w_two):
     frames, rows, channels, cols = x.shape
+    lay_forward(k_two, w_two)
     fill(pa, act, a_far, side, 0, False, flags[0] == 0, lambda v: v)
     for f in range(frames // 2):
 
@@ -204,15 +205,28 @@
                 input_out[at, r] = c[at, r].astype(F32) + grad_in
 
 
-def weights_kernel(first, second, w_one, w_two_back, w_two, w_one_back):
-    channels = first.shape[0]
-    for source, ahead, back in ((first, w_one, w_one_back), (second, w_two, w_two_back)):
-        whole = source[...].astype(F32)
-        taps = [whole[:, t * channels : (t + 1) * channels] for t in range(27)]
-        for kw in range(3):
-            rows = pl.ds(kw * channels, channels)
-            ahead[rows, :] = jnp.concatenate([taps[3 * k + kw] for k in range(9)], axis=1).astype(BF16)
-            back[rows, :] = jnp.concatenate([taps[26 - 3 * k - kw].T for k in range(9)], axis=1).astype(BF16)
+def lay_forward(kernel, laid):
+    channels = kernel.shape[0]
+    whole = kernel[...].astype(F32)
+    taps = [whole[:, t * channels : (t + 1) * channels] for t in range(27)]
+    for kw in range(3):
+        row = jnp.concatenate([taps[3 * k + kw] for k in range(9)], axis=1)
+        laid[pl.ds(kw * channels, channels), :] = row.astype(BF16)
+
+
+def lay_backward(kernel, laid):
+    channels = kernel.shape[0]
+    whole = kernel[...].astype(F32)
+    taps = [whole[:, t * channels : (t + 1) * channels] for t in range(27)]
+    for kw in range(3):
+        row = jnp.concatenate([taps[26 - 3 * k - kw].T for k in range(9)], axis=1)
+        laid[pl.ds(kw * channels, channels), :] = row.astype(BF16)
+
+
+def weights_kernel(first, second, w_one, w_two_back, w_one_back):
+    lay_forward(first, w_one)
+    lay_backward(second, w_two_back)
+    lay_backward(first, w_one_back)
 
 
 def weights(first, second):
@@ -220,9 +234,9 @@
     vmem = pl.BlockSpec(memory_space=pltpu.VMEM)
     return pl.pallas_call(
         weights_kernel,
-        out_shape=(turned,) * 4,
+        out_shape=(turned,) * 3,
         in_specs=[vmem] * 2,
-        out_specs=[vmem] * 4,
+        out_specs=[vmem] * 3,
         compiler_params=pltpu.CompilerParams(vmem_limit_bytes=10 * 1024 * 1024),
         cost_estimate=pl.CostEstimate(flops=3 * 10**9, bytes_accessed=6 * first.size, transcendentals=0),
     )(first, second)
@@ -242,15 +256,23 @@
     )(*args)
 
 
-def from_before(field, edge):
-    frames = field.shape[0]
-    sent = jnp.concatenate([field[frames - 2 :], edge[frames - 2 : frames, None]], axis=1)
+def join_kernel(earlier, later, side, last, first):
+    frames, rows = earlier.shape[0], earlier.shape[1]
+    for f in range(2):
+        last[f, pl.ds(0, rows)] = earlier[frames - 2 + f]
+        last[f, rows] = side[frames - 2 + f]
+        first[f, pl.ds(0, rows)] = later[f]
+        first[f, rows] = side[frames + f]
+
+
+def joined(earlier, later, side):
+    _, rows, channels, cols = earlier.shape
+    out = jax.ShapeDtypeStruct((2, rows + 1, channels, cols), BF16)
+    return small_call(join_kernel, (out, out), (earlier, later, side), False)
+
+
+def from_before(sent):
     return lax.ppermute(sent, TIME, [(i, i + 1) for i in range(lax.axis_size(TIME) - 1)])
-
-
-def ahead_of(field, edge):
-    frames = field.shape[0]
-    return jnp.concatenate([field[:2], edge[frames : frames + 2, None]], axis=1)
 
 
 def from_after(sent):
@@ -258,7 +280,7 @@
 
 
 def chip_total(kept, given):
-    return (kept + lax.ppermute(given, "core", SWAP)).astype(BF16)
+    return (kept + lax.ppermute(given, "core", SWAP).astype(F32)).astype(BF16)
 
 
 def clip_total(pieces):
@@ -330,7 +352,7 @@
     conv_flops = 2 * 27 * channels * channels * frames * rows * cols
     return call(
         functools.partial(head_kernel, scale, owners),
-        (field, field, jax.ShapeDtypeStruct((2 * frames, channels, cols), BF16), packed, packed),
+        (field, field, jax.ShapeDtypeStruct((2 * frames, channels, cols), BF16), packed, jax.ShapeDtypeStruct(packed.shape, BF16)),
         [
             pairs,
             pairs,
@@ -353,10 +375,10 @@
     side = jnp.concatenate(
         [lax.dynamic_index_in_dim(a, edge, 1, keepdims=False) for a in (source, upstream)], axis=0
     )
-    w_one, w_two_back, w_two, w_one_back = weights(first_kernel.T, second_kernel.T)
+    w_one, w_two_back, w_one_back = weights(first_kernel.T, second_kernel.T)
     side = lax.ppermute(side, "x_hi", SWAP)
-    x_far = from_before(source, side)
-    c_far = from_after(ahead_of(upstream, side))
+    x_sent, c_sent = joined(source, upstream, side)
+    x_far, c_far = from_before(x_sent), from_after(c_sent)
 
     owners = lax.axis_size(CLIP_AXES)
     positions = frames * rows * cols * lax.axis_size(CLIP_AXES + HALVES)
@@ -366,14 +388,16 @@
     pairs = pltpu.VMEM((frames, rows + 2, channels, 2 * cols), BF16)
     conv_flops = 2 * 27 * channels * channels * frames * rows * cols
     out = jax.ShapeDtypeStruct(source.shape, F32)
+    laid = pltpu.VMEM((3 * channels, 9 * channels), BF16)
     peers = lax.axis_size("z")
     part_shape = (MAIN // peers, cols)
 
     pieces, side = lax.optimization_barrier((chip_total(kept, given), side))
     clip_sum = clip_total(pieces)
     side = lax.ppermute(side, "x_hi", SWAP)
-    a_far = from_before(act, side)
-    clip_sum, g_sent = lax.optimization_barrier((clip_sum, ahead_of(grad, side)))
+    a_sent, g_sent = joined(act, grad, side)
+    a_far = from_before(a_sent)
+    clip_sum, g_sent = lax.optimization_barrier((clip_sum, g_sent))
     parts = exchanged(clip_sum.reshape((peers,) + part_shape))
     g_far = from_after(g_sent)
     part = jax.ShapeDtypeStruct(part_shape, F32)
@@ -381,7 +405,7 @@
     part_sum, a_far = lax.optimization_barrier((part_sum, a_far))
     part_other = lax.ppermute(part_sum, "x_hi", SWAP)
     (block_output,) = call(
-        branch_kernel, (out,), [pairs], conv_flops, (flags, source, act, a_far, side, w_two)
+        branch_kernel, (out,), [pairs, laid], conv_flops, (flags, source, act, a_far, side, second_kernel.T)
     )
     part_other, block_output = lax.optimization_barrier((part_other, block_output))
     spread = jax.ShapeDtypeStruct((peers,) + part_shape, F32)

time: 92.4 us -> 95.5 us (1.034)
  waiting for transfers between devices: 21.5 us -> 29.9 us
  starting transfers between devices: 45.9 us -> 40.2 us
  local copies, waits for them, and re-layouts: 2.92 us -> 3.92 us
    ppermute x2, waiting for transfers between devices: 4.32 us -> 14.3 us  [local(): side = lax.ppermute(side, 'x_hi', SWAP)]
    ppermute x2, starting transfers between devices: 6.34 us -> 3.94 us  [from_after(): lax.ppermute(sent, TIME, [(i + 1, i) for i in range(lax.axis_size(TIME) -...]
    all_to_all x1, waiting for transfers between devices: 2.12 us -> 0.01 us  [clip_total(): arrived = lax.all_to_all(pieces, CLIP_AXES, 0, 0, tiled=True)]
    all_to_all x2, waiting for transfers between devices: 8.41 us -> 10.5 us  [exchanged(): return lax.all_to_all(parts, 'z', 0, 0, tiled=True)]
    ppermute x1, starting transfers between devices: 4.96 us -> 3.59 us  [local(): other = lax.ppermute(whole, 'core', SWAP)]
    all_to_all x2, starting transfers between devices: 11.4 us -> 10.1 us  [exchanged(): return lax.all_to_all(parts, 'z', 0, 0, tiled=True)]
    ppermute x1, starting transfers between devices: 2.02 us -> 0.81 us  [local(): part_other = lax.ppermute(part_sum, 'x_hi', SWAP)]
    ppermute x2, waiting for transfers between devices: 3.01 us -> 1.81 us  [from_after(): lax.ppermute(sent, TIME, [(i + 1, i) for i in range(lax.axis_size(TIME) -...]
  transfers between devices with their start and end apart: 12 -> 12, of which waited for: 8 -> 8; matrix products, arithmetic and copies ran while one was open for 1% -> 0% of each run, Pallas kernels for 10% -> 10%
where the time goes in v4:
time: 95.5 us; the launch traced here: 95 us
  starting transfers between devices  40.2 us (42%)
  waiting for transfers between devices  29.9 us (31%)
  Pallas kernels  19.1 us (20%)
  local copies, waits for them, and re-layouts  3.92 us (4%)
  other arithmetic  1.02 us (1%)
    ppermute x2, waiting for transfers between devices, local(): side = lax.ppermute(side, 'x_hi', SWAP)  14.3 us
    pallas_call x3, Pallas kernels, call(): pl.pallas_call(kernel, out_shape=outs, in_specs=[pl.BlockSpec(memory_spac...  14.2 us
    all_to_all x2, waiting for transfers between devices, exchanged(): return lax.all_to_all(parts, 'z', 0, 0, tiled=True)  10.5 us
    ppermute x2, starting transfers between devices, from_before(): lax.ppermute(sent, TIME, [(i, i + 1) for i in range(lax.axis_size(TIME) -...  10.5 us
    all_to_all x2, starting transfers between devices, exchanged(): return lax.all_to_all(parts, 'z', 0, 0, tiled=True)  10.1 us
    ppermute x2, starting transfers between devices, local(): side = lax.ppermute(side, 'x_hi', SWAP)  6.09 us
    all_to_all x1, starting transfers between devices, clip_total(): arrived = lax.all_to_all(pieces, CLIP_AXES, 0, 0, tiled=True)  5.12 us
    ppermute x2, starting transfers between devices, from_after(): lax.ppermute(sent, TIME, [(i + 1, i) for i in range(lax.axis_size(TIME) -...  3.94 us
  transfers between devices with their start and end apart: 12, of which 8 were waited for; matrix products, arithmetic and copies ran while one was open for 0% of the time, Pallas kernels for 10%

profile of v4, /device:TPU:1, one launch (start us, length us, event | category | flops | bytes accessed | tf_op | source)
XLA Modules:
  0.0 95.0 jit_solution(4616398975651884400)
XLA Ops:
  0.6 0.0 copy-start
  0.6 0.0 copy-start.1
  0.7 1.0 %dynamic-slice_bitcast_fusion = (bf16[4,96,128]{2,1,0:T(8,128)(2,1)S(1)}, bf16[4,96,128]{2,1,0:T(8,128)(2,1)S(1)}) fusion(bf16[1,4,4,96,128]{4,3,2,1,0:T(8,128)(2,1)} %param.5, s32[]{:T(128)S(6)} %select_n.7, bf16[1,4,4,96,128]{4,3,2,1,0:T(8,128)(2,1)} %param.4), kind=kLoop, calls=%fused_computation.2 | loop fusion | bytes 393220 | tf_op jit(solution)/shard_map/jit(dynamic_index_in_dim)/squeeze | solution.py:376
  1.7 0.0 copy-start.2
  1.7 3.7 %collective-permute-start = (bf16[8,96,128]{2,1,0:T(8,128)(2,1)S(1)}, bf16[8,96,128]{2,1,0:T(8,128)(2,1)S(1)}, u32[]{:S(2)}, u32[]{:S(2)}) collective-permute-start(bf16[8,96,128]{2,1,0:T(8,128)(2,1)S(1)} %pad_maximum_fusion), channel_id=1, source_target_pairs={{0,1},{1,0},{2,3},{3,2},{4,5},{5,4},{6,7},{7,6},{8,9},{9,8},{10,11... | collective-permute-start | bytes 589832 | tf_op jit(solution)/shard_map/ppermute | solution.py:379
  5.4 0.1 pad_add_fusion.flags
  5.5 3.5 %collective-permute-done.side = bf16[8,96,128]{2,1,0:T(8,128)(2,1)S(1)} collective-permute-done((bf16[8,96,128]{2,1,0:T(8,128)(2,1)S(1)}, bf16[8,96,128]{2,1,0:T(8,128)(2,1)S(1)}, u32[]{:S(2)}, u32[]{:S(2)}) %collective-permute-start) | collective-permute-done | bytes 196640 | tf_op jit(solution)/shard_map/ppermute | solution.py:379
  9.0 0.0 copy-done
  9.0 0.0 copy-done.1
  9.0 5.9 %collective-permute-start.1 = (bf16[2,5,96,128]{3,2,1,0:T(8,128)(2,1)S(1)}, bf16[2,5,96,128]{3,2,1,0:T(8,128)(2,1)S(1)}, u32[]{:S(2)}, u32[]{:S(2)}) collective-permute-start(bf16[2,5,96,128]{3,2,1,0:T(8,128)(2,1)S(1)} %get-tuple-element.30), channel_id=1, source_target_pairs={{0,2},{2,4},{4,6},{6,8},{8,10},{10,12},{12,14},{14,16},{16,18},{18... | collective-permute-start | bytes 737288 | tf_op jit(solution)/shard_map/ppermute | solution.py:275
  15.0 1.9 %collective-permute-start.2 = (bf16[2,5,96,128]{3,2,1,0:T(8,128)(2,1)S(1)}, bf16[2,5,96,128]{3,2,1,0:T(8,128)(2,1)S(1)}, u32[]{:S(2)}, u32[]{:S(2)}) collective-permute-start(bf16[2,5,96,128]{3,2,1,0:T(8,128)(2,1)S(1)} %get-tuple-element.31), channel_id=1, source_target_pairs={{2,0},{4,2},{6,4},{8,6},{10,8},{12,10},{14,12},{16,14},{18,16},{20... | collective-permute-start | bytes 737288 | tf_op jit(solution)/shard_map/ppermute | solution.py:279
  16.9 0.0 copy-done.2
  16.9 0.0 copy-start.3
  16.9 1.0 %copy-done.3 = bf16[2592,96]{0,1:T(8,128)(2,1)S(1)} copy-done((bf16[2592,96]{0,1:T(8,128)(2,1)S(1)}, bf16[2592,96]{0,1:T(8,128)(2,1)}, u32[]{:S(2)}) %copy-start.3) | copy-done | bytes 497688
  17.9 1.9 %shard_map.76 = (bf16[288,864]{1,0:T(8,128)(2,1)S(1)}, bf16[288,864]{1,0:T(8,128)(2,1)S(1)}, bf16[288,864]{1,0:T(8,128)(2,1)S(1)}) custom-call(bf16[96,2592]{1,0:T(8,128)(2,1)S(1)} %bitcast.25, bf16[96,2592]{1,0:T(8,128)(2,1)S(1)} %bitcast.26), custom_call_target="tpu_custom_call" | custom-call | flops 3000000000 | bytes 1492992 | tf_op jit(solution)/shard_map/pallas_call | solution.py:235
  19.8 0.0 copy-start.5
  19.9 0.8 copy-done.5
  20.7 0.0 collective-permute-done.1.x_far
  20.7 1.8 %collective-permute-done.2.c_far = bf16[2,5,96,128]{3,2,1,0:T(8,128)(2,1)S(1)} collective-permute-done((bf16[2,5,96,128]{3,2,1,0:T(8,128)(2,1)S(1)}, bf16[2,5,96,128]{3,2,1,0:T(8,128)(2,1)S(1)}, u32[]{:S(2)}, u32[]{:S(2)}) %collective-permute-start.2) | collective-permute-done | bytes 245792 | tf_op jit(solution)/shard_map/ppermute | solution.py:279
  22.5 8.1 %shard_map.77 = (bf16[4,4,96,128]{3,2,1,0:T(8,128)(2,1)S(1)}, bf16[4,4,96,128]{3,2,1,0:T(8,128)(2,1)S(1)}, bf16[8,96,128]{2,1,0:T(8,128)(2,1)S(1)}, f32[8,256,128]{2,1,0:T(8,128)S(1)}, bf16[8,256,128]{2,1,0:T(8,128)(2,1)S(1)}) custom-call(s32[2]{0:T(128)S(1)} %pad_add_fusion.flags, bf16[4,4,96,128]{3,2,1,0:T(8,128)(2,1)S(1)} %bitcast.17, ...), custom_call_target="tpu_custom_call" | custom-call | flops 4076863488 | bytes 5025792 | tf_op jit(solution)/shard_map/pallas_call | solution.py:248
  30.5 0.1 collective-permute-start.3
  30.6 1.9 %collective-permute-done.3 = bf16[8,256,128]{2,1,0:T(8,128)(2,1)S(1)} collective-permute-done((bf16[8,256,128]{2,1,0:T(8,128)(2,1)S(1)}, bf16[8,256,128]{2,1,0:T(8,128)(2,1)S(1)}, u32[]{:S(2)}, u32[]{:S(2)}) %collective-permute-start.3) | collective-permute-done | bytes 524320 | tf_op jit(solution)/shard_map/ppermute | solution.py:283
  32.5 0.9 add_convert_fusion
  33.5 5.1 %all-to-all-start = ((bf16[8,256,128]{2,1,0:T(8,128)(2,1)}), bf16[8,256,128]{2,1,0:T(8,128)(2,1)S(1)}, u32[]{:S(2)}, u32[]{:S(2)}) async-start(bf16[8,256,128]{2,1,0:T(8,128)(2,1)} %add_convert_fusion), calls=%async_computation | async-start | bytes 1048576 | tf_op jit(solution)/shard_map/all_to_all | solution.py:287
  38.6 2.4 %collective-permute-start.4 = (bf16[8,96,128]{2,1,0:T(8,128)(2,1)S(1)}, bf16[8,96,128]{2,1,0:T(8,128)(2,1)S(1)}, u32[]{:S(2)}, u32[]{:S(2)}) collective-permute-start(bf16[8,96,128]{2,1,0:T(8,128)(2,1)S(1)} %get-tuple-element.40), channel_id=1, source_target_pairs={{0,1},{1,0},{2,3},{3,2},{4,5},{5,4},{6,7},{7,6},{8,9},{9,8},{10,11... | collective-permute-start | bytes 589832 | tf_op jit(solution)/shard_map/ppermute | solution.py:397
  41.0 10.8 %collective-permute-done.4.side = bf16[8,96,128]{2,1,0:T(8,128)(2,1)S(1)} collective-permute-done((bf16[8,96,128]{2,1,0:T(8,128)(2,1)S(1)}, bf16[8,96,128]{2,1,0:T(8,128)(2,1)S(1)}, u32[]{:S(2)}, u32[]{:S(2)}) %collective-permute-start.4) | collective-permute-done | bytes 196640 | tf_op jit(solution)/shard_map/ppermute | solution.py:397
  51.8 0.0 copy-start.4
  51.8 4.5 %collective-permute-start.5 = (bf16[2,5,96,128]{3,2,1,0:T(8,128)(2,1)S(1)}, bf16[2,5,96,128]{3,2,1,0:T(8,128)(2,1)S(1)}, u32[]{:S(2)}, u32[]{:S(2)}) collective-permute-start(bf16[2,5,96,128]{3,2,1,0:T(8,128)(2,1)S(1)} %get-tuple-element.43), channel_id=1, source_target_pairs={{0,2},{2,4},{4,6},{6,8},{8,10},{10,12},{12,14},{14,16},{16,18},{18... | collective-permute-start | bytes 737288 | tf_op jit(solution)/shard_map/ppermute | solution.py:275
  56.4 0.0 all-to-all-done.arrived
  56.4 0.7 shard_map.78
  57.1 6.7 %all-to-all-start.1 = ((f32[8,32,128]{2,1,0:T(8,128)}), f32[8,32,128]{2,1,0:T(8,128)S(1)}, u32[]{:S(2)}, u32[]{:S(2)}) async-start(f32[8,32,128]{2,1,0:T(8,128)} %bitcast.8), calls=%async_computation.1 | async-start | bytes 262144 | tf_op jit(solution)/shard_map/all_to_all | solution.py:293
  63.8 2.0 %collective-permute-start.7 = (bf16[2,5,96,128]{3,2,1,0:T(8,128)(2,1)S(1)}, bf16[2,5,96,128]{3,2,1,0:T(8,128)(2,1)S(1)}, u32[]{:S(2)}, u32[]{:S(2)}) collective-permute-start(bf16[2,5,96,128]{3,2,1,0:T(8,128)(2,1)S(1)} %get-tuple-element.48), channel_id=1, source_target_pairs={{2,0},{4,2},{6,4},{8,6},{10,8},{12,10},{14,12},{16,14},{18,16},{20... | collective-permute-start | bytes 737288 | tf_op jit(solution)/shard_map/ppermute | solution.py:279
  65.8 6.6 %all-to-all-done.1.arrived = f32[8,32,128]{2,1,0:T(8,128)S(1)} async-done(((f32[8,32,128]{2,1,0:T(8,128)}), f32[8,32,128]{2,1,0:T(8,128)S(1)}, u32[]{:S(2)}, u32[]{:S(2)}) %all-to-all-start.1) | async-done | bytes 131104 | tf_op jit(solution)/shard_map/all_to_all | solution.py:293
  72.4 0.0 collective-permute-done.5.a_far
  72.4 0.8 collective-permute-start.6
  73.3 0.0 copy-done.4
  73.3 3.0 %shard_map.81 = f32[4,4,96,128]{3,2,1,0:T(8,128)} custom-call(s32[2]{0:T(128)S(1)} %pad_add_fusion.flags, bf16[4,4,96,128]{3,2,1,0:T(8,128)(2,1)S(1)} %bitcast.18, bf16[4,4,96,128]{3,2,1,0:T(8,128)(2,1)S(1)} %get-tuple-element.38.earlier.act, bf16[2,5,96,128]{3,2,1,0:T(8,128)(2,1)S(1)} %collective-permute-done.5.a_far, ...), custom_call_target="tpu_custom_call" | custom-call | flops 1019215872 | bytes 2512896 | tf_op jit(solution)/shard_map/pallas_call | solution.py:248
  76.3 0.5 collective-permute-done.6.other
  76.8 0.7 shard_map.82
  77.5 0.0 collective-permute-done.7.g_far
  77.5 3.4 %all-to-all-start.2 = ((f32[8,32,128]{2,1,0:T(8,128)}), f32[8,32,128]{2,1,0:T(8,128)S(1)}, u32[]{:S(2)}, u32[]{:S(2)}) async-start(f32[8,32,128]{2,1,0:T(8,128)} %shard_map.82), calls=%async_computation.2 | async-start | bytes 262144 | tf_op jit(solution)/shard_map/all_to_all | solution.py:293
  80.9 0.0 copy-start.6
  80.9 1.0 %copy-done.6 = bf16[288,864]{1,0:T(8,128)(2,1)S(1)} copy-done((bf16[288,864]{1,0:T(8,128)(2,1)S(1)}, bf16[288,864]{1,0:T(8,128)(2,1)}, u32[]{:S(2)}) %copy-start.6) | copy-done | bytes 497688
  81.9 3.0 %shard_map.83 = f32[4,4,96,128]{3,2,1,0:T(8,128)} custom-call(s32[2]{0:T(128)S(1)} %pad_add_fusion.flags, bf16[4,4,96,128]{3,2,1,0:T(8,128)(2,1)S(1)} %bitcast.19, bf16[4,4,96,128]{3,2,1,0:T(8,128)(2,1)S(1)} %bitcast.22, bf16[4,4,96,128]{3,2,1,0:T(8,128)(2,1)S(1)} %get-tuple-element.39.later.grad, bf16[2,5,96,128]{3,2,1,0:T(8,128)(2,1)S(1)} %collective-permute-done.7.g_far, ...), custom_call_target="tpu_custom_call" | custom-call | flops 1019215872 | bytes 2906112 | tf_op jit(solution)/shard_map/pallas_call | solution.py:248
  84.9 3.8 %all-to-all-done.2 = f32[8,32,128]{2,1,0:T(8,128)S(1)} async-done(((f32[8,32,128]{2,1,0:T(8,128)}), f32[8,32,128]{2,1,0:T(8,128)S(1)}, u32[]{:S(2)}, u32[]{:S(2)}) %all-to-all-start.2) | async-done | bytes 131104 | tf_op jit(solution)/shard_map/all_to_all | solution.py:293
  88.8 3.6 %collective-permute-start.8 = (f32[256,128]{1,0:T(8,128)S(1)}, f32[256,128]{1,0:T(8,128)S(1)}, u32[]{:S(2)}, u32[]{:S(2)}) collective-permute-start(f32[256,128]{1,0:T(8,128)S(1)} %bitcast.23), channel_id=1, source_target_pairs={{0,2},{2,0},{1,3},{3,1},{4,6},{6,4},{5,7},{7,5},{8,10},{10,8},{9,1... | collective-permute-start | bytes 393224 | tf_op jit(solution)/shard_map/ppermute | solution.py:419
  92.4 1.0 %collective-permute-done.8.other = f32[256,128]{1,0:T(8,128)S(1)} collective-permute-done((f32[256,128]{1,0:T(8,128)S(1)}, f32[256,128]{1,0:T(8,128)S(1)}, u32[]{:S(2)}, u32[]{:S(2)}) %collective-permute-start.8) | collective-permute-done | bytes 131104 | tf_op jit(solution)/shard_map/ppermute | solution.py:419
  93.4 1.6 %shard_map.84 = (f32[96,324]{1,0:T(8,128)}, f32[96,324]{1,0:T(8,128)}) custom-call(s32[2]{0:T(128)S(1)} %pad_add_fusion.flags, f32[256,128]{1,0:T(8,128)S(1)} %bitcast.24, f32[256,128]{1,0:T(8,128)S(1)} %collective-permute-done.8.other), custom_call_target="tpu_custom_call" | custom-call | bytes 510984 | tf_op jit(solution)/shard_map/pallas_call | solution.py:336
  (4 shorter events, 0.1 us)
Async XLA Ops:
  0.6 8.3 %copy-start = (bf16[1,4,4,96,128]{4,3,2,1,0:T(8,128)(2,1)S(1)}, bf16[1,4,4,96,128]{4,3,2,1,0:T(8,128)(2,1)}, u32[]{:S(2)}) copy-start(bf16[1,4,4,96,128]{4,3,2,1,0:T(8,128)(2,1)} %param.4) | copy-start | bytes 1179652
  0.6 8.3 %copy-start.1 = (bf16[1,4,4,96,128]{4,3,2,1,0:T(8,128)(2,1)S(1)}, bf16[1,4,4,96,128]{4,3,2,1,0:T(8,128)(2,1)}, u32[]{:S(2)}) copy-start(bf16[1,4,4,96,128]{4,3,2,1,0:T(8,128)(2,1)} %param.5) | copy-start | bytes 1179652
  1.7 15.2 %copy-start.2 = (bf16[2592,96]{0,1:T(8,128)(2,1)S(1)}, bf16[2592,96]{0,1:T(8,128)(2,1)}, u32[]{:S(2)}) copy-start(bf16[2592,96]{0,1:T(8,128)(2,1)} %param.6) | copy-start | bytes 1492996
  1.7 7.2 %collective-permute-start = (bf16[8,96,128]{2,1,0:T(8,128)(2,1)S(1)}, bf16[8,96,128]{2,1,0:T(8,128)(2,1)S(1)}, u32[]{:S(2)}, u32[]{:S(2)}) collective-permute-start(bf16[8,96,128]{2,1,0:T(8,128)(2,1)S(1)} %pad_maximum_fusion), channel_id=1, source_target_pairs={{0,1},{1,0},{2,3},{3,2},{4,5},{5,4},{6,7},{7,6},{8,9},{9,8},{10,11... | collective-permute-start | bytes 589832 | tf_op jit(solution)/shard_map/ppermute | solution.py:379
  9.0 11.7 %collective-permute-start.1 = (bf16[2,5,96,128]{3,2,1,0:T(8,128)(2,1)S(1)}, bf16[2,5,96,128]{3,2,1,0:T(8,128)(2,1)S(1)}, u32[]{:S(2)}, u32[]{:S(2)}) collective-permute-start(bf16[2,5,96,128]{3,2,1,0:T(8,128)(2,1)S(1)} %get-tuple-element.30), channel_id=1, source_target_pairs={{0,2},{2,4},{4,6},{6,8},{8,10},{10,12},{12,14},{14,16},{16,18},{18... | collective-permute-start | bytes 737288 | tf_op jit(solution)/shard_map/ppermute | solution.py:275
  15.0 7.5 %collective-permute-start.2 = (bf16[2,5,96,128]{3,2,1,0:T(8,128)(2,1)S(1)}, bf16[2,5,96,128]{3,2,1,0:T(8,128)(2,1)S(1)}, u32[]{:S(2)}, u32[]{:S(2)}) collective-permute-start(bf16[2,5,96,128]{3,2,1,0:T(8,128)(2,1)S(1)} %get-tuple-element.31), channel_id=1, source_target_pairs={{2,0},{4,2},{6,4},{8,6},{10,8},{12,10},{14,12},{16,14},{18,16},{20... | collective-permute-start | bytes 737288 | tf_op jit(solution)/shard_map/ppermute | solution.py:279
  16.9 1.0 %copy-start.3 = (bf16[2592,96]{0,1:T(8,128)(2,1)S(1)}, bf16[2592,96]{0,1:T(8,128)(2,1)}, u32[]{:S(2)}) copy-start(bf16[2592,96]{0,1:T(8,128)(2,1)} %param.7) | copy-start | bytes 1492996
  19.8 0.8 copy-start.5
  30.5 2.0 %collective-permute-start.3 = (bf16[8,256,128]{2,1,0:T(8,128)(2,1)S(1)}, bf16[8,256,128]{2,1,0:T(8,128)(2,1)S(1)}, u32[]{:S(2)}, u32[]{:S(2)}) collective-permute-start(bf16[8,256,128]{2,1,0:T(8,128)(2,1)S(1)} %get-tuple-element.35), channel_id=1, source_target_pairs={{0,2},{2,0},{1,3},{3,1},{4,6},{6,4},{5,7},{7,5},{8,10},{10,8},{9,1... | collective-permute-start | bytes 1572872 | tf_op jit(solution)/shard_map/ppermute | solution.py:283
  33.5 22.9 %all-to-all-start = ((bf16[8,256,128]{2,1,0:T(8,128)(2,1)}), bf16[8,256,128]{2,1,0:T(8,128)(2,1)S(1)}, u32[]{:S(2)}, u32[]{:S(2)}) async-start(bf16[8,256,128]{2,1,0:T(8,128)(2,1)} %add_convert_fusion), calls=%async_computation | async-start | bytes 1048576 | tf_op jit(solution)/shard_map/all_to_all | solution.py:287
  38.6 13.2 %collective-permute-start.4 = (bf16[8,96,128]{2,1,0:T(8,128)(2,1)S(1)}, bf16[8,96,128]{2,1,0:T(8,128)(2,1)S(1)}, u32[]{:S(2)}, u32[]{:S(2)}) collective-permute-start(bf16[8,96,128]{2,1,0:T(8,128)(2,1)S(1)} %get-tuple-element.40), channel_id=1, source_target_pairs={{0,1},{1,0},{2,3},{3,2},{4,5},{5,4},{6,7},{7,6},{8,9},{9,8},{10,11... | collective-permute-start | bytes 589832 | tf_op jit(solution)/shard_map/ppermute | solution.py:397
  51.8 21.4 %copy-start.4 = (bf16[2592,96]{0,1:T(8,128)(2,1)S(1)}, bf16[2592,96]{0,1:T(8,128)(2,1)}, u32[]{:S(2)}) copy-start(bf16[2592,96]{0,1:T(8,128)(2,1)} %param.7) | copy-start | bytes 1492996
  51.8 20.6 %collective-permute-start.5 = (bf16[2,5,96,128]{3,2,1,0:T(8,128)(2,1)S(1)}, bf16[2,5,96,128]{3,2,1,0:T(8,128)(2,1)S(1)}, u32[]{:S(2)}, u32[]{:S(2)}) collective-permute-start(bf16[2,5,96,128]{3,2,1,0:T(8,128)(2,1)S(1)} %get-tuple-element.43), channel_id=1, source_target_pairs={{0,2},{2,4},{4,6},{6,8},{8,10},{10,12},{12,14},{14,16},{16,18},{18... | collective-permute-start | bytes 737288 | tf_op jit(solution)/shard_map/ppermute | solution.py:275
  57.1 15.3 %all-to-all-start.1 = ((f32[8,32,128]{2,1,0:T(8,128)}), f32[8,32,128]{2,1,0:T(8,128)S(1)}, u32[]{:S(2)}, u32[]{:S(2)}) async-start(f32[8,32,128]{2,1,0:T(8,128)} %bitcast.8), calls=%async_computation.1 | async-start | bytes 262144 | tf_op jit(solution)/shard_map/all_to_all | solution.py:293
  63.8 13.7 %collective-permute-start.7 = (bf16[2,5,96,128]{3,2,1,0:T(8,128)(2,1)S(1)}, bf16[2,5,96,128]{3,2,1,0:T(8,128)(2,1)S(1)}, u32[]{:S(2)}, u32[]{:S(2)}) collective-permute-start(bf16[2,5,96,128]{3,2,1,0:T(8,128)(2,1)S(1)} %get-tuple-element.48), channel_id=1, source_target_pairs={{2,0},{4,2},{6,4},{8,6},{10,8},{12,10},{14,12},{16,14},{18,16},{20... | collective-permute-start | bytes 737288 | tf_op jit(solution)/shard_map/ppermute | solution.py:279
  72.4 4.4 %collective-permute-start.6 = (f32[32,128]{1,0:T(8,128)S(1)}, f32[32,128]{1,0:T(8,128)S(1)}, u32[]{:S(2)}, u32[]{:S(2)}) collective-permute-start(f32[32,128]{1,0:T(8,128)S(1)} %shard_map.80.mine), channel_id=1, source_target_pairs={{0,1},{1,0},{2,3},{3,2},{4,5},{5,4},{6,7},{7,6},{8,9},{9,8},{10,11... | collective-permute-start | bytes 49160 | tf_op jit(solution)/shard_map/ppermute | solution.py:406
  77.5 11.3 %all-to-all-start.2 = ((f32[8,32,128]{2,1,0:T(8,128)}), f32[8,32,128]{2,1,0:T(8,128)S(1)}, u32[]{:S(2)}, u32[]{:S(2)}) async-start(f32[8,32,128]{2,1,0:T(8,128)} %shard_map.82), calls=%async_computation.2 | async-start | bytes 262144 | tf_op jit(solution)/shard_map/all_to_all | solution.py:293
  80.9 1.0 %copy-start.6 = (bf16[288,864]{1,0:T(8,128)(2,1)S(1)}, bf16[288,864]{1,0:T(8,128)(2,1)}, u32[]{:S(2)}) copy-start(bf16[288,864]{1,0:T(8,128)(2,1)} %copy-done.5) | copy-start | bytes 1492996
  88.8 4.6 %collective-permute-start.8 = (f32[256,128]{1,0:T(8,128)S(1)}, f32[256,128]{1,0:T(8,128)S(1)}, u32[]{:S(2)}, u32[]{:S(2)}) collective-permute-start(f32[256,128]{1,0:T(8,128)S(1)} %bitcast.23), channel_id=1, source_target_pairs={{0,2},{2,0},{1,3},{3,1},{4,6},{6,4},{5,7},{7,5},{8,10},{10,8},{9,1... | collective-permute-start | bytes 393224 | tf_op jit(solution)/shard_map/ppermute | solution.py:419

commit v5 on v4

--- a/solution.py
+++ b/solution.py
@@ -256,23 +256,15 @@
     )(*args)
 
 
-def join_kernel(earlier, later, side, last, first):
-    frames, rows = earlier.shape[0], earlier.shape[1]
-    for f in range(2):
-        last[f, pl.ds(0, rows)] = earlier[frames - 2 + f]
-        last[f, rows] = side[frames - 2 + f]
-        first[f, pl.ds(0, rows)] = later[f]
-        first[f, rows] = side[frames + f]
-
-
-def joined(earlier, later, side):
-    _, rows, channels, cols = earlier.shape
-    out = jax.ShapeDtypeStruct((2, rows + 1, channels, cols), BF16)
-    return small_call(join_kernel, (out, out), (earlier, later, side), False)
-
-
-def from_before(sent):
+def from_before(field, edge):
+    frames = field.shape[0]
+    sent = jnp.concatenate([field[frames - 2 :], edge[frames - 2 : frames, None]], axis=1)
     return lax.ppermute(sent, TIME, [(i, i + 1) for i in range(lax.axis_size(TIME) - 1)])
+
+
+def ahead_of(field, edge):
+    frames = field.shape[0]
+    return jnp.concatenate([field[:2], edge[frames : frames + 2, None]], axis=1)
 
 
 def from_after(sent):
@@ -377,8 +369,8 @@
     )
     w_one, w_two_back, w_one_back = weights(first_kernel.T, second_kernel.T)
     side = lax.ppermute(side, "x_hi", SWAP)
-    x_sent, c_sent = joined(source, upstream, side)
-    x_far, c_far = from_before(x_sent), from_after(c_sent)
+    x_far = from_before(source, side)
+    c_far = from_after(ahead_of(upstream, side))
 
     owners = lax.axis_size(CLIP_AXES)
     positions = frames * rows * cols * lax.axis_size(CLIP_AXES + HALVES)
@@ -395,9 +387,8 @@
     pieces, side = lax.optimization_barrier((chip_total(kept, given), side))
     clip_sum = clip_total(pieces)
     side = lax.ppermute(side, "x_hi", SWAP)
-    a_sent, g_sent = joined(act, grad, side)
-    a_far = from_before(a_sent)
-    clip_sum, g_sent = lax.optimization_barrier((clip_sum, g_sent))
+    a_far = from_before(act, side)
+    clip_sum, g_sent = lax.optimization_barrier((clip_sum, ahead_of(grad, side)))
     parts = exchanged(clip_sum.reshape((peers,) + part_shape))
     g_far = from_after(g_sent)
     part = jax.ShapeDtypeStruct(part_shape, F32)

time: 95.5 us -> 90.8 us (0.951)
  waiting for transfers between devices: 29.9 us -> 19.6 us
  starting transfers between devices: 40.2 us -> 46 us
  local copies, waits for them, and re-layouts: 3.92 us -> 2.93 us
    ppermute x2, waiting for transfers between devices: 14.3 us -> 4.32 us  [local(): side = lax.ppermute(side, 'x_hi', SWAP)]
    all_to_all x2, waiting for transfers between devices: 10.5 us -> 7.41 us  [exchanged(): return lax.all_to_all(parts, 'z', 0, 0, tiled=True)]
    ppermute x2, starting transfers between devices: 3.94 us -> 6.34 us  [from_after(): lax.ppermute(sent, TIME, [(i + 1, i) for i in range(lax.axis_size(TIME) -...]
    all_to_all x1, waiting for transfers between devices: 0.01 us -> 2.12 us  [clip_total(): arrived = lax.all_to_all(pieces, CLIP_AXES, 0, 0, tiled=True)]
    ppermute x1, starting transfers between devices: 3.59 us -> 5.12 us  [local(): other = lax.ppermute(whole, 'core', SWAP)]
    all_to_all x2, starting transfers between devices: 10.1 us -> 11.4 us  [exchanged(): return lax.all_to_all(parts, 'z', 0, 0, tiled=True)]
    ppermute x1, starting transfers between devices: 0.81 us -> 2.02 us  [local(): part_other = lax.ppermute(part_sum, 'x_hi', SWAP)]
    unnamed x14 -> x12, local copies, waits for them, and re-layouts: 2.89 us -> 1.84 us
  transfers between devices with their start and end apart: 12 -> 12, of which waited for: 8 -> 8; matrix products, arithmetic and copies ran while one was open for 0% -> 1% of each run, Pallas kernels for 10% -> 10%
where the time goes in v5:
time: 90.8 us; the launch traced here: 90.3 us
  starting transfers between devices  46 us (51%)
  waiting for transfers between devices  19.6 us (22%)
  Pallas kernels  19.1 us (21%)
  local copies, waits for them, and re-layouts  2.93 us (3%)
  other arithmetic  1.79 us (2%)
    pallas_call x3, Pallas kernels, call(): pl.pallas_call(kernel, out_shape=outs, in_specs=[pl.BlockSpec(memory_spac...  14.2 us
    all_to_all x2, starting transfers between devices, exchanged(): return lax.all_to_all(parts, 'z', 0, 0, tiled=True)  11.4 us
    ppermute x2, starting transfers between devices, from_before(): lax.ppermute(sent, TIME, [(i, i + 1) for i in range(lax.axis_size(TIME) -...  10.4 us
    all_to_all x2, waiting for transfers between devices, exchanged(): return lax.all_to_all(parts, 'z', 0, 0, tiled=True)  7.41 us
    ppermute x2, starting transfers between devices, local(): side = lax.ppermute(side, 'x_hi', SWAP)  6.38 us
    ppermute x2, starting transfers between devices, from_after(): lax.ppermute(sent, TIME, [(i + 1, i) for i in range(lax.axis_size(TIME) -...  6.34 us
    ppermute x1, starting transfers between devices, local(): other = lax.ppermute(whole, 'core', SWAP)  5.12 us
    ppermute x2, waiting for transfers between devices, local(): side = lax.ppermute(side, 'x_hi', SWAP)  4.32 us
  transfers between devices with their start and end apart: 12, of which 8 were waited for; matrix products, arithmetic and copies ran while one was open for 1% of the time, Pallas kernels for 10%

profile of v5, /device:TPU:1, one launch (start us, length us, event | category | flops | bytes accessed | tf_op | source)
XLA Modules:
  0.0 90.3 jit_solution(15876762895981248987)
XLA Ops:
  0.6 0.0 copy-start
  0.6 1.0 %dynamic-slice_bitcast_fusion = (bf16[4,96,128]{2,1,0:T(8,128)(2,1)S(1)}, bf16[4,96,128]{2,1,0:T(8,128)(2,1)S(1)}) fusion(bf16[1,4,4,96,128]{4,3,2,1,0:T(8,128)(2,1)} %param.5, s32[]{:T(128)S(6)} %select_n.7, bf16[1,4,4,96,128]{4,3,2,1,0:T(8,128)(2,1)} %param.4), kind=kLoop, calls=%fused_computation.8 | loop fusion | bytes 393220 | tf_op jit(solution)/shard_map/jit(dynamic_index_in_dim)/squeeze | solution.py:368
  1.7 0.0 copy-start.1
  1.7 3.7 %collective-permute-start = (bf16[8,96,128]{2,1,0:T(8,128)(2,1)S(1)}, bf16[8,96,128]{2,1,0:T(8,128)(2,1)S(1)}, u32[]{:S(2)}, u32[]{:S(2)}) collective-permute-start(bf16[8,96,128]{2,1,0:T(8,128)(2,1)S(1)} %pad_maximum_fusion.4), channel_id=1, source_target_pairs={{0,1},{1,0},{2,3},{3,2},{4,5},{5,4},{6,7},{7,6},{8,9},{9,8},{10,11... | collective-permute-start | bytes 589832 | tf_op jit(solution)/shard_map/ppermute | solution.py:371
  5.4 0.0 copy-done
  5.4 0.1 pad_add_fusion.flags
  5.5 0.0 copy-done.1
  5.5 3.4 %collective-permute-done.side = bf16[8,96,128]{2,1,0:T(8,128)(2,1)S(1)} collective-permute-done((bf16[8,96,128]{2,1,0:T(8,128)(2,1)S(1)}, bf16[8,96,128]{2,1,0:T(8,128)(2,1)S(1)}, u32[]{:S(2)}, u32[]{:S(2)}) %collective-permute-start) | collective-permute-done | bytes 196640 | tf_op jit(solution)/shard_map/ppermute | solution.py:371
  8.9 0.0 copy-start.3
  8.9 0.0 copy-start.2
  9.0 6.1 %collective-permute-start.1 = (bf16[2,5,96,128]{3,2,1,0:T(8,128)(2,1)S(1)}, bf16[2,5,96,128]{3,2,1,0:T(8,128)(2,1)S(1)}, u32[]{:S(2)}, u32[]{:S(2)}) collective-permute-start(bf16[2,5,96,128]{3,2,1,0:T(8,128)(2,1)S(1)} %pad_maximum_fusion), channel_id=1, source_target_pairs={{0,2},{2,4},{4,6},{6,8},{8,10},{10,12},{12,14},{14,16},{16,18},{18... | collective-permute-start | bytes 737288 | tf_op jit(solution)/shard_map/ppermute | solution.py:262
  15.1 1.9 %collective-permute-start.2 = (bf16[2,5,96,128]{3,2,1,0:T(8,128)(2,1)S(1)}, bf16[2,5,96,128]{3,2,1,0:T(8,128)(2,1)S(1)}, u32[]{:S(2)}, u32[]{:S(2)}) collective-permute-start(bf16[2,5,96,128]{3,2,1,0:T(8,128)(2,1)S(1)} %pad_maximum_fusion.1), channel_id=1, source_target_pairs={{2,0},{4,2},{6,4},{8,6},{10,8},{12,10},{14,12},{16,14},{18,16},{20... | collective-permute-start | bytes 737288 | tf_op jit(solution)/shard_map/ppermute | solution.py:271
  17.0 0.0 copy-done.3
  17.0 0.0 copy-done.2
  17.1 1.9 %shard_map.75 = (bf16[288,864]{1,0:T(8,128)(2,1)S(1)}, bf16[288,864]{1,0:T(8,128)(2,1)S(1)}, bf16[288,864]{1,0:T(8,128)(2,1)S(1)}) custom-call(bf16[96,2592]{1,0:T(8,128)(2,1)S(1)} %bitcast.43, bf16[96,2592]{1,0:T(8,128)(2,1)S(1)} %bitcast.44), custom_call_target="tpu_custom_call" | custom-call | flops 3000000000 | bytes 1492992 | tf_op jit(solution)/shard_map/pallas_call | solution.py:235
  19.0 0.0 copy-start.4
  19.0 0.8 copy-done.4
  19.8 0.0 collective-permute-done.1.x_far
  19.8 2.8 %collective-permute-done.2.c_far = bf16[2,5,96,128]{3,2,1,0:T(8,128)(2,1)S(1)} collective-permute-done((bf16[2,5,96,128]{3,2,1,0:T(8,128)(2,1)S(1)}, bf16[2,5,96,128]{3,2,1,0:T(8,128)(2,1)S(1)}, u32[]{:S(2)}, u32[]{:S(2)}) %collective-permute-start.2) | collective-permute-done | bytes 245792 | tf_op jit(solution)/shard_map/ppermute | solution.py:271
  22.6 8.1 %shard_map.76 = (bf16[4,4,96,128]{3,2,1,0:T(8,128)(2,1)S(1)}, bf16[4,4,96,128]{3,2,1,0:T(8,128)(2,1)S(1)}, bf16[8,96,128]{2,1,0:T(8,128)(2,1)S(1)}, f32[8,256,128]{2,1,0:T(8,128)S(1)}, bf16[8,256,128]{2,1,0:T(8,128)(2,1)S(1)}) custom-call(s32[2]{0:T(128)S(1)} %pad_add_fusion.flags, bf16[4,4,96,128]{3,2,1,0:T(8,128)(2,1)S(1)} %bitcast.38, ...), custom_call_target="tpu_custom_call" | custom-call | flops 4076863488 | bytes 5025792 | tf_op jit(solution)/shard_map/pallas_call | solution.py:248
  30.7 0.1 collective-permute-start.3
  30.8 1.9 %collective-permute-done.3 = bf16[8,256,128]{2,1,0:T(8,128)(2,1)S(1)} collective-permute-done((bf16[8,256,128]{2,1,0:T(8,128)(2,1)S(1)}, bf16[8,256,128]{2,1,0:T(8,128)(2,1)S(1)}, u32[]{:S(2)}, u32[]{:S(2)}) %collective-permute-start.3) | collective-permute-done | bytes 524320 | tf_op jit(solution)/shard_map/ppermute | solution.py:275
  32.7 0.9 add_convert_fusion
  33.6 2.7 %collective-permute-start.4 = (bf16[8,96,128]{2,1,0:T(8,128)(2,1)S(1)}, bf16[8,96,128]{2,1,0:T(8,128)(2,1)S(1)}, u32[]{:S(2)}, u32[]{:S(2)}) collective-permute-start(bf16[8,96,128]{2,1,0:T(8,128)(2,1)S(1)} %get-tuple-element.33), channel_id=1, source_target_pairs={{0,1},{1,0},{2,3},{3,2},{4,5},{5,4},{6,7},{7,6},{8,9},{9,8},{10,11... | collective-permute-start | bytes 589832 | tf_op jit(solution)/shard_map/ppermute | solution.py:389
  36.4 4.2 %all-to-all-start = ((bf16[8,256,128]{2,1,0:T(8,128)(2,1)}), bf16[8,256,128]{2,1,0:T(8,128)(2,1)S(1)}, u32[]{:S(2)}, u32[]{:S(2)}) async-start(bf16[8,256,128]{2,1,0:T(8,128)(2,1)} %add_convert_fusion), calls=%async_computation | async-start | bytes 1048576 | tf_op jit(solution)/shard_map/all_to_all | solution.py:279
  40.6 0.9 collective-permute-done.4.side
  41.5 0.7 pad_maximum_fusion.3
  42.2 4.4 %collective-permute-start.5 = (bf16[2,5,96,128]{3,2,1,0:T(8,128)(2,1)}, bf16[2,5,96,128]{3,2,1,0:T(8,128)(2,1)S(1)}, u32[]{:S(2)}, u32[]{:S(2)}) collective-permute-start(bf16[2,5,96,128]{3,2,1,0:T(8,128)(2,1)} %pad_maximum_fusion.3), channel_id=1, source_target_pairs={{0,2},{2,4},{4,6},{6,8},{8,10},{10,12},{12,14},{14,16},{16,18},{18... | collective-permute-start | bytes 737288 | tf_op jit(solution)/shard_map/ppermute | solution.py:262
  46.6 2.1 %all-to-all-done.arrived = bf16[8,256,128]{2,1,0:T(8,128)(2,1)S(1)} async-done(((bf16[8,256,128]{2,1,0:T(8,128)(2,1)}), bf16[8,256,128]{2,1,0:T(8,128)(2,1)S(1)}, u32[]{:S(2)}, u32[]{:S(2)}) %all-to-all-start) | async-done | bytes 524320 | tf_op jit(solution)/shard_map/all_to_all | solution.py:279
  48.7 0.7 shard_map.77
  49.4 8.0 %all-to-all-start.1 = ((f32[8,32,128]{2,1,0:T(8,128)}), f32[8,32,128]{2,1,0:T(8,128)S(1)}, u32[]{:S(2)}, u32[]{:S(2)}) async-start(f32[8,32,128]{2,1,0:T(8,128)} %bitcast.16), calls=%async_computation.1 | async-start | bytes 262144 | tf_op jit(solution)/shard_map/all_to_all | solution.py:285
  57.5 4.4 %collective-permute-start.7 = (bf16[2,5,96,128]{3,2,1,0:T(8,128)(2,1)S(1)}, bf16[2,5,96,128]{3,2,1,0:T(8,128)(2,1)S(1)}, u32[]{:S(2)}, u32[]{:S(2)}) collective-permute-start(bf16[2,5,96,128]{3,2,1,0:T(8,128)(2,1)S(1)} %pad_maximum_fusion.2), channel_id=1, source_target_pairs={{2,0},{4,2},{6,4},{8,6},{10,8},{12,10},{14,12},{16,14},{18,16},{20... | collective-permute-start | bytes 737288 | tf_op jit(solution)/shard_map/ppermute | solution.py:271
  61.9 3.6 %all-to-all-done.1.arrived = f32[8,32,128]{2,1,0:T(8,128)S(1)} async-done(((f32[8,32,128]{2,1,0:T(8,128)}), f32[8,32,128]{2,1,0:T(8,128)S(1)}, u32[]{:S(2)}, u32[]{:S(2)}) %all-to-all-start.1) | async-done | bytes 131104 | tf_op jit(solution)/shard_map/all_to_all | solution.py:285
  65.5 0.0 collective-permute-done.5.a_far
  65.5 2.0 %collective-permute-start.6 = (f32[32,128]{1,0:T(8,128)S(1)}, f32[32,128]{1,0:T(8,128)S(1)}, u32[]{:S(2)}, u32[]{:S(2)}) collective-permute-start(f32[32,128]{1,0:T(8,128)S(1)} %shard_map.78.mine), channel_id=1, source_target_pairs={{0,1},{1,0},{2,3},{3,2},{4,5},{5,4},{6,7},{7,6},{8,9},{9,8},{10,11... | collective-permute-start | bytes 49160 | tf_op jit(solution)/shard_map/ppermute | solution.py:397
  67.6 3.1 %shard_map.79 = f32[4,4,96,128]{3,2,1,0:T(8,128)} custom-call(s32[2]{0:T(128)S(1)} %pad_add_fusion.flags, bf16[4,4,96,128]{3,2,1,0:T(8,128)(2,1)S(1)} %bitcast.39, bf16[4,4,96,128]{3,2,1,0:T(8,128)(2,1)S(1)} %get-tuple-element.35.act, bf16[2,5,96,128]{3,2,1,0:T(8,128)(2,1)S(1)} %collective-permute-done.5.a_far, ...), custom_call_target="tpu_custom_call" | custom-call | flops 1019215872 | bytes 2512896 | tf_op jit(solution)/shard_map/pallas_call | solution.py:248
  70.6 0.0 collective-permute-done.6.other
  70.6 0.7 shard_map.80
  71.3 0.0 collective-permute-done.7.g_far
  71.3 3.4 %all-to-all-start.2 = ((f32[8,32,128]{2,1,0:T(8,128)}), f32[8,32,128]{2,1,0:T(8,128)S(1)}, u32[]{:S(2)}, u32[]{:S(2)}) async-start(f32[8,32,128]{2,1,0:T(8,128)} %shard_map.80), calls=%async_computation.2 | async-start | bytes 262144 | tf_op jit(solution)/shard_map/all_to_all | solution.py:285
  74.7 0.0 copy-start.5
  74.7 1.0 %copy-done.5 = bf16[288,864]{1,0:T(8,128)(2,1)S(1)} copy-done((bf16[288,864]{1,0:T(8,128)(2,1)S(1)}, bf16[288,864]{1,0:T(8,128)(2,1)}, u32[]{:S(2)}) %copy-start.5) | copy-done | bytes 497688
  75.7 3.0 %shard_map.81 = f32[4,4,96,128]{3,2,1,0:T(8,128)} custom-call(s32[2]{0:T(128)S(1)} %pad_add_fusion.flags, bf16[4,4,96,128]{3,2,1,0:T(8,128)(2,1)S(1)} %bitcast.40, bf16[4,4,96,128]{3,2,1,0:T(8,128)(2,1)S(1)} %bitcast.42, bf16[4,4,96,128]{3,2,1,0:T(8,128)(2,1)S(1)} %get-tuple-element.32.grad, bf16[2,5,96,128]{3,2,1,0:T(8,128)(2,1)S(1)} %collective-permute-done.7.g_far, ...), custom_call_target="tpu_custom_call" | custom-call | flops 1019215872 | bytes 2906112 | tf_op jit(solution)/shard_map/pallas_call | solution.py:248
  78.8 3.8 %all-to-all-done.2 = f32[8,32,128]{2,1,0:T(8,128)S(1)} async-done(((f32[8,32,128]{2,1,0:T(8,128)}), f32[8,32,128]{2,1,0:T(8,128)S(1)}, u32[]{:S(2)}, u32[]{:S(2)}) %all-to-all-start.2) | async-done | bytes 131104 | tf_op jit(solution)/shard_map/all_to_all | solution.py:285
  82.6 5.1 %collective-permute-start.8 = (f32[256,128]{1,0:T(8,128)S(1)}, f32[256,128]{1,0:T(8,128)S(1)}, u32[]{:S(2)}, u32[]{:S(2)}) collective-permute-start(f32[256,128]{1,0:T(8,128)S(1)} %bitcast.36), channel_id=1, source_target_pairs={{0,2},{2,0},{1,3},{3,1},{4,6},{6,4},{5,7},{7,5},{8,10},{10,8},{9,1... | collective-permute-start | bytes 393224 | tf_op jit(solution)/shard_map/ppermute | solution.py:410
  87.7 1.0 %collective-permute-done.8.other = f32[256,128]{1,0:T(8,128)S(1)} collective-permute-done((f32[256,128]{1,0:T(8,128)S(1)}, f32[256,128]{1,0:T(8,128)S(1)}, u32[]{:S(2)}, u32[]{:S(2)}) %collective-permute-start.8) | collective-permute-done | bytes 131104 | tf_op jit(solution)/shard_map/ppermute | solution.py:410
  88.7 1.6 %shard_map.82 = (f32[96,324]{1,0:T(8,128)}, f32[96,324]{1,0:T(8,128)}) custom-call(s32[2]{0:T(128)S(1)} %pad_add_fusion.flags, f32[256,128]{1,0:T(8,128)S(1)} %bitcast.37, f32[256,128]{1,0:T(8,128)S(1)} %collective-permute-done.8.other), custom_call_target="tpu_custom_call" | custom-call | bytes 510984 | tf_op jit(solution)/shard_map/pallas_call | solution.py:328
  (11 shorter events, 0.2 us)
Async XLA Ops:
  0.6 4.7 %copy-start = (bf16[1,4,4,96,128]{4,3,2,1,0:T(8,128)(2,1)S(1)}, bf16[1,4,4,96,128]{4,3,2,1,0:T(8,128)(2,1)}, u32[]{:S(2)}) copy-start(bf16[1,4,4,96,128]{4,3,2,1,0:T(8,128)(2,1)} %param.4) | copy-start | bytes 1179652
  1.7 3.8 %copy-start.1 = (bf16[1,4,4,96,128]{4,3,2,1,0:T(8,128)(2,1)S(1)}, bf16[1,4,4,96,128]{4,3,2,1,0:T(8,128)(2,1)}, u32[]{:S(2)}) copy-start(bf16[1,4,4,96,128]{4,3,2,1,0:T(8,128)(2,1)} %param.5) | copy-start | bytes 1179652
  1.7 7.2 %collective-permute-start = (bf16[8,96,128]{2,1,0:T(8,128)(2,1)S(1)}, bf16[8,96,128]{2,1,0:T(8,128)(2,1)S(1)}, u32[]{:S(2)}, u32[]{:S(2)}) collective-permute-start(bf16[8,96,128]{2,1,0:T(8,128)(2,1)S(1)} %pad_maximum_fusion.4), channel_id=1, source_target_pairs={{0,1},{1,0},{2,3},{3,2},{4,5},{5,4},{6,7},{7,6},{8,9},{9,8},{10,11... | collective-permute-start | bytes 589832 | tf_op jit(solution)/shard_map/ppermute | solution.py:371
  8.9 8.1 %copy-start.3 = (bf16[2592,96]{0,1:T(8,128)(2,1)S(1)}, bf16[2592,96]{0,1:T(8,128)(2,1)}, u32[]{:S(2)}) copy-start(bf16[2592,96]{0,1:T(8,128)(2,1)} %param.7) | copy-start | bytes 1492996
  8.9 8.1 %copy-start.2 = (bf16[2592,96]{0,1:T(8,128)(2,1)S(1)}, bf16[2592,96]{0,1:T(8,128)(2,1)}, u32[]{:S(2)}) copy-start(bf16[2592,96]{0,1:T(8,128)(2,1)} %param.6) | copy-start | bytes 1492996
  9.0 10.8 %collective-permute-start.1 = (bf16[2,5,96,128]{3,2,1,0:T(8,128)(2,1)S(1)}, bf16[2,5,96,128]{3,2,1,0:T(8,128)(2,1)S(1)}, u32[]{:S(2)}, u32[]{:S(2)}) collective-permute-start(bf16[2,5,96,128]{3,2,1,0:T(8,128)(2,1)S(1)} %pad_maximum_fusion), channel_id=1, source_target_pairs={{0,2},{2,4},{4,6},{6,8},{8,10},{10,12},{12,14},{14,16},{16,18},{18... | collective-permute-start | bytes 737288 | tf_op jit(solution)/shard_map/ppermute | solution.py:262
  15.1 7.5 %collective-permute-start.2 = (bf16[2,5,96,128]{3,2,1,0:T(8,128)(2,1)S(1)}, bf16[2,5,96,128]{3,2,1,0:T(8,128)(2,1)S(1)}, u32[]{:S(2)}, u32[]{:S(2)}) collective-permute-start(bf16[2,5,96,128]{3,2,1,0:T(8,128)(2,1)S(1)} %pad_maximum_fusion.1), channel_id=1, source_target_pairs={{2,0},{4,2},{6,4},{8,6},{10,8},{12,10},{14,12},{16,14},{18,16},{20... | collective-permute-start | bytes 737288 | tf_op jit(solution)/shard_map/ppermute | solution.py:271
  19.0 0.8 copy-start.4
  30.7 2.0 %collective-permute-start.3 = (bf16[8,256,128]{2,1,0:T(8,128)(2,1)S(1)}, bf16[8,256,128]{2,1,0:T(8,128)(2,1)S(1)}, u32[]{:S(2)}, u32[]{:S(2)}) collective-permute-start(bf16[8,256,128]{2,1,0:T(8,128)(2,1)S(1)} %get-tuple-element.29), channel_id=1, source_target_pairs={{0,2},{2,0},{1,3},{3,1},{4,6},{6,4},{5,7},{7,5},{8,10},{10,8},{9,1... | collective-permute-start | bytes 1572872 | tf_op jit(solution)/shard_map/ppermute | solution.py:275
  33.6 7.9 %collective-permute-start.4 = (bf16[8,96,128]{2,1,0:T(8,128)(2,1)S(1)}, bf16[8,96,128]{2,1,0:T(8,128)(2,1)S(1)}, u32[]{:S(2)}, u32[]{:S(2)}) collective-permute-start(bf16[8,96,128]{2,1,0:T(8,128)(2,1)S(1)} %get-tuple-element.33), channel_id=1, source_target_pairs={{0,1},{1,0},{2,3},{3,2},{4,5},{5,4},{6,7},{7,6},{8,9},{9,8},{10,11... | collective-permute-start | bytes 589832 | tf_op jit(solution)/shard_map/ppermute | solution.py:389
  36.4 12.4 %all-to-all-start = ((bf16[8,256,128]{2,1,0:T(8,128)(2,1)}), bf16[8,256,128]{2,1,0:T(8,128)(2,1)S(1)}, u32[]{:S(2)}, u32[]{:S(2)}) async-start(bf16[8,256,128]{2,1,0:T(8,128)(2,1)} %add_convert_fusion), calls=%async_computation | async-start | bytes 1048576 | tf_op jit(solution)/shard_map/all_to_all | solution.py:279
  42.2 23.4 %collective-permute-start.5 = (bf16[2,5,96,128]{3,2,1,0:T(8,128)(2,1)}, bf16[2,5,96,128]{3,2,1,0:T(8,128)(2,1)S(1)}, u32[]{:S(2)}, u32[]{:S(2)}) collective-permute-start(bf16[2,5,96,128]{3,2,1,0:T(8,128)(2,1)} %pad_maximum_fusion.3), channel_id=1, source_target_pairs={{0,2},{2,4},{4,6},{6,8},{8,10},{10,12},{12,14},{14,16},{16,18},{18... | collective-permute-start | bytes 737288 | tf_op jit(solution)/shard_map/ppermute | solution.py:262
  49.4 16.1 %all-to-all-start.1 = ((f32[8,32,128]{2,1,0:T(8,128)}), f32[8,32,128]{2,1,0:T(8,128)S(1)}, u32[]{:S(2)}, u32[]{:S(2)}) async-start(f32[8,32,128]{2,1,0:T(8,128)} %bitcast.16), calls=%async_computation.1 | async-start | bytes 262144 | tf_op jit(solution)/shard_map/all_to_all | solution.py:285
  57.5 13.8 %collective-permute-start.7 = (bf16[2,5,96,128]{3,2,1,0:T(8,128)(2,1)S(1)}, bf16[2,5,96,128]{3,2,1,0:T(8,128)(2,1)S(1)}, u32[]{:S(2)}, u32[]{:S(2)}) collective-permute-start(bf16[2,5,96,128]{3,2,1,0:T(8,128)(2,1)S(1)} %pad_maximum_fusion.2), channel_id=1, source_target_pairs={{2,0},{4,2},{6,4},{8,6},{10,8},{12,10},{14,12},{16,14},{18,16},{20... | collective-permute-start | bytes 737288 | tf_op jit(solution)/shard_map/ppermute | solution.py:271
  65.5 5.1 %collective-permute-start.6 = (f32[32,128]{1,0:T(8,128)S(1)}, f32[32,128]{1,0:T(8,128)S(1)}, u32[]{:S(2)}, u32[]{:S(2)}) collective-permute-start(f32[32,128]{1,0:T(8,128)S(1)} %shard_map.78.mine), channel_id=1, source_target_pairs={{0,1},{1,0},{2,3},{3,2},{4,5},{5,4},{6,7},{7,6},{8,9},{9,8},{10,11... | collective-permute-start | bytes 49160 | tf_op jit(solution)/shard_map/ppermute | solution.py:397
  71.3 11.3 %all-to-all-start.2 = ((f32[8,32,128]{2,1,0:T(8,128)}), f32[8,32,128]{2,1,0:T(8,128)S(1)}, u32[]{:S(2)}, u32[]{:S(2)}) async-start(f32[8,32,128]{2,1,0:T(8,128)} %shard_map.80), calls=%async_computation.2 | async-start | bytes 262144 | tf_op jit(solution)/shard_map/all_to_all | solution.py:285
  74.7 1.0 %copy-start.5 = (bf16[288,864]{1,0:T(8,128)(2,1)S(1)}, bf16[288,864]{1,0:T(8,128)(2,1)}, u32[]{:S(2)}) copy-start(bf16[288,864]{1,0:T(8,128)(2,1)} %copy-done.4) | copy-start | bytes 1492996
  82.6 6.1 %collective-permute-start.8 = (f32[256,128]{1,0:T(8,128)S(1)}, f32[256,128]{1,0:T(8,128)S(1)}, u32[]{:S(2)}, u32[]{:S(2)}) collective-permute-start(f32[256,128]{1,0:T(8,128)S(1)} %bitcast.36), channel_id=1, source_target_pairs={{0,2},{2,0},{1,3},{3,1},{4,6},{6,4},{5,7},{7,5},{8,10},{10,8},{9,1... | collective-permute-start | bytes 393224 | tf_op jit(solution)/shard_map/ppermute | solution.py:410
